TPU v7x, 128 devices: a whole 4x4x4 slice. The times are simulated.
128 devices in a mesh: replica: 8 (over y_hi, x), shard: 16 (over y_lo, z, core).
Axes of the slice: x: 4, y: 4 (y_hi: 2, y_lo: 2; y = y_hi * 2 + y_lo), z: 4, core: 2. Of those that a mesh axis runs over, the one named last changes fastest.
Arguments:
- global_params: float32 [2, 8192, 2048], P(None, 'shard'), may hold values from -6 to 6, as said below
- replica_params: bfloat16 [8, 2, 8192, 2048], P('replica', None, 'shard'), may hold values from -400 to 400
- momentum: float32 [2, 8192, 2048], P(None, 'shard', 'replica'), may hold values from -6 to 6
Outputs:
- new_params: float32 [2, 8192, 2048], P(None, 'shard')
- new_momentum: float32 [2, 8192, 2048], P(None, 'shard', 'replica')
- backup_momentum: float32 [2, 8192, 2048], P(None, 'shard', 'replica')
Inputs may be any that keep to these rules, and one draw needn't show every extreme that they name: `global_params`: normally distributed entries clipped to the range.
All inputs are finite; a program needn't handle non-finite values.
Results may differ from a plain program's by a relative error of at most 0.0003.
Values sent between devices are 32-bit elements; how exact they have to be, the bound alone decides.
No kernel may reach another device: no remote copies, remote signals or barrier semaphores. Data moves between devices by JAX's collectives and lax.ppermute only.
A program may use at most 128 MiB of HBM per device.

v0:
```python
import jax
import jax.numpy as jnp
from jax import lax
from jax.sharding import PartitionSpec as P

D = 8192
LAYERS = 2
KV2 = 2048


outer_beta = 0.9
outer_rate = 0.7
clip_rms = 1.0


def clip_factor(square_sum):
    element_count = LAYERS * D * KV2
    rms_value = jnp.sqrt(square_sum / element_count + 1e-06)
    return jnp.minimum(1.0, clip_rms / rms_value)


def per_device(global_params, replica_params, momentum):
    replicas = lax.axis_size("replica")
    drift_term = global_params - replica_params[0].astype(jnp.float32)
    block_cols = momentum.shape[2]
    summed = lax.psum(drift_term, "replica")
    pseudo_grad = summed / replicas
    square_sum = lax.psum(jnp.sum(pseudo_grad * pseudo_grad), "shard")
    clipped = pseudo_grad * clip_factor(square_sum)
    full_momentum = lax.all_gather(momentum, "replica", axis=2, tiled=True)
    momentum_all = outer_beta * full_momentum + clipped
    new_params = global_params - outer_rate * (clipped + outer_beta * momentum_all)
    own_block = lax.axis_index("replica")
    new_momentum = lax.dynamic_slice_in_dim(momentum_all, own_block * block_cols, block_cols, 2)
    previous = (own_block + replicas - 1) % replicas
    backup_momentum = lax.dynamic_slice_in_dim(momentum_all, previous * block_cols, block_cols, 2)
    return (new_params, new_momentum, backup_momentum)


def solution(mesh):
    in_specs = (
        P(None, "shard", None),
        P("replica", None, "shard", None),
        P(None, "shard", "replica"),
    )
    out_specs = (P(None, "shard", None), P(None, "shard", "replica"), P(None, "shard", "replica"))
    return jax.shard_map(
        per_device, mesh=mesh, in_specs=in_specs, out_specs=out_specs, check_vma=False
    )
```

profile of v0, /device:TPU:4, one launch (start us, length us, event | category | flops | bytes accessed | tf_op | source)
XLA Modules:
  0.0 346.4 jit_solution(17788448043397815985)
XLA Ops:
  7.2 0.0 all-reduce.2.cloned.1.call-start
  7.2 10.1 %convert_subtract_fusion = f32[2,512,2048]{2,1,0:T(8,128)} fusion(f32[2,512,2048]{2,1,0:T(8,128)} %param.3, bf16[1,2,512,2048]{3,2,1,0:T(8,128)(2,1)} %param.4), kind=kLoop, calls=%fused_computation | loop fusion | flops 4194304 | bytes 20971520 | tf_op jit(solution)/shard_map/sub | solution.py:24
  17.3 0.0 all-reduce.2.cloned.1.call-update
  17.3 0.0 all-gather.2.cloned.1.call-start
  17.4 0.7 all-gather.2.cloned.1.call-update
  18.1 183.7 %all-reduce.2.cloned.1.call-done = f32[2,512,2048]{2,1,0:T(8,128)} async-done(((f32[2,512,2048]{2,1,0:T(8,128)}), f32[2,512,2048]{2,1,0:T(8,128)}) %all-reduce.2.cloned.1.call-update) | async-done | bytes 8388624 | tf_op jit(solution)/shard_map/psum | solution.py:26
  201.8 6.1 %multiply_reduce_fusion = f32[]{:T(128)} fusion(f32[2,512,2048]{2,1,0:T(8,128)} %all-reduce.2.cloned.1.call-done), kind=kLoop, calls=%fused_computation.3 | loop fusion | flops 6291455 | bytes 8388612 | tf_op jit(solution)/shard_map/reduce_sum | solution.py:28
  207.9 31.3 %psum.15 = f32[]{:T(128)} all-reduce(f32[]{:T(128)} %multiply_reduce_fusion), channel_id=1, replica_groups=mesh['replica'=8,'shard'=16] {'shard'}, use_global_device_ids=true, to_apply=%region_2.0 | all-reduce | flops 1 | bytes 8 | tf_op jit(solution)/shard_map/psum | solution.py:28
  239.9 84.4 %all-gather.2.cloned.1.call-done = f32[2,512,2048]{2,1,0:T(8,128)} async-done(((f32[2,512,256]{2,1,0:T(8,128)}), f32[2,512,2048]{2,1,0:T(8,128)}) %all-gather.2.cloned.1.call-update) | async-done | bytes 8388624 | tf_op jit(solution)/shard_map/all_gather | solution.py:30
  324.3 13.7 %multiply_add_fusion = (f32[2,512,2048]{2,1,0:T(8,128)S(1)}, f32[2,512,2048]{2,1,0:T(8,128)}) fusion(f32[2,512,2048]{2,1,0:T(8,128)} %all-gather.2.cloned.1.call-done, f32[2,512,2048]{2,1,0:T(8,128)} %all-reduce.2.cloned.1.call-done, f32[]{:T(128)S(6)} %mul.30, f32[2,512,2048]{2,1,0:T(8,128)} %param.3), kind=kLoop, calls=%fused_computation.2 | loop fusion | flops 14680064 | bytes 41943044 | tf_op jit(solution)/shard_map/add | solution.py:31
  338.0 1.6 constant_dynamic-slice_fusion
Async XLA Ops:
  7.2 194.6 %all-reduce.2.cloned.1.call-start = ((), (), s32[]{:S(2)}) async-start(), calls=%async_computation | async-start | bytes 16777216 | tf_op jit(solution)/shard_map/psum | solution.py:26
  17.3 307.0 %all-gather.2.cloned.1.call-start = ((), (), s32[]{:S(2)}) async-start(), calls=%async_computation.1 | async-start | bytes 9437184 | tf_op jit(solution)/shard_map/all_gather | solution.py:30
Sparse Core Ops, SparseCore 0:
  17.4 184.2 all-reduce.1
  203.9 120.3 all-gather.1
where the time goes:
time: 348 us; the launch traced here: 346 us
  waiting for transfers between devices  269 us (77%)
  blocking collectives  31.3 us (9%)
  other arithmetic  29.9 us (9%)
  between operations  14.8 us (4%)
    psum x1, waiting for transfers between devices, per_device(): summed = lax.psum(drift_term, 'replica')  184 us
    all_gather x1, waiting for transfers between devices, per_device(): full_momentum = lax.all_gather(momentum, 'replica', axis=2, tiled=True)  84.4 us
    psum x1, blocking collectives, per_device(): square_sum = lax.psum(jnp.sum(pseudo_grad * pseudo_grad), 'shard')  31.3 us
    add x1, other arithmetic, per_device(): momentum_all = outer_beta * full_momentum + clipped  13.7 us
    sub x1, other arithmetic, per_device(): drift_term = global_params - replica_params[0].astype(jnp.float32)  10.1 us
  transfers between devices with their start and end apart: 2, of which 2 were waited for; matrix products, arithmetic and copies ran while one was open for 2% of the time, Pallas kernels for 0%

commit v1 on v0

v1 whole, which is shorter than its diff:
```python
import functools

import jax
import jax.numpy as jnp
from jax import lax
from jax.experimental import pallas as pl
from jax.experimental.pallas import tpu as pltpu
from jax.sharding import PartitionSpec as P

D = 8192
LAYERS = 2
KV2 = 2048

outer_beta = 0.9
outer_rate = 0.7
clip_rms = 1.0

grad_gain = outer_rate * (1.0 + outer_beta)
momentum_gain = outer_rate * outer_beta * outer_beta

FLIP = (1, 3, 4)
ORDERS = ((0, 1, 2), (1, 2, 0), (2, 0, 1))
SHARD_FLIP = (1, 2, 6, 8)


def exchange(value, flip, axis, size):
    return lax.ppermute(value, axis, [(i, i ^ flip) for i in range(size)])


def flip_of(order, bits):
    total = 0
    for edge, bit in zip(order, bits):
        if bit:
            total ^= FLIP[edge]
    return total


def part_rows(rows):
    unit = 16
    tiles = rows // unit
    counts = [tiles // 3 + (1 if k < tiles % 3 else 0) for k in range(3)]
    starts = [sum(counts[:k]) for k in range(3)]
    return [(s * unit, c * unit) for s, c in zip(starts, counts)]


def blocks_of(first_bit):
    return [(k, j, flip_of(ORDERS[k], (first_bit, j // 2, j % 2))) for j in range(4) for k in range(3)]


def drift_kernel(spans, block_cols, items, g_ref, r_ref, *rest):
    outs, (g_buf, r_buf, g_sem, r_sem, o_sem) = rest[:3], rest[3:]
    own = lax.axis_index("replica")

    def loads(n):
        k, j, flip = items[n]
        start, count = spans[k]
        cols = pl.ds(pl.multiple_of((own ^ flip) * block_cols, block_cols), block_cols)
        rows = pl.ds(start, count)
        return (
            pltpu.make_async_copy(g_ref.at[rows, cols], g_buf.at[n, pl.ds(0, count)], g_sem.at[n]),
            pltpu.make_async_copy(r_ref.at[rows, cols], r_buf.at[n, pl.ds(0, count)], r_sem.at[n]),
        )

    def store(n):
        k, j, _ = items[n]
        count = spans[k][1]
        return pltpu.make_async_copy(g_buf.at[n, pl.ds(0, count)], outs[k].at[j], o_sem.at[n])

    for n in range(len(items)):
        for copy in loads(n):
            copy.start()
    for n in range(len(items)):
        for copy in loads(n):
            copy.wait()
        count = spans[items[n][0]][1]
        g_buf[n, :count] = g_buf[n, :count] - r_buf[n, :count].astype(jnp.float32)
        store(n).start()
    for n in range(len(items)):
        store(n).wait()


def drift(g, r, spans, block_cols, first_bit):
    items = blocks_of(first_bit)
    most = max(count for _, count in spans)
    n = len(items)
    return pl.pallas_call(
        functools.partial(drift_kernel, spans, block_cols, items),
        out_shape=[jax.ShapeDtypeStruct((4, count, block_cols), jnp.float32) for _, count in spans],
        in_specs=[pl.BlockSpec(memory_space=pl.ANY)] * 2,
        out_specs=[pl.BlockSpec(memory_space=pl.ANY)] * 3,
        scratch_shapes=[
            pltpu.VMEM((n, most, block_cols), jnp.float32),
            pltpu.VMEM((n, most, block_cols), jnp.bfloat16),
            pltpu.SemaphoreType.DMA((n,)),
            pltpu.SemaphoreType.DMA((n,)),
            pltpu.SemaphoreType.DMA((n,)),
        ],
        compiler_params=pltpu.CompilerParams(vmem_limit_bytes=12 * 1024 * 1024),
        cost_estimate=pl.CostEstimate(flops=n * most * block_cols, bytes_accessed=10 * n * most * block_cols, transcendentals=0),
        name="drift",
    )(g, r)


def apply_kernel(spans, block_cols, items, g_ref, u0, u1, u2, prev_ref, out_ref, g_buf, u_buf, g_sem, u_sem, o_sem):
    us = (u0, u1, u2)
    own = lax.axis_index("replica")

    def place(n):
        k, j, flip = items[n]
        start, count = spans[k]
        return pl.ds(start, count), pl.ds(pl.multiple_of((own ^ flip) * block_cols, block_cols), block_cols), count

    def loads(n):
        k, j, _ = items[n]
        rows, cols, count = place(n)
        return (
            pltpu.make_async_copy(g_ref.at[rows, cols], g_buf.at[n, pl.ds(0, count)], g_sem.at[n]),
            pltpu.make_async_copy(us[k].at[j], u_buf.at[n, pl.ds(0, count)], u_sem.at[n]),
        )

    def store(n):
        rows, cols, count = place(n)
        return pltpu.make_async_copy(g_buf.at[n, pl.ds(0, count)], out_ref.at[rows, cols], o_sem.at[n])

    for n in range(len(items)):
        for copy in loads(n):
            copy.start()
    for n in range(len(items)):
        for copy in loads(n):
            copy.wait()
        count = spans[items[n][0]][1]
        g_buf[n, :count] = g_buf[n, :count] - u_buf[n, :count]
        store(n).start()
    for n in range(len(items)):
        store(n).wait()


def apply(g, us, before, spans, block_cols, first_bit):
    items = blocks_of(first_bit)
    most = max(count for _, count in spans)
    n = len(items)
    operands = [g, *us] + ([] if before is None else [before])

    def body(*refs):
        inputs, rest = refs[: len(operands)], refs[len(operands) :]
        apply_kernel(spans, block_cols, items, *inputs[:4], None, *rest)

    return pl.pallas_call(
        body,
        out_shape=jax.ShapeDtypeStruct(g.shape, jnp.float32),
        in_specs=[pl.BlockSpec(memory_space=pl.ANY)] * len(operands),
        out_specs=pl.BlockSpec(memory_space=pl.ANY),
        input_output_aliases={} if before is None else {4: 0},
        scratch_shapes=[
            pltpu.VMEM((n, most, block_cols), jnp.float32),
            pltpu.VMEM((n, most, block_cols), jnp.float32),
            pltpu.SemaphoreType.DMA((n,)),
            pltpu.SemaphoreType.DMA((n,)),
            pltpu.SemaphoreType.DMA((n,)),
        ],
        compiler_params=pltpu.CompilerParams(vmem_limit_bytes=12 * 1024 * 1024),
        cost_estimate=pl.CostEstimate(flops=n * most * block_cols, bytes_accessed=12 * n * most * block_cols, transcendentals=0),
        name="apply",
    )(*operands)


def clip_factor(square_sum):
    element_count = LAYERS * D * KV2
    rms_value = jnp.sqrt(square_sum / element_count + 1e-06)
    return jnp.minimum(1.0, clip_rms / rms_value)


def per_device(global_params, replica_params, momentum):
    replicas = 8
    layers, rows, cols = global_params.shape
    block_cols = cols // replicas
    g = global_params.reshape(layers * rows, cols)
    r = replica_params.reshape(layers * rows, cols)
    m = momentum.reshape(layers * rows, block_cols)
    spans = part_rows(layers * rows)
    own = lax.axis_index("replica")

    sent = drift(g, r, spans, block_cols, 1)
    got = [exchange(sent[k], FLIP[ORDERS[k][0]], "replica", replicas) for k in range(3)]
    kept = drift(g, r, spans, block_cols, 0)
    prior_m = lax.ppermute(m, "replica", [(i, (i + 1) % replicas) for i in range(replicas)])
    grads = []
    for k in range(3):
        send2 = kept[k][2:] + got[k][2:]
        got2 = exchange(send2, FLIP[ORDERS[k][1]], "replica", replicas)
        keep2 = kept[k][:2] + got[k][:2]
        send3 = keep2[1] + got2[1]
        got3 = exchange(send3, FLIP[ORDERS[k][2]], "replica", replicas)
        grads.append((keep2[0] + got2[0] + got3) / replicas)

    squares = sum(jnp.sum((p * p).reshape(-1, 8, block_cols // 128, 128), axis=(0, 2)) for p in grads)
    for flip in FLIP:
        squares = squares + exchange(squares, flip, "replica", 8)
    for flip in SHARD_FLIP:
        squares = squares + exchange(squares, flip, "shard", 16)
    factor = clip_factor(jnp.sum(squares))

    news, updates = [], []
    for k, (start, count) in enumerate(spans):
        clipped = grads[k] * factor
        mine = m[start : start + count]
        news.append(outer_beta * mine + clipped)
        u = grad_gain * clipped + momentum_gain * mine
        half = jnp.stack([u, exchange(u, FLIP[ORDERS[k][2]], "replica", replicas)])
        most = jnp.concatenate([half, exchange(half, FLIP[ORDERS[k][1]], "replica", replicas)])
        updates.append((most, exchange(most, FLIP[ORDERS[k][0]], "replica", replicas)))
    new_momentum = jnp.concatenate(news)
    params = apply(g, [u[0] for u in updates], None, spans, block_cols, 0)
    params = apply(g, [u[1] for u in updates], params, spans, block_cols, 1)

    back = own ^ ((own + replicas - 1) % replicas)
    pieces = []
    for k, (start, count) in enumerate(spans):
        where = {}
        for j in range(8):
            where[flip_of(ORDERS[k], (j // 4, j // 2 % 2, j % 2))] = updates[k][j // 4][j % 4]
        u_prior = jnp.where(back == 1, where[1], jnp.where(back == 3, where[3], where[7]))
        old = prior_m[start : start + count]
        pieces.append(u_prior * (1.0 / grad_gain) + (outer_beta - momentum_gain / grad_gain) * old)
    backup = jnp.concatenate(pieces)
    return (
        params.reshape(layers, rows, cols),
        new_momentum.reshape(layers, rows, block_cols),
        backup.reshape(layers, rows, block_cols),
    )


def solution(mesh):
    in_specs = (
        P(None, "shard", None),
        P("replica", None, "shard", None),
        P(None, "shard", "replica"),
    )
    out_specs = (P(None, "shard", None), P(None, "shard", "replica"), P(None, "shard", "replica"))
    return jax.shard_map(
        per_device, mesh=mesh, in_specs=in_specs, out_specs=out_specs, check_vma=False
    )
```

time: 348 us -> 203 us (0.58)
  waiting for transfers between devices: 269 us -> 109 us
  starting transfers between devices: 0.08 us -> 49.1 us
  blocking collectives: 31.3 us -> 0 us
  other arithmetic: 29.9 us -> 13.2 us
  Pallas kernels: 0 us -> 13.5 us
  between operations: 14.8 us -> 1.64 us
  local copies, waits for them, and re-layouts: 1.55 us -> 13.1 us
    psum x1 -> x0, waiting for transfers between devices: 184 us -> none  [per_device(): summed = lax.psum(drift_term, 'replica')]
    ppermute x0 -> x26, waiting for transfers between devices: none -> 109 us  [the longest x25 73.4 us: exchange(): return lax.ppermute(value, axis, [(i, i ^ flip) for i in range(size)])]
    all_gather x1 -> x0, waiting for transfers between devices: 84.4 us -> none  [per_device(): full_momentum = lax.all_gather(momentum, 'replica', axis=2, tiled=True)]
    ppermute x0 -> x26, starting transfers between devices: none -> 49.1 us  [the longest x25 47.3 us: exchange(): return lax.ppermute(value, axis, [(i, i ^ flip) for i in range(size)])]
    psum x1 -> x0, blocking collectives: 31.3 us -> none  [per_device(): square_sum = lax.psum(jnp.sum(pseudo_grad * pseudo_grad), 'shard')]
    pallas_call x0 -> x4, Pallas kernels: none -> 13.5 us  [the longest x2 7.59 us: apply(): pl.pallas_call(body, out_shape=jax.ShapeDtypeStruct(g.shape, jnp.float32)...]
    unnamed x0 -> x16, local copies, waits for them, and re-layouts: none -> 13.1 us
    sub x1 -> x0, other arithmetic: 10.1 us -> none  [per_device(): drift_term = global_params - replica_params[0].astype(jnp.float32)]
  transfers between devices with their start and end apart: 2 -> 26, of which waited for: 2 -> 16; matrix products, arithmetic and copies ran while one was open for 2% -> 4% of each run, Pallas kernels for 0% -> 3%
where the time goes in v1:
time: 203 us; the launch traced here: 200 us
  waiting for transfers between devices  109 us (54%)
  starting transfers between devices  49.1 us (24%)
  Pallas kernels  13.5 us (7%)
  other arithmetic  13.2 us (7%)
  local copies, waits for them, and re-layouts  13.1 us (6%)
    ppermute x25, waiting for transfers between devices, exchange(): return lax.ppermute(value, axis, [(i, i ^ flip) for i in range(size)])  73.4 us
    ppermute x25, starting transfers between devices, exchange(): return lax.ppermute(value, axis, [(i, i ^ flip) for i in range(size)])  47.3 us
    ppermute x1, waiting for transfers between devices, per_device(): lax.ppermute(m, 'replica', [(i, (i + 1) % replicas) for i in range(replic...  35.8 us
    unnamed x16, local copies, waits for them, and re-layouts  13.1 us
    pallas_call x2, Pallas kernels, apply(): pl.pallas_call(body, out_shape=jax.ShapeDtypeStruct(g.shape, jnp.float32)...  7.59 us
    pallas_call x2, Pallas kernels, drift(): pl.pallas_call(functools.partial(drift_kernel, spans, block_cols, items),...  5.89 us
  transfers between devices with their start and end apart: 26, of which 16 were waited for; matrix products, arithmetic and copies ran while one was open for 4% of the time, Pallas kernels for 3%

profile of v1, /device:TPU:4, one launch (start us, length us, event | category | flops | bytes accessed | tf_op | source)
XLA Modules:
  0.0 199.6 jit_solution(7534734468102340746)
XLA Ops:
  0.6 3.4 %copy-done = f32[2,512,2048]{2,1,0:T(8,128)S(1)} copy-done((f32[2,512,2048]{2,1,0:T(8,128)S(1)}, f32[2,512,2048]{2,1,0:T(8,128)}, u32[]{:S(2)}) %copy-start) | copy-done | bytes 8388632
  4.0 2.2 %copy-done.3 = bf16[1,2,512,2048]{3,2,1,0:T(8,128)(2,1)S(1)} copy-done((bf16[1,2,512,2048]{3,2,1,0:T(8,128)(2,1)S(1)}, bf16[1,2,512,2048]{3,2,1,0:T(8,128)(2,1)}, u32[]{:S(2)}) %copy-start.3) | copy-done | bytes 4194328
  6.2 2.9 %drift.3 = (f32[4,352,256]{2,1,0:T(8,128)S(1)}, f32[4,336,256]{2,1,0:T(8,128)S(1)}, f32[4,336,256]{2,1,0:T(8,128)S(1)}) custom-call(f32[1024,2048]{1,0:T(8,128)S(1)} %bitcast.65, bf16[1024,2048]{1,0:T(8,128)(2,1)S(1)} %bitcast.69), custom_call_target="tpu_custom_call" | custom-call | flops 1081344 | bytes 10813440 | tf_op jit(solution)/shard_map/drift/pallas_call | solution.py:86
  9.2 3.3 %collective-permute-start.6 = (f32[4,336,256]{2,1,0:T(8,128)S(1)}, f32[4,336,256]{2,1,0:T(8,128)S(1)}, u32[]{:S(2)}, u32[]{:S(2)}) collective-permute-start(f32[4,336,256]{2,1,0:T(8,128)S(1)} %get-tuple-element.14), channel_id=1, source_target_pairs={{0,64},{16,80},{32,96},{48,112},{64,0},{80,16},{96,32},{112,48},{1... | collective-permute-start | bytes 4128776 | tf_op jit(solution)/shard_map/ppermute | solution.py:27
  12.4 0.5 collective-permute-start.3
  13.0 1.1 collective-permute-start
  14.1 2.9 %drift.2 = (f32[4,352,256]{2,1,0:T(8,128)S(1)}, f32[4,336,256]{2,1,0:T(8,128)S(1)}, f32[4,336,256]{2,1,0:T(8,128)S(1)}) custom-call(f32[1024,2048]{1,0:T(8,128)S(1)} %bitcast.66, bf16[1024,2048]{1,0:T(8,128)(2,1)S(1)} %bitcast.70), custom_call_target="tpu_custom_call" | custom-call | flops 1081344 | bytes 10813440 | tf_op jit(solution)/shard_map/drift/pallas_call | solution.py:86
  17.1 25.6 %collective-permute-done.6 = f32[4,336,256]{2,1,0:T(8,128)S(1)} collective-permute-done((f32[4,336,256]{2,1,0:T(8,128)S(1)}, f32[4,336,256]{2,1,0:T(8,128)S(1)}, u32[]{:S(2)}, u32[]{:S(2)}) %collective-permute-start.6) | collective-permute-done | bytes 1376288 | tf_op jit(solution)/shard_map/ppermute | solution.py:27
  42.7 0.2 slice_add_fusion.3
  42.8 1.3 collective-permute-start.7
  44.1 0.2 slice_add_fusion.5
  44.3 3.3 %collective-permute-start.4 = (f32[2,336,256]{2,1,0:T(8,128)S(1)}, f32[2,336,256]{2,1,0:T(8,128)S(1)}, u32[]{:S(2)}, u32[]{:S(2)}) collective-permute-start(f32[2,336,256]{2,1,0:T(8,128)S(1)} %get-tuple-element.24), channel_id=1, source_target_pairs={{0,64},{16,80},{32,96},{48,112},{64,0},{80,16},{96,32},{112,48},{1... | collective-permute-start | bytes 2064392 | tf_op jit(solution)/shard_map/ppermute | solution.py:27
  47.6 0.2 slice_add_fusion.1
  47.8 1.5 collective-permute-start.1
  49.3 11.2 %collective-permute-done.7 = f32[2,336,256]{2,1,0:T(8,128)S(1)} collective-permute-done((f32[2,336,256]{2,1,0:T(8,128)S(1)}, f32[2,336,256]{2,1,0:T(8,128)S(1)}, u32[]{:S(2)}, u32[]{:S(2)}) %collective-permute-start.7) | collective-permute-done | bytes 688160 | tf_op jit(solution)/shard_map/ppermute | solution.py:27
  60.5 1.6 collective-permute-start.8
  62.2 2.4 %collective-permute-start.5 = (f32[336,256]{1,0:T(8,128)S(1)}, f32[336,256]{1,0:T(8,128)S(1)}, u32[]{:S(2)}, u32[]{:S(2)}) collective-permute-start(f32[336,256]{1,0:T(8,128)S(1)} %fusion.18), channel_id=1, source_target_pairs={{0,16},{16,0},{32,48},{48,32},{64,80},{80,64},{96,112},{112,96},{1... | collective-permute-start | bytes 1032200 | tf_op jit(solution)/shard_map/ppermute | solution.py:27
  64.6 1.8 collective-permute-done.1
  66.5 0.1 collective-permute-start.2
  66.6 5.1 %collective-permute-done.8 = f32[336,256]{1,0:T(8,128)S(1)} collective-permute-done((f32[336,256]{1,0:T(8,128)S(1)}, f32[336,256]{1,0:T(8,128)S(1)}, u32[]{:S(2)}, u32[]{:S(2)}) %collective-permute-start.8) | collective-permute-done | bytes 344096 | tf_op jit(solution)/shard_map/ppermute | solution.py:27
  71.7 0.1 bitcast_reduce_fusion.1
  71.8 0.1 bitcast_reduce_fusion.2
  71.9 3.6 %collective-permute-done.2 = f32[352,256]{1,0:T(8,128)S(1)} collective-permute-done((f32[352,256]{1,0:T(8,128)S(1)}, f32[352,256]{1,0:T(8,128)S(1)}, u32[]{:S(2)}, u32[]{:S(2)}) %collective-permute-start.2) | collective-permute-done | bytes 360480 | tf_op jit(solution)/shard_map/ppermute | solution.py:27
  75.5 0.1 bitcast_reduce_fusion
  75.6 1.8 collective-permute-start.9
  77.4 1.9 collective-permute-done.9
  79.3 3.6 %collective-permute-done.10 = f32[8,128]{1,0:T(8,128)S(1)} collective-permute-done((f32[8,128]{1,0:T(8,128)S(1)}, f32[8,128]{1,0:T(8,128)S(1)}, u32[]{:S(2)}, u32[]{:S(2)}) %collective-permute-start.10) | collective-permute-done | bytes 4128 | tf_op jit(solution)/shard_map/ppermute | solution.py:27
  82.9 2.3 %collective-permute-start.11 = (f32[8,128]{1,0:T(8,128)S(1)}, f32[8,128]{1,0:T(8,128)S(1)}, u32[]{:S(2)}, u32[]{:S(2)}) collective-permute-start(f32[8,128]{1,0:T(8,128)S(1)} %add.152), channel_id=1, source_target_pairs={{0,64},{16,80},{32,96},{48,112},{64,0},{80,16},{96,32},{112,48},{1... | collective-permute-start | bytes 12296 | tf_op jit(solution)/shard_map/ppermute | solution.py:27
  85.2 2.8 %collective-permute-done.11 = f32[8,128]{1,0:T(8,128)S(1)} collective-permute-done((f32[8,128]{1,0:T(8,128)S(1)}, f32[8,128]{1,0:T(8,128)S(1)}, u32[]{:S(2)}, u32[]{:S(2)}) %collective-permute-start.11) | collective-permute-done | bytes 4128 | tf_op jit(solution)/shard_map/ppermute | solution.py:27
  88.0 1.2 collective-permute-done.12
  89.2 1.9 collective-permute-start.13
  91.1 1.7 collective-permute-done.13
  92.8 4.0 %collective-permute-start.14 = (f32[8,128]{1,0:T(8,128)S(1)}, f32[8,128]{1,0:T(8,128)S(1)}, u32[]{:S(2)}, u32[]{:S(2)}) collective-permute-start(f32[8,128]{1,0:T(8,128)S(1)} %add.155), channel_id=1, source_target_pairs={{0,6},{1,7},{2,4},{3,5},{4,2},{5,3},{6,0},{7,1},{8,14},{9,15},{10,... | collective-permute-start | bytes 12296 | tf_op jit(solution)/shard_map/ppermute | solution.py:27
  96.8 1.6 collective-permute-done.14
  98.4 1.0 collective-permute-start.15
  99.4 2.6 %collective-permute-done.15 = f32[8,128]{1,0:T(8,128)S(1)} collective-permute-done((f32[8,128]{1,0:T(8,128)S(1)}, f32[8,128]{1,0:T(8,128)S(1)}, u32[]{:S(2)}, u32[]{:S(2)}) %collective-permute-start.15) | collective-permute-done | bytes 4128 | tf_op jit(solution)/shard_map/ppermute | solution.py:27
  102.0 0.6 add_reduce_fusion
  103.3 2.1 %multiply_add_fusion.3 = (f32[336,256]{1,0:T(8,128)}, f32[336,256]{1,0:T(8,128)S(1)}, f32[336,256]{1,0:T(8,128)S(1)}, f32[336,256]{1,0:T(8,128)}) fusion(f32[1024,256]{1,0:T(8,128)} %bitcast.11, f32[336,256]{1,0:T(8,128)S(1)} %get-tuple-element.16, f32[]{:T(128)S(6)} %mul.93, f32[336,256]{1,0:T(8,128)S(1)} %get-tuple-element.20), kind=kLoop, calls=%fused_computation.54 | loop fusion | flops 1032192 | bytes 2752516 | tf_op jit(solution)/shard_map/add | solution.py:207
  105.5 3.1 %collective-permute-start.19 = (f32[336,256]{1,0:T(8,128)S(1)}, f32[336,256]{1,0:T(8,128)S(1)}, u32[]{:S(2)}, u32[]{:S(2)}) collective-permute-start(f32[336,256]{1,0:T(8,128)S(1)} %get-tuple-element.30), channel_id=1, source_target_pairs={{0,16},{16,0},{32,48},{48,32},{64,80},{80,64},{96,112},{112,96},{1... | collective-permute-start | bytes 1032200 | tf_op jit(solution)/shard_map/ppermute | solution.py:27
  108.6 1.8 multiply_add_fusion
  110.4 2.4 %collective-permute-start.16 = (f32[352,256]{1,0:T(8,128)S(1)}, f32[352,256]{1,0:T(8,128)S(1)}, u32[]{:S(2)}, u32[]{:S(2)}) collective-permute-start(f32[352,256]{1,0:T(8,128)S(1)} %get-tuple-element.28), channel_id=1, source_target_pairs={{0,64},{16,80},{32,96},{48,112},{64,0},{80,16},{96,32},{112,48},{1... | collective-permute-start | bytes 1081352 | tf_op jit(solution)/shard_map/ppermute | solution.py:27
  112.8 4.1 %collective-permute-start.23 = (f32[2,336,256]{2,1,0:T(8,128)S(1)}, f32[2,336,256]{2,1,0:T(8,128)S(1)}, u32[]{:S(2)}, u32[]{:S(2)}) collective-permute-start(f32[2,336,256]{2,1,0:T(8,128)S(1)} %pad_maximum_fusion.7), channel_id=1, source_target_pairs={{0,16},{16,0},{32,48},{48,32},{64,80},{80,64},{96,112},{112,96},{1... | collective-permute-start | bytes 2064392 | tf_op jit(solution)/shard_map/ppermute | solution.py:27
  117.0 2.7 %collective-permute-start.20 = (f32[2,336,256]{2,1,0:T(8,128)S(1)}, f32[2,336,256]{2,1,0:T(8,128)S(1)}, u32[]{:S(2)}, u32[]{:S(2)}) collective-permute-start(f32[2,336,256]{2,1,0:T(8,128)S(1)} %pad_maximum_fusion.6), channel_id=1, source_target_pairs={{0,64},{16,80},{32,96},{48,112},{64,0},{80,16},{96,32},{112,48},{1... | collective-permute-start | bytes 2064392 | tf_op jit(solution)/shard_map/ppermute | solution.py:27
  119.7 2.1 %collective-permute-done.16 = f32[352,256]{1,0:T(8,128)S(1)} collective-permute-done((f32[352,256]{1,0:T(8,128)S(1)}, f32[352,256]{1,0:T(8,128)S(1)}, u32[]{:S(2)}, u32[]{:S(2)}) %collective-permute-start.16) | collective-permute-done | bytes 360480 | tf_op jit(solution)/shard_map/ppermute | solution.py:27
  121.8 4.0 %collective-permute-start.17 = (f32[2,352,256]{2,1,0:T(8,128)S(1)}, f32[2,352,256]{2,1,0:T(8,128)S(1)}, u32[]{:S(2)}, u32[]{:S(2)}) collective-permute-start(f32[2,352,256]{2,1,0:T(8,128)S(1)} %pad_maximum_fusion.5), channel_id=1, source_target_pairs={{0,48},{16,32},{32,16},{48,0},{64,112},{80,96},{96,80},{112,64},{1... | collective-permute-start | bytes 2162696 | tf_op jit(solution)/shard_map/ppermute | solution.py:27
  125.8 2.7 %collective-permute-done.23 = f32[2,336,256]{2,1,0:T(8,128)S(1)} collective-permute-done((f32[2,336,256]{2,1,0:T(8,128)S(1)}, f32[2,336,256]{2,1,0:T(8,128)S(1)}, u32[]{:S(2)}, u32[]{:S(2)}) %collective-permute-start.23) | collective-permute-done | bytes 688160 | tf_op jit(solution)/shard_map/ppermute | solution.py:27
  128.5 0.1 pad_maximum_fusion.2.refs_3_
  128.6 2.6 %collective-permute-start.24 = (f32[4,336,256]{2,1,0:T(8,128)S(1)}, f32[4,336,256]{2,1,0:T(8,128)}, u32[]{:S(2)}, u32[]{:S(2)}) collective-permute-start(f32[4,336,256]{2,1,0:T(8,128)S(1)} %pad_maximum_fusion.2.refs_3_), channel_id=1, source_target_pairs={{0,64},{16,80},{32,96},{48,112},{64,0},{80,16},{96,32},{112,48},{1... | collective-permute-start | bytes 4128776 | tf_op jit(solution)/shard_map/ppermute | solution.py:27
  131.2 5.8 %collective-permute-done.20 = f32[2,336,256]{2,1,0:T(8,128)S(1)} collective-permute-done((f32[2,336,256]{2,1,0:T(8,128)S(1)}, f32[2,336,256]{2,1,0:T(8,128)S(1)}, u32[]{:S(2)}, u32[]{:S(2)}) %collective-permute-start.20) | collective-permute-done | bytes 688160 | tf_op jit(solution)/shard_map/ppermute | solution.py:27
  137.0 1.2 pad_maximum_fusion.1.refs_2_
  138.2 2.2 %collective-permute-start.21 = (f32[4,336,256]{2,1,0:T(8,128)}, f32[4,336,256]{2,1,0:T(8,128)}, u32[]{:S(2)}, u32[]{:S(2)}) collective-permute-start(f32[4,336,256]{2,1,0:T(8,128)} %pad_maximum_fusion.1.refs_2_), channel_id=1, source_target_pairs={{0,48},{16,32},{32,16},{48,0},{64,112},{80,96},{96,80},{112,64},{1... | collective-permute-start | bytes 4128776 | tf_op jit(solution)/shard_map/ppermute | solution.py:27
  140.4 0.1 pad_maximum_fusion.refs_1_
  140.5 0.7 copy-done.4
  141.2 0.2 collective-permute-start.18
  141.4 1.8 collective-permute-start.25
  143.2 2.2 %pad_maximum_fusion.3 = f32[1024,256]{1,0:T(8,128)} fusion(f32[336,256]{1,0:T(8,128)} %get-tuple-element.36, f32[336,256]{1,0:T(8,128)} %get-tuple-element.29, f32[352,256]{1,0:T(8,128)} %get-tuple-element.27), kind=kLoop, calls=%fused_computation.3 | loop fusion | flops 524288 | bytes 2097152 | tf_op jit(solution)/shard_map/concatenate | solution.py:212
  145.5 3.4 %copy-done.1 = f32[2,512,2048]{2,1,0:T(8,128)S(1)} copy-done((f32[2,512,2048]{2,1,0:T(8,128)S(1)}, f32[2,512,2048]{2,1,0:T(8,128)}, u32[]{:S(2)}) %copy-start.1) | copy-done | bytes 8388632
  148.9 3.7 %apply.2.refs_4_ = f32[1024,2048]{1,0:T(8,128)} custom-call(f32[1024,2048]{1,0:T(8,128)S(1)} %bitcast.67, f32[4,352,256]{2,1,0:T(8,128)S(1)} %pad_maximum_fusion.refs_1_, f32[4,336,256]{2,1,0:T(8,128)} %pad_maximum_fusion.1.refs_2_, f32[4,336,256]{2,1,0:T(8,128)S(1)} %pad_maximum_fusion.2.refs_3_), custom_call_target="tpu_custom_call" | custom-call | flops 1081344 | bytes 12976128 | tf_op jit(solution)/shard_map/apply/pallas_call | solution.py:148
  152.6 35.8 %collective-permute-done.25 = f32[1024,256]{1,0:T(8,128)} collective-permute-done((f32[1024,256]{1,0:T(8,128)}, f32[1024,256]{1,0:T(8,128)}, u32[]{:S(2)}, u32[]{:S(2)}) %collective-permute-start.25) | collective-permute-done | bytes 1048608 | tf_op jit(solution)/shard_map/ppermute | solution.py:186
  188.4 1.6 fusion.11
  190.0 1.2 fusion
  191.2 1.0 pad_maximum_fusion.4
  192.2 3.4 %copy-done.2 = f32[2,512,2048]{2,1,0:T(8,128)S(1)} copy-done((f32[2,512,2048]{2,1,0:T(8,128)S(1)}, f32[2,512,2048]{2,1,0:T(8,128)}, u32[]{:S(2)}) %copy-start.2) | copy-done | bytes 8388632
  195.6 3.9 %apply.3 = f32[1024,2048]{1,0:T(8,128)} custom-call(f32[1024,2048]{1,0:T(8,128)S(1)} %bitcast.68, f32[4,352,256]{2,1,0:T(8,128)} %collective-permute-done.18.refs_1_, f32[4,336,256]{2,1,0:T(8,128)} %collective-permute-done.21.refs_2_, f32[4,336,256]{2,1,0:T(8,128)} %collective-permute-done.24.refs_3_, ...), custom_call_target="tpu_custom_call", output_to_operand_aliasing={{}: (4, {})} | custom-call | flops 1081344 | bytes 12976128 | tf_op jit(solution)/shard_map/apply/pallas_call | solution.py:148
  (37 shorter events, 0.4 us)
Async XLA Ops:
  0.6 3.4 %copy-start = (f32[2,512,2048]{2,1,0:T(8,128)S(1)}, f32[2,512,2048]{2,1,0:T(8,128)}, u32[]{:S(2)}) copy-start(f32[2,512,2048]{2,1,0:T(8,128)} %param.3) | copy-start | bytes 25165828
  4.0 2.2 %copy-start.3 = (bf16[1,2,512,2048]{3,2,1,0:T(8,128)(2,1)S(1)}, bf16[1,2,512,2048]{3,2,1,0:T(8,128)(2,1)}, u32[]{:S(2)}) copy-start(bf16[1,2,512,2048]{3,2,1,0:T(8,128)(2,1)} %param.4) | copy-start | bytes 12582916
  9.2 33.5 %collective-permute-start.6 = (f32[4,336,256]{2,1,0:T(8,128)S(1)}, f32[4,336,256]{2,1,0:T(8,128)S(1)}, u32[]{:S(2)}, u32[]{:S(2)}) collective-permute-start(f32[4,336,256]{2,1,0:T(8,128)S(1)} %get-tuple-element.14), channel_id=1, source_target_pairs={{0,64},{16,80},{32,96},{48,112},{64,0},{80,16},{96,32},{112,48},{1... | collective-permute-start | bytes 4128776 | tf_op jit(solution)/shard_map/ppermute | solution.py:27
  12.4 31.7 %collective-permute-start.3 = (f32[4,336,256]{2,1,0:T(8,128)S(1)}, f32[4,336,256]{2,1,0:T(8,128)S(1)}, u32[]{:S(2)}, u32[]{:S(2)}) collective-permute-start(f32[4,336,256]{2,1,0:T(8,128)S(1)} %get-tuple-element.12), channel_id=1, source_target_pairs={{0,48},{16,32},{32,16},{48,0},{64,112},{80,96},{96,80},{112,64},{1... | collective-permute-start | bytes 4128776 | tf_op jit(solution)/shard_map/ppermute | solution.py:27
  13.0 34.6 %collective-permute-start = (f32[4,352,256]{2,1,0:T(8,128)S(1)}, f32[4,352,256]{2,1,0:T(8,128)S(1)}, u32[]{:S(2)}, u32[]{:S(2)}) collective-permute-start(f32[4,352,256]{2,1,0:T(8,128)S(1)} %get-tuple-element.10), channel_id=1, source_target_pairs={{0,16},{16,0},{32,48},{48,32},{64,80},{80,64},{96,112},{112,96},{1... | collective-permute-start | bytes 4325384 | tf_op jit(solution)/shard_map/ppermute | solution.py:27
  42.8 17.6 %collective-permute-start.7 = (f32[2,336,256]{2,1,0:T(8,128)S(1)}, f32[2,336,256]{2,1,0:T(8,128)S(1)}, u32[]{:S(2)}, u32[]{:S(2)}) collective-permute-start(f32[2,336,256]{2,1,0:T(8,128)S(1)} %get-tuple-element.26), channel_id=1, source_target_pairs={{0,16},{16,0},{32,48},{48,32},{64,80},{80,64},{96,112},{112,96},{1... | collective-permute-start | bytes 2064392 | tf_op jit(solution)/shard_map/ppermute | solution.py:27
  44.3 17.9 %collective-permute-start.4 = (f32[2,336,256]{2,1,0:T(8,128)S(1)}, f32[2,336,256]{2,1,0:T(8,128)S(1)}, u32[]{:S(2)}, u32[]{:S(2)}) collective-permute-start(f32[2,336,256]{2,1,0:T(8,128)S(1)} %get-tuple-element.24), channel_id=1, source_target_pairs={{0,64},{16,80},{32,96},{48,112},{64,0},{80,16},{96,32},{112,48},{1... | collective-permute-start | bytes 2064392 | tf_op jit(solution)/shard_map/ppermute | solution.py:27
  47.8 18.6 %collective-permute-start.1 = (f32[2,352,256]{2,1,0:T(8,128)S(1)}, f32[2,352,256]{2,1,0:T(8,128)S(1)}, u32[]{:S(2)}, u32[]{:S(2)}) collective-permute-start(f32[2,352,256]{2,1,0:T(8,128)S(1)} %get-tuple-element.22), channel_id=1, source_target_pairs={{0,48},{16,32},{32,16},{48,0},{64,112},{80,96},{96,80},{112,64},{1... | collective-permute-start | bytes 2162696 | tf_op jit(solution)/shard_map/ppermute | solution.py:27
  60.5 11.2 %collective-permute-start.8 = (f32[336,256]{1,0:T(8,128)S(1)}, f32[336,256]{1,0:T(8,128)S(1)}, u32[]{:S(2)}, u32[]{:S(2)}) collective-permute-start(f32[336,256]{1,0:T(8,128)S(1)} %fusion.15), channel_id=1, source_target_pairs={{0,48},{16,32},{32,16},{48,0},{64,112},{80,96},{96,80},{112,64},{1... | collective-permute-start | bytes 1032200 | tf_op jit(solution)/shard_map/ppermute | solution.py:27
  62.2 9.6 %collective-permute-start.5 = (f32[336,256]{1,0:T(8,128)S(1)}, f32[336,256]{1,0:T(8,128)S(1)}, u32[]{:S(2)}, u32[]{:S(2)}) collective-permute-start(f32[336,256]{1,0:T(8,128)S(1)} %fusion.18), channel_id=1, source_target_pairs={{0,16},{16,0},{32,48},{48,32},{64,80},{80,64},{96,112},{112,96},{1... | collective-permute-start | bytes 1032200 | tf_op jit(solution)/shard_map/ppermute | solution.py:27
  66.5 9.0 %collective-permute-start.2 = (f32[352,256]{1,0:T(8,128)S(1)}, f32[352,256]{1,0:T(8,128)S(1)}, u32[]{:S(2)}, u32[]{:S(2)}) collective-permute-start(f32[352,256]{1,0:T(8,128)S(1)} %fusion.4), channel_id=1, source_target_pairs={{0,64},{16,80},{32,96},{48,112},{64,0},{80,16},{96,32},{112,48},{1... | collective-permute-start | bytes 1081352 | tf_op jit(solution)/shard_map/ppermute | solution.py:27
  75.6 3.7 %collective-permute-start.9 = (f32[8,128]{1,0:T(8,128)S(1)}, f32[8,128]{1,0:T(8,128)S(1)}, u32[]{:S(2)}, u32[]{:S(2)}) collective-permute-start(f32[8,128]{1,0:T(8,128)S(1)} %add_add_fusion), channel_id=1, source_target_pairs={{0,16},{16,0},{32,48},{48,32},{64,80},{80,64},{96,112},{112,96},{1... | collective-permute-start | bytes 12296 | tf_op jit(solution)/shard_map/ppermute | solution.py:27
  79.3 3.6 %collective-permute-start.10 = (f32[8,128]{1,0:T(8,128)S(1)}, f32[8,128]{1,0:T(8,128)S(1)}, u32[]{:S(2)}, u32[]{:S(2)}) collective-permute-start(f32[8,128]{1,0:T(8,128)S(1)} %add.151), channel_id=1, source_target_pairs={{0,48},{16,32},{32,16},{48,0},{64,112},{80,96},{96,80},{112,64},{1... | collective-permute-start | bytes 12296 | tf_op jit(solution)/shard_map/ppermute | solution.py:27
  82.9 5.1 %collective-permute-start.11 = (f32[8,128]{1,0:T(8,128)S(1)}, f32[8,128]{1,0:T(8,128)S(1)}, u32[]{:S(2)}, u32[]{:S(2)}) collective-permute-start(f32[8,128]{1,0:T(8,128)S(1)} %add.152), channel_id=1, source_target_pairs={{0,64},{16,80},{32,96},{48,112},{64,0},{80,16},{96,32},{112,48},{1... | collective-permute-start | bytes 12296 | tf_op jit(solution)/shard_map/ppermute | solution.py:27
  88.0 1.2 collective-permute-start.12
  89.2 3.6 %collective-permute-start.13 = (f32[8,128]{1,0:T(8,128)S(1)}, f32[8,128]{1,0:T(8,128)S(1)}, u32[]{:S(2)}, u32[]{:S(2)}) collective-permute-start(f32[8,128]{1,0:T(8,128)S(1)} %add.154), channel_id=1, source_target_pairs={{0,2},{1,3},{2,0},{3,1},{4,6},{5,7},{6,4},{7,5},{8,10},{9,11},{10,... | collective-permute-start | bytes 12296 | tf_op jit(solution)/shard_map/ppermute | solution.py:27
  92.8 5.6 %collective-permute-start.14 = (f32[8,128]{1,0:T(8,128)S(1)}, f32[8,128]{1,0:T(8,128)S(1)}, u32[]{:S(2)}, u32[]{:S(2)}) collective-permute-start(f32[8,128]{1,0:T(8,128)S(1)} %add.155), channel_id=1, source_target_pairs={{0,6},{1,7},{2,4},{3,5},{4,2},{5,3},{6,0},{7,1},{8,14},{9,15},{10,... | collective-permute-start | bytes 12296 | tf_op jit(solution)/shard_map/ppermute | solution.py:27
  98.4 3.6 %collective-permute-start.15 = (f32[8,128]{1,0:T(8,128)S(1)}, f32[8,128]{1,0:T(8,128)S(1)}, u32[]{:S(2)}, u32[]{:S(2)}) collective-permute-start(f32[8,128]{1,0:T(8,128)S(1)} %add.156), channel_id=1, source_target_pairs={{0,8},{1,9},{2,10},{3,11},{4,12},{5,13},{6,14},{7,15},{8,0},{9,1},... | collective-permute-start | bytes 12296 | tf_op jit(solution)/shard_map/ppermute | solution.py:27
  105.5 7.3 %collective-permute-start.22 = (f32[336,256]{1,0:T(8,128)S(1)}, f32[336,256]{1,0:T(8,128)S(1)}, u32[]{:S(2)}, u32[]{:S(2)}) collective-permute-start(f32[336,256]{1,0:T(8,128)S(1)} %get-tuple-element.35), channel_id=1, source_target_pairs={{0,48},{16,32},{32,16},{48,0},{64,112},{80,96},{96,80},{112,64},{1... | collective-permute-start | bytes 1032200 | tf_op jit(solution)/shard_map/ppermute | solution.py:27
  105.5 11.5 %collective-permute-start.19 = (f32[336,256]{1,0:T(8,128)S(1)}, f32[336,256]{1,0:T(8,128)S(1)}, u32[]{:S(2)}, u32[]{:S(2)}) collective-permute-start(f32[336,256]{1,0:T(8,128)S(1)} %get-tuple-element.30), channel_id=1, source_target_pairs={{0,16},{16,0},{32,48},{48,32},{64,80},{80,64},{96,112},{112,96},{1... | collective-permute-start | bytes 1032200 | tf_op jit(solution)/shard_map/ppermute | solution.py:27
  110.4 11.4 %collective-permute-start.16 = (f32[352,256]{1,0:T(8,128)S(1)}, f32[352,256]{1,0:T(8,128)S(1)}, u32[]{:S(2)}, u32[]{:S(2)}) collective-permute-start(f32[352,256]{1,0:T(8,128)S(1)} %get-tuple-element.28), channel_id=1, source_target_pairs={{0,64},{16,80},{32,96},{48,112},{64,0},{80,16},{96,32},{112,48},{1... | collective-permute-start | bytes 1081352 | tf_op jit(solution)/shard_map/ppermute | solution.py:27
  112.8 15.7 %collective-permute-start.23 = (f32[2,336,256]{2,1,0:T(8,128)S(1)}, f32[2,336,256]{2,1,0:T(8,128)S(1)}, u32[]{:S(2)}, u32[]{:S(2)}) collective-permute-start(f32[2,336,256]{2,1,0:T(8,128)S(1)} %pad_maximum_fusion.7), channel_id=1, source_target_pairs={{0,16},{16,0},{32,48},{48,32},{64,80},{80,64},{96,112},{112,96},{1... | collective-permute-start | bytes 2064392 | tf_op jit(solution)/shard_map/ppermute | solution.py:27
  117.0 20.0 %collective-permute-start.20 = (f32[2,336,256]{2,1,0:T(8,128)S(1)}, f32[2,336,256]{2,1,0:T(8,128)S(1)}, u32[]{:S(2)}, u32[]{:S(2)}) collective-permute-start(f32[2,336,256]{2,1,0:T(8,128)S(1)} %pad_maximum_fusion.6), channel_id=1, source_target_pairs={{0,64},{16,80},{32,96},{48,112},{64,0},{80,16},{96,32},{112,48},{1... | collective-permute-start | bytes 2064392 | tf_op jit(solution)/shard_map/ppermute | solution.py:27
  121.8 18.5 %collective-permute-start.17 = (f32[2,352,256]{2,1,0:T(8,128)S(1)}, f32[2,352,256]{2,1,0:T(8,128)S(1)}, u32[]{:S(2)}, u32[]{:S(2)}) collective-permute-start(f32[2,352,256]{2,1,0:T(8,128)S(1)} %pad_maximum_fusion.5), channel_id=1, source_target_pairs={{0,48},{16,32},{32,16},{48,0},{64,112},{80,96},{96,80},{112,64},{1... | collective-permute-start | bytes 2162696 | tf_op jit(solution)/shard_map/ppermute | solution.py:27
  128.5 9.7 %copy-start.6 = (f32[2,336,256]{2,1,0:T(8,128)}, f32[2,336,256]{2,1,0:T(8,128)S(1)}, u32[]{:S(2)}) copy-start(f32[2,336,256]{2,1,0:T(8,128)S(1)} %collective-permute-done.23) | copy-start | bytes 2064388
  128.6 59.7 %collective-permute-start.24 = (f32[4,336,256]{2,1,0:T(8,128)S(1)}, f32[4,336,256]{2,1,0:T(8,128)}, u32[]{:S(2)}, u32[]{:S(2)}) collective-permute-start(f32[4,336,256]{2,1,0:T(8,128)S(1)} %pad_maximum_fusion.2.refs_3_), channel_id=1, source_target_pairs={{0,64},{16,80},{32,96},{48,112},{64,0},{80,16},{96,32},{112,48},{1... | collective-permute-start | bytes 4128776 | tf_op jit(solution)/shard_map/ppermute | solution.py:27
  138.2 50.2 %collective-permute-start.21 = (f32[4,336,256]{2,1,0:T(8,128)}, f32[4,336,256]{2,1,0:T(8,128)}, u32[]{:S(2)}, u32[]{:S(2)}) collective-permute-start(f32[4,336,256]{2,1,0:T(8,128)} %pad_maximum_fusion.1.refs_2_), channel_id=1, source_target_pairs={{0,48},{16,32},{32,16},{48,0},{64,112},{80,96},{96,80},{112,64},{1... | collective-permute-start | bytes 4128776 | tf_op jit(solution)/shard_map/ppermute | solution.py:27
  140.4 0.9 copy-start.4
  141.2 48.8 %collective-permute-start.18 = (f32[4,352,256]{2,1,0:T(8,128)S(1)}, f32[4,352,256]{2,1,0:T(8,128)}, u32[]{:S(2)}, u32[]{:S(2)}) collective-permute-start(f32[4,352,256]{2,1,0:T(8,128)S(1)} %pad_maximum_fusion.refs_1_), channel_id=1, source_target_pairs={{0,16},{16,0},{32,48},{48,32},{64,80},{80,64},{96,112},{112,96},{1... | collective-permute-start | bytes 4325384 | tf_op jit(solution)/shard_map/ppermute | solution.py:27
  141.4 46.9 %collective-permute-start.25 = (f32[1024,256]{1,0:T(8,128)}, f32[1024,256]{1,0:T(8,128)}, u32[]{:S(2)}, u32[]{:S(2)}) collective-permute-start(f32[1024,256]{1,0:T(8,128)} %bitcast.11), channel_id=1, source_target_pairs={{0,16},{16,32},{32,48},{48,64},{64,80},{80,96},{96,112},{112,0},{1... | collective-permute-start | bytes 3145736 | tf_op jit(solution)/shard_map/ppermute | solution.py:186
  145.5 3.4 %copy-start.1 = (f32[2,512,2048]{2,1,0:T(8,128)S(1)}, f32[2,512,2048]{2,1,0:T(8,128)}, u32[]{:S(2)}) copy-start(f32[2,512,2048]{2,1,0:T(8,128)} %param.3) | copy-start | bytes 25165828
  148.9 39.5 %copy-start.7 = (f32[2,336,256]{2,1,0:T(8,128)S(1)}, f32[2,336,256]{2,1,0:T(8,128)}, u32[]{:S(2)}) copy-start(f32[2,336,256]{2,1,0:T(8,128)} %copy-done.6) | copy-start | bytes 2064388
  152.6 37.4 %copy-start.5 = (f32[2,352,256]{2,1,0:T(8,128)S(1)}, f32[2,352,256]{2,1,0:T(8,128)}, u32[]{:S(2)}) copy-start(f32[2,352,256]{2,1,0:T(8,128)} %copy-done.4) | copy-start | bytes 2162692
  192.2 3.4 %copy-start.2 = (f32[2,512,2048]{2,1,0:T(8,128)S(1)}, f32[2,512,2048]{2,1,0:T(8,128)}, u32[]{:S(2)}) copy-start(f32[2,512,2048]{2,1,0:T(8,128)} %param.3) | copy-start | bytes 25165828

commit v2 on v1

v2 whole, which is shorter than its diff:
```python
import functools

import jax
import jax.numpy as jnp
from jax import lax
from jax.experimental import pallas as pl
from jax.experimental.pallas import tpu as pltpu
from jax.sharding import PartitionSpec as P

D = 8192
LAYERS = 2
KV2 = 2048

outer_beta = 0.9
outer_rate = 0.7
clip_rms = 1.0

grad_gain = outer_rate * (1.0 + outer_beta)
momentum_gain = outer_rate * outer_beta * outer_beta

FLIP = (1, 3, 4)
ORDERS = ((0, 1, 2), (1, 2, 0), (2, 0, 1))


def exchange(value, flip, axis, size):
    return lax.ppermute(value, axis, [(i, i ^ flip) for i in range(size)])


def tie(*values):
    return lax.optimization_barrier(values)


def flip_of(order, bits):
    total = 0
    for edge, bit in zip(order, bits):
        if bit:
            total ^= FLIP[edge]
    return total


def part_rows(rows):
    unit = 16
    tiles = rows // unit
    counts = [tiles // 3 + (1 if k < tiles % 3 else 0) for k in range(3)]
    starts = [sum(counts[:k]) for k in range(3)]
    return [(s * unit, c * unit) for s, c in zip(starts, counts)]


def flips(k, *bits):
    return flip_of(ORDERS[k], bits)


FIRST = ((1, 1, 0), (1, 1, 1))
SECOND = ((1, 0, 0), (1, 0, 1))
KEPT = ((0, 0, 0), (0, 0, 1), (0, 1, 0), (0, 1, 1))


def block_at(own, flip, block_cols):
    return pl.ds(pl.multiple_of((own ^ flip) * block_cols, block_cols), block_cols)


def in_hbm(value):
    return pltpu.with_memory_space_constraint(value, pltpu.HBM)


def drift_kernel(spans, block_cols, items, n_outs, g_ref, r_ref, *rest):
    outs, (g_buf, r_buf, g_sem, r_sem, o_sem) = rest[:n_outs], rest[n_outs:]
    own = lax.axis_index("replica")

    def loads(n):
        k, flip, _, _ = items[n]
        start, count = spans[k]
        place = (pl.ds(start, count), block_at(own, flip, block_cols))
        return (
            pltpu.make_async_copy(g_ref.at[place], g_buf.at[n, pl.ds(0, count)], g_sem.at[n]),
            pltpu.make_async_copy(r_ref.at[place], r_buf.at[n, pl.ds(0, count)], r_sem.at[n]),
        )

    def store(n):
        k, _, out, j = items[n]
        return pltpu.make_async_copy(g_buf.at[n, pl.ds(0, spans[k][1])], outs[out].at[j], o_sem.at[n])

    for n in range(len(items)):
        for copy in loads(n):
            copy.start()
    for n in range(len(items)):
        for copy in loads(n):
            copy.wait()
        count = spans[items[n][0]][1]
        g_buf[n, :count] = g_buf[n, :count] - r_buf[n, :count].astype(jnp.float32)
        store(n).start()
    for n in range(len(items)):
        store(n).wait()


def drift(g, r, spans, block_cols, groups):
    items, shapes = [], []
    for i, group in enumerate(groups):
        for k in range(3):
            shapes.append(jax.ShapeDtypeStruct((len(group), spans[k][1], block_cols), jnp.float32))
        for j, bits in enumerate(group):
            items += [(k, flips(k, *bits), 3 * i + k, j) for k in range(3)]
    most = max(count for _, count in spans)
    n = len(items)
    outs = pl.pallas_call(
        functools.partial(drift_kernel, spans, block_cols, items, len(shapes)),
        out_shape=shapes,
        in_specs=[pl.BlockSpec(memory_space=pltpu.HBM)] * 2,
        out_specs=[pl.BlockSpec(memory_space=pl.ANY)] * len(shapes),
        scratch_shapes=[
            pltpu.VMEM((n, most, block_cols), jnp.float32),
            pltpu.VMEM((n, most, block_cols), jnp.bfloat16),
            pltpu.SemaphoreType.DMA((n,)),
            pltpu.SemaphoreType.DMA((n,)),
            pltpu.SemaphoreType.DMA((n,)),
        ],
        compiler_params=pltpu.CompilerParams(vmem_limit_bytes=16 * 1024 * 1024),
        cost_estimate=pl.CostEstimate(flops=n * most * block_cols, bytes_accessed=10 * n * most * block_cols, transcendentals=0),
        name="drift",
    )(in_hbm(g), in_hbm(r))
    return [outs[3 * i : 3 * i + 3] for i in range(len(groups))]


def apply_kernel(spans, block_cols, items, priors, n_us, before, *refs):
    g_ref, us, (m_ref,) = refs[0], refs[1 : 1 + n_us], refs[1 + n_us : 2 + n_us]
    rest = refs[2 + n_us + before :]
    out_ref, b_ref, g_buf, u_buf, m_buf, v_buf, g_sem, u_sem, m_sem, v_sem, o_sem, b_sem = rest
    own = lax.axis_index("replica")
    back = own ^ lax.rem(own + 7, 8)

    def source(where):
        which, j = where
        return us[which] if j is None else us[which].at[j]

    def loads(n):
        k, flip, where = items[n]
        start, count = spans[k]
        return (
            pltpu.make_async_copy(
                g_ref.at[pl.ds(start, count), block_at(own, flip, block_cols)], g_buf.at[n, pl.ds(0, count)], g_sem.at[n]
            ),
            pltpu.make_async_copy(source(where), u_buf.at[n, pl.ds(0, count)], u_sem.at[n]),
        )

    def store(n):
        k, flip, _ = items[n]
        start, count = spans[k]
        return pltpu.make_async_copy(
            g_buf.at[n, pl.ds(0, count)], out_ref.at[pl.ds(start, count), block_at(own, flip, block_cols)], o_sem.at[n]
        )

    def prior_loads(i):
        k, wheres = priors[i]
        start, count = spans[k]
        m_copy = pltpu.make_async_copy(m_ref.at[pl.ds(start, count)], m_buf.at[i, pl.ds(0, count)], m_sem.at[i])
        v_copies = [
            (flip, pltpu.make_async_copy(source(where), v_buf.at[i, pl.ds(0, count)], v_sem.at[i])) for flip, where in wheres
        ]
        return m_copy, v_copies

    def prior_store(i):
        start, count = spans[priors[i][0]]
        return pltpu.make_async_copy(m_buf.at[i, pl.ds(0, count)], b_ref.at[pl.ds(start, count)], b_sem.at[i])

    for n in range(len(items)):
        for copy in loads(n):
            copy.start()
    for i in range(len(priors)):
        m_copy, v_copies = prior_loads(i)
        m_copy.start()
        for flip, copy in v_copies:
            pl.when(back == flip)(copy.start)
    for n in range(len(items)):
        for copy in loads(n):
            copy.wait()
        count = spans[items[n][0]][1]
        g_buf[n, :count] = g_buf[n, :count] - u_buf[n, :count]
        store(n).start()
    for i in range(len(priors)):
        m_copy, v_copies = prior_loads(i)
        m_copy.wait()
        v_copies[0][1].wait()
        count = spans[priors[i][0]][1]
        m_buf[i, :count] = v_buf[i, :count] * (1.0 / grad_gain) + (outer_beta - momentum_gain / grad_gain) * m_buf[i, :count]
        prior_store(i).start()
    for n in range(len(items)):
        store(n).wait()
    for i in range(len(priors)):
        prior_store(i).wait()


def apply(g, us, prior_m, spans, block_cols, items, priors, before=None):
    most = max(count for _, count in spans)
    n, p = len(items), len(priors)
    operands = [in_hbm(g), *us, prior_m] + ([] if before is None else [in_hbm(b) for b in before])
    hbm, anywhere = pl.BlockSpec(memory_space=pltpu.HBM), pl.BlockSpec(memory_space=pl.ANY)
    return pl.pallas_call(
        functools.partial(apply_kernel, spans, block_cols, items, priors, len(us), 0 if before is None else 2),
        out_shape=[jax.ShapeDtypeStruct(g.shape, jnp.float32), jax.ShapeDtypeStruct(prior_m.shape, jnp.float32)],
        in_specs=[hbm] + [anywhere] * (len(us) + 1) + ([] if before is None else [hbm, hbm]),
        out_specs=[hbm, hbm],
        input_output_aliases={} if before is None else {len(us) + 2: 0, len(us) + 3: 1},
        scratch_shapes=[
            pltpu.VMEM((n, most, block_cols), jnp.float32),
            pltpu.VMEM((n, most, block_cols), jnp.float32),
            pltpu.VMEM((p, most, block_cols), jnp.float32),
            pltpu.VMEM((p, most, block_cols), jnp.float32),
            *[pltpu.SemaphoreType.DMA((count,)) for count in (n, n, p, p, n, p)],
        ],
        compiler_params=pltpu.CompilerParams(vmem_limit_bytes=20 * 1024 * 1024),
        cost_estimate=pl.CostEstimate(flops=n * most * block_cols, bytes_accessed=12 * n * most * block_cols, transcendentals=0),
        name="apply",
    )(*operands)


def clip_factor(square_sum):
    element_count = LAYERS * D * KV2
    rms_value = jnp.sqrt(square_sum / element_count + 1e-06)
    return jnp.minimum(1.0, clip_rms / rms_value)


def per_device(global_params, replica_params, momentum):
    replicas = 8
    layers, rows, cols = global_params.shape
    block_cols = cols // replicas
    g = global_params.reshape(layers * rows, cols)
    r = replica_params.reshape(layers * rows, cols)
    m = momentum.reshape(layers * rows, block_cols)
    spans = part_rows(layers * rows)
    parts = range(3)

    def cross(k, step, value):
        return exchange(value, FLIP[ORDERS[k][step]], "replica", replicas)

    (first,) = drift(g, r, spans, block_cols, [FIRST])
    got1 = [cross(k, 0, first[k]) for k in parts]
    (second,) = drift(g, r, spans, block_cols, [SECOND])
    got2 = [cross(k, 0, second[k]) for k in parts]
    (kept,) = drift(g, r, spans, block_cols, [KEPT])
    third = [kept[k][2:] + got1[k] for k in parts]
    got3 = [cross(k, 1, third[k]) for k in parts]
    fourth = [kept[k][1] + got2[k][1] + got3[k][1] for k in parts]
    got4 = [cross(k, 2, fourth[k]) for k in parts]
    grads = [(kept[k][0] + got2[k][0] + got3[k][0] + got4[k]) / replicas for k in parts]

    squares = jnp.broadcast_to(sum(jnp.sum(p * p, axis=0) for p in grads), (8, block_cols))
    squares = squares + exchange(squares, 8, "shard", 16)
    squares = squares + exchange(squares, 4, "replica", replicas)
    squares, m = tie(squares, m)
    prior_m = lax.ppermute(m, "replica", [(i, (i + 1) % replicas) for i in range(replicas)])
    for flip in (2, 6, 1):
        squares = squares + exchange(squares, flip, "shard", 16)
    around = [squares]
    for _ in range(3):
        around.append(lax.ppermute(around[-1], "replica", [(i, i // 4 * 4 + (i + 3) % 4) for i in range(replicas)]))
    squares = (around[0] + around[2]) + (around[1] + around[3])
    factor = clip_factor(jnp.sum(squares[0]))
    factor, prior_m = lax.optimization_barrier((factor, prior_m))

    clipped = [p * factor for p in grads]
    mine = [m[start : start + count] for start, count in spans]
    u = [grad_gain * clipped[k] + momentum_gain * mine[k] for k in parts]
    new_momentum = jnp.concatenate([outer_beta * mine[k] + clipped[k] for k in parts])
    got_c = [cross(k, 2, u[k]) for k in parts]
    pair = [jnp.stack([u[k], got_c[k]]) for k in parts]
    got_b = [cross(k, 1, pair[k]) for k in parts]
    pair = list(tie(*pair))
    pair[2], got_b[1] = tie(pair[2], got_b[1])
    got_ac = [cross(k, 0, pair[k]) for k in parts]
    pair[2], got_b[0] = tie(pair[2], got_b[0])
    got_ab = [cross(k, 0, got_b[k]) for k in parts]

    early = [*u, *got_c, *got_b, *got_ac]
    early_at = [
        ((0, 0, 0), 0, None),
        ((0, 0, 1), 3, None),
        ((0, 1, 0), 6, 0),
        ((0, 1, 1), 6, 1),
        ((1, 0, 0), 9, 0),
        ((1, 0, 1), 9, 1),
    ]
    late_at = [((1, 1, 0), 0, 0), ((1, 1, 1), 0, 1)]
    early_items = [(k, flips(k, *bits), (at + k, j)) for bits, at, j in early_at for k in parts]
    late_items = [(k, flips(k, *bits), (at + k, j)) for bits, at, j in late_at for k in parts]
    early_priors = [(k, [(f, w) for kk, f, w in early_items if kk == k and f in (1, 3, 7)]) for k in (0, 2)]
    late_priors = [(1, [(f, w) for kk, f, w in late_items if kk == 1 and f in (1, 3, 7)])]
    for i, (f, w) in enumerate([(f, w) for kk, f, w in early_items if kk == 1 and f in (1, 3, 7)]):
        late_priors[0][1].append((f, (3 + i, w[1])))
    extra = [early[w[0]] for kk, f, w in early_items if kk == 1 and f in (1, 3, 7)]
    outs = apply(g, early, prior_m, spans, block_cols, early_items, early_priors)
    params, backup = apply(g, [*got_ab, *extra], prior_m, spans, block_cols, late_items, late_priors, outs)
    return (
        params.reshape(layers, rows, cols),
        new_momentum.reshape(layers, rows, block_cols),
        backup.reshape(layers, rows, block_cols),
    )


def solution(mesh):
    in_specs = (
        P(None, "shard", None),
        P("replica", None, "shard", None),
        P(None, "shard", "replica"),
    )
    out_specs = (P(None, "shard", None), P(None, "shard", "replica"), P(None, "shard", "replica"))
    return jax.shard_map(
        per_device, mesh=mesh, in_specs=in_specs, out_specs=out_specs, check_vma=False
    )
```

time: 203 us -> 164 us (0.81); the launches traced: 200 us -> 164 us
  local copies, waits for them, and re-layouts: 13.1 us -> 0.01 us
  waiting for transfers between devices: 109 us -> 97.9 us
  other arithmetic: 13.2 us -> 2.85 us
  starting transfers between devices: 49.1 us -> 44.4 us
  Pallas kernels: 13.5 us -> 17 us
    ppermute x1, waiting for transfers between devices: 35.8 us -> 0.01 us  [per_device(): lax.ppermute(m, 'replica', [(i, (i + 1) % replicas) for i in range(replic...]
    ppermute x25 -> x29, waiting for transfers between devices: 73.4 us -> 89.3 us  [exchange(): return lax.ppermute(value, axis, [(i, i ^ flip) for i in range(size)])]
    unnamed x16 -> x2, local copies, waits for them, and re-layouts: 13.1 us -> 0.01 us
    ppermute x0 -> x3, waiting for transfers between devices: none -> 8.57 us  [per_device(): lax.ppermute(around[-1], 'replica', [(i, i // 4 * 4 + (i + 3) % 4) for i...]
    ppermute x25 -> x29, starting transfers between devices: 47.3 us -> 39.7 us  [exchange(): return lax.ppermute(value, axis, [(i, i ^ flip) for i in range(size)])]
    add x14 -> x11, other arithmetic: 7.41 us -> 0.73 us  [the longest x3 0.27 us: per_device(): third = [kept[k][2:] + got1[k] for k in parts]]
    ppermute x0 -> x3, starting transfers between devices: none -> 4.37 us  [per_device(): lax.ppermute(around[-1], 'replica', [(i, i // 4 * 4 + (i + 3) % 4) for i...]
    concatenate x5 -> x1, other arithmetic: 4.68 us -> 1.04 us  [per_device(): jnp.concatenate([outer_beta * mine[k] + clipped[k] for k in parts])]
  transfers between devices with their start and end apart: 26 -> 33, of which waited for: 16 -> 24; matrix products, arithmetic and copies ran while one was open for 4% -> 2% of each run, Pallas kernels for 3% -> 7%
where the time goes in v2:
time: 164 us
  waiting for transfers between devices  97.9 us (60%)
  starting transfers between devices  44.4 us (27%)
  Pallas kernels  17 us (10%)
  other arithmetic  2.85 us (2%)
  between operations  1.65 us (1%)
    ppermute x29, waiting for transfers between devices, exchange(): return lax.ppermute(value, axis, [(i, i ^ flip) for i in range(size)])  89.3 us
    ppermute x29, starting transfers between devices, exchange(): return lax.ppermute(value, axis, [(i, i ^ flip) for i in range(size)])  39.7 us
    pallas_call x2, Pallas kernels, apply(): pl.pallas_call(functools.partial(apply_kernel, spans, block_cols, items,...  9.23 us
    ppermute x3, waiting for transfers between devices, per_device(): lax.ppermute(around[-1], 'replica', [(i, i // 4 * 4 + (i + 3) % 4) for i...  8.57 us
    pallas_call x3, Pallas kernels, drift(): pl.pallas_call(functools.partial(drift_kernel, spans, block_cols, items,...  7.81 us
    ppermute x3, starting transfers between devices, per_device(): lax.ppermute(around[-1], 'replica', [(i, i // 4 * 4 + (i + 3) % 4) for i...  4.37 us
  transfers between devices with their start and end apart: 33, of which 24 were waited for; matrix products, arithmetic and copies ran while one was open for 2% of the time, Pallas kernels for 7%

profile of v2, /device:TPU:4, one launch (start us, length us, event | category | flops | bytes accessed | tf_op | source)
XLA Modules:
  0.0 163.9 jit_solution(13465080353791522282)
XLA Ops:
  0.6 2.2 %drift.5 = (f32[2,352,256]{2,1,0:T(8,128)S(1)}, f32[2,336,256]{2,1,0:T(8,128)S(1)}, f32[2,336,256]{2,1,0:T(8,128)S(1)}) custom-call(f32[1024,2048]{1,0:T(8,128)} %bitcast.39, bf16[1024,2048]{1,0:T(8,128)(2,1)} %bitcast.44), custom_call_target="tpu_custom_call" | custom-call | flops 540672 | bytes 5406720 | tf_op jit(solution)/shard_map/drift/pallas_call | solution.py:105
  2.9 3.3 %collective-permute-start.9 = (f32[2,336,256]{2,1,0:T(8,128)S(1)}, f32[2,336,256]{2,1,0:T(8,128)S(1)}, u32[]{:S(2)}, u32[]{:S(2)}) collective-permute-start(f32[2,336,256]{2,1,0:T(8,128)S(1)} %get-tuple-element.34), channel_id=1, source_target_pairs={{0,64},{16,80},{32,96},{48,112},{64,0},{80,16},{96,32},{112,48},{1... | collective-permute-start | bytes 2064392 | tf_op jit(solution)/shard_map/ppermute | solution.py:26
  6.1 0.5 collective-permute-start.5
  6.7 1.1 collective-permute-start.1
  7.8 2.2 %drift.4 = (f32[2,352,256]{2,1,0:T(8,128)S(1)}, f32[2,336,256]{2,1,0:T(8,128)S(1)}, f32[2,336,256]{2,1,0:T(8,128)S(1)}) custom-call(f32[1024,2048]{1,0:T(8,128)} %bitcast.40, bf16[1024,2048]{1,0:T(8,128)(2,1)} %bitcast.45), custom_call_target="tpu_custom_call" | custom-call | flops 540672 | bytes 5406720 | tf_op jit(solution)/shard_map/drift/pallas_call | solution.py:105
  10.0 2.2 %collective-permute-start.4 = (f32[2,336,256]{2,1,0:T(8,128)S(1)}, f32[2,336,256]{2,1,0:T(8,128)S(1)}, u32[]{:S(2)}, u32[]{:S(2)}) collective-permute-start(f32[2,336,256]{2,1,0:T(8,128)S(1)} %get-tuple-element.30), channel_id=1, source_target_pairs={{0,48},{16,32},{32,16},{48,0},{64,112},{80,96},{96,80},{112,64},{1... | collective-permute-start | bytes 2064392 | tf_op jit(solution)/shard_map/ppermute | solution.py:26
  12.3 0.3 collective-permute-start.8
  12.6 3.4 %drift.3 = (f32[4,352,256]{2,1,0:T(8,128)S(1)}, f32[4,336,256]{2,1,0:T(8,128)S(1)}, f32[4,336,256]{2,1,0:T(8,128)S(1)}) custom-call(f32[1024,2048]{1,0:T(8,128)} %bitcast.41, bf16[1024,2048]{1,0:T(8,128)(2,1)} %bitcast.46), custom_call_target="tpu_custom_call" | custom-call | flops 1081344 | bytes 10813440 | tf_op jit(solution)/shard_map/drift/pallas_call | solution.py:105
  16.0 6.8 %collective-permute-done.9 = f32[2,336,256]{2,1,0:T(8,128)S(1)} collective-permute-done((f32[2,336,256]{2,1,0:T(8,128)S(1)}, f32[2,336,256]{2,1,0:T(8,128)S(1)}, u32[]{:S(2)}, u32[]{:S(2)}) %collective-permute-start.9) | collective-permute-done | bytes 688160 | tf_op jit(solution)/shard_map/ppermute | solution.py:26
  22.8 1.2 collective-permute-start
  24.0 0.1 slice_add_fusion.1
  24.1 0.4 collective-permute-done.5
  24.5 2.4 %collective-permute-start.10 = (f32[2,336,256]{2,1,0:T(8,128)S(1)}, f32[2,336,256]{2,1,0:T(8,128)S(1)}, u32[]{:S(2)}, u32[]{:S(2)}) collective-permute-start(f32[2,336,256]{2,1,0:T(8,128)S(1)} %slice_add_fusion.1), channel_id=1, source_target_pairs={{0,16},{16,0},{32,48},{48,32},{64,80},{80,64},{96,112},{112,96},{1... | collective-permute-start | bytes 2064392 | tf_op jit(solution)/shard_map/ppermute | solution.py:26
  26.9 0.1 slice_add_fusion.2
  27.0 1.3 collective-permute-start.6
  28.4 0.1 slice_add_fusion
  28.4 9.1 %collective-permute-done.8 = f32[2,336,256]{2,1,0:T(8,128)S(1)} collective-permute-done((f32[2,336,256]{2,1,0:T(8,128)S(1)}, f32[2,336,256]{2,1,0:T(8,128)S(1)}, u32[]{:S(2)}, u32[]{:S(2)}) %collective-permute-start.8) | collective-permute-done | bytes 688160 | tf_op jit(solution)/shard_map/ppermute | solution.py:26
  37.5 0.5 collective-permute-start.2
  38.0 16.1 %collective-permute-done.10 = f32[2,336,256]{2,1,0:T(8,128)S(1)} collective-permute-done((f32[2,336,256]{2,1,0:T(8,128)S(1)}, f32[2,336,256]{2,1,0:T(8,128)S(1)}, u32[]{:S(2)}, u32[]{:S(2)}) %collective-permute-start.10) | collective-permute-done | bytes 688160 | tf_op jit(solution)/shard_map/ppermute | solution.py:26
  54.3 1.6 collective-permute-start.11
  56.0 2.4 %collective-permute-start.7 = (f32[336,256]{1,0:T(8,128)S(1)}, f32[336,256]{1,0:T(8,128)S(1)}, u32[]{:S(2)}, u32[]{:S(2)}) collective-permute-start(f32[336,256]{1,0:T(8,128)S(1)} %fusion.6), channel_id=1, source_target_pairs={{0,16},{16,0},{32,48},{48,32},{64,80},{80,64},{96,112},{112,96},{1... | collective-permute-start | bytes 1032200 | tf_op jit(solution)/shard_map/ppermute | solution.py:26
  58.5 0.5 collective-permute-start.3
  58.9 3.6 %collective-permute-done.11 = f32[336,256]{1,0:T(8,128)S(1)} collective-permute-done((f32[336,256]{1,0:T(8,128)S(1)}, f32[336,256]{1,0:T(8,128)S(1)}, u32[]{:S(2)}, u32[]{:S(2)}) %collective-permute-start.11) | collective-permute-done | bytes 344096 | tf_op jit(solution)/shard_map/ppermute | solution.py:26
  62.5 0.1 multiply_reduce_fusion.1
  62.6 2.1 %collective-permute-done.7 = f32[336,256]{1,0:T(8,128)S(1)} collective-permute-done((f32[336,256]{1,0:T(8,128)S(1)}, f32[336,256]{1,0:T(8,128)S(1)}, u32[]{:S(2)}, u32[]{:S(2)}) %collective-permute-start.7) | collective-permute-done | bytes 344096 | tf_op jit(solution)/shard_map/ppermute | solution.py:26
  64.7 0.1 multiply_reduce_fusion.2
  64.8 3.5 %collective-permute-done.3 = f32[352,256]{1,0:T(8,128)S(1)} collective-permute-done((f32[352,256]{1,0:T(8,128)S(1)}, f32[352,256]{1,0:T(8,128)S(1)}, u32[]{:S(2)}, u32[]{:S(2)}) %collective-permute-start.3) | collective-permute-done | bytes 360480 | tf_op jit(solution)/shard_map/ppermute | solution.py:26
  68.2 0.1 multiply_reduce_fusion
  68.4 0.8 collective-permute-start.12
  69.1 3.0 %collective-permute-done.12 = f32[8,256]{1,0:T(8,128)S(1)} collective-permute-done((f32[8,256]{1,0:T(8,128)S(1)}, f32[8,256]{1,0:T(8,128)S(1)}, u32[]{:S(2)}, u32[]{:S(2)}) %collective-permute-start.12) | collective-permute-done | bytes 8224 | tf_op jit(solution)/shard_map/ppermute | solution.py:26
  72.1 0.2 collective-permute-start.13
  72.3 5.0 %collective-permute-done.13 = f32[8,256]{1,0:T(8,128)S(1)} collective-permute-done((f32[8,256]{1,0:T(8,128)S(1)}, f32[8,256]{1,0:T(8,128)S(1)}, u32[]{:S(2)}, u32[]{:S(2)}) %collective-permute-start.13) | collective-permute-done | bytes 8224 | tf_op jit(solution)/shard_map/ppermute | solution.py:26
  77.3 0.4 collective-permute-start.20
  77.7 1.9 %collective-permute-start.14 = (f32[8,256]{1,0:T(8,128)S(1)}, f32[8,256]{1,0:T(8,128)S(1)}, u32[]{:S(2)}, u32[]{:S(2)}) collective-permute-start(f32[8,256]{1,0:T(8,128)S(1)} %fusion.14), channel_id=1, source_target_pairs={{0,2},{1,3},{2,0},{3,1},{4,6},{5,7},{6,4},{7,5},{8,10},{9,11},{10,... | collective-permute-start | bytes 24584 | tf_op jit(solution)/shard_map/ppermute | solution.py:26
  79.6 1.7 %collective-permute-done.14 = f32[8,256]{1,0:T(8,128)S(1)} collective-permute-done((f32[8,256]{1,0:T(8,128)S(1)}, f32[8,256]{1,0:T(8,128)S(1)}, u32[]{:S(2)}, u32[]{:S(2)}) %collective-permute-start.14) | collective-permute-done | bytes 8224 | tf_op jit(solution)/shard_map/ppermute | solution.py:26
  81.3 4.0 %collective-permute-start.15 = (f32[8,256]{1,0:T(8,128)S(1)}, f32[8,256]{1,0:T(8,128)S(1)}, u32[]{:S(2)}, u32[]{:S(2)}) collective-permute-start(f32[8,256]{1,0:T(8,128)S(1)} %add.157), channel_id=1, source_target_pairs={{0,6},{1,7},{2,4},{3,5},{4,2},{5,3},{6,0},{7,1},{8,14},{9,15},{10,... | collective-permute-start | bytes 24584 | tf_op jit(solution)/shard_map/ppermute | solution.py:26
  85.3 1.6 collective-permute-done.15
  87.0 1.2 collective-permute-done.16
  88.2 1.7 %collective-permute-start.17 = (f32[8,256]{1,0:T(8,128)S(1)}, f32[8,256]{1,0:T(8,128)S(1)}, u32[]{:S(2)}, u32[]{:S(2)}) collective-permute-start(f32[8,256]{1,0:T(8,128)S(1)} %add.159), channel_id=1, source_target_pairs={{0,48},{16,0},{32,16},{48,32},{64,112},{80,64},{96,80},{112,96},{1... | collective-permute-start | bytes 24584 | tf_op jit(solution)/shard_map/ppermute | solution.py:255
  89.9 1.9 %collective-permute-done.17 = f32[8,256]{1,0:T(8,128)S(1)} collective-permute-done((f32[8,256]{1,0:T(8,128)S(1)}, f32[8,256]{1,0:T(8,128)S(1)}, u32[]{:S(2)}, u32[]{:S(2)}) %collective-permute-start.17) | collective-permute-done | bytes 8224 | tf_op jit(solution)/shard_map/ppermute | solution.py:255
  91.8 1.7 %collective-permute-start.18 = (f32[8,256]{1,0:T(8,128)S(1)}, f32[8,256]{1,0:T(8,128)S(1)}, u32[]{:S(2)}, u32[]{:S(2)}) collective-permute-start(f32[8,256]{1,0:T(8,128)S(1)} %collective-permute-done.17), channel_id=1, source_target_pairs={{0,48},{16,0},{32,16},{48,32},{64,112},{80,64},{96,80},{112,96},{1... | collective-permute-start | bytes 24584 | tf_op jit(solution)/shard_map/ppermute | solution.py:255
  93.5 2.7 %collective-permute-done.18 = f32[8,256]{1,0:T(8,128)S(1)} collective-permute-done((f32[8,256]{1,0:T(8,128)S(1)}, f32[8,256]{1,0:T(8,128)S(1)}, u32[]{:S(2)}, u32[]{:S(2)}) %collective-permute-start.18) | collective-permute-done | bytes 8224 | tf_op jit(solution)/shard_map/ppermute | solution.py:255
  96.2 0.9 collective-permute-start.19
  97.2 3.9 %collective-permute-done.19 = f32[8,256]{1,0:T(8,128)S(1)} collective-permute-done((f32[8,256]{1,0:T(8,128)S(1)}, f32[8,256]{1,0:T(8,128)S(1)}, u32[]{:S(2)}, u32[]{:S(2)}) %collective-permute-start.19) | collective-permute-done | bytes 8224 | tf_op jit(solution)/shard_map/ppermute | solution.py:255
  101.1 0.6 fusion.10
  102.4 0.2 multiply_add_fusion.3
  102.6 3.3 %collective-permute-start.22 = (f32[336,256]{1,0:T(8,128)S(1)}, f32[336,256]{1,0:T(8,128)S(1)}, u32[]{:S(2)}, u32[]{:S(2)}) collective-permute-start(f32[336,256]{1,0:T(8,128)S(1)} %get-tuple-element.58.refs_2_), channel_id=1, source_target_pairs={{0,16},{16,0},{32,48},{48,32},{64,80},{80,64},{96,112},{112,96},{1... | collective-permute-start | bytes 1032200 | tf_op jit(solution)/shard_map/ppermute | solution.py:26
  106.0 1.8 %collective-permute-start.21 = (f32[352,256]{1,0:T(8,128)S(1)}, f32[352,256]{1,0:T(8,128)S(1)}, u32[]{:S(2)}, u32[]{:S(2)}) collective-permute-start(f32[352,256]{1,0:T(8,128)S(1)} %get-tuple-element.56.refs_1_), channel_id=1, source_target_pairs={{0,64},{16,80},{32,96},{48,112},{64,0},{80,16},{96,32},{112,48},{1... | collective-permute-start | bytes 1081352 | tf_op jit(solution)/shard_map/ppermute | solution.py:26
  107.8 3.3 %collective-permute-done.22.refs_5_.refs_4_ = f32[336,256]{1,0:T(8,128)S(1)} collective-permute-done((f32[336,256]{1,0:T(8,128)S(1)}, f32[336,256]{1,0:T(8,128)S(1)}, u32[]{:S(2)}, u32[]{:S(2)}) %collective-permute-start.22) | collective-permute-done | bytes 344096 | tf_op jit(solution)/shard_map/ppermute | solution.py:26
  111.2 1.8 %collective-permute-start.24 = (f32[2,336,256]{2,1,0:T(8,128)S(1)}, f32[2,336,256]{2,1,0:T(8,128)S(1)}, u32[]{:S(2)}, u32[]{:S(2)}) collective-permute-start(f32[2,336,256]{2,1,0:T(8,128)S(1)} %pad_maximum_fusion.2), channel_id=1, source_target_pairs={{0,64},{16,80},{32,96},{48,112},{64,0},{80,16},{96,32},{112,48},{1... | collective-permute-start | bytes 2064392 | tf_op jit(solution)/shard_map/ppermute | solution.py:26
  113.0 5.8 %collective-permute-done.21.refs_4_ = f32[352,256]{1,0:T(8,128)S(1)} collective-permute-done((f32[352,256]{1,0:T(8,128)S(1)}, f32[352,256]{1,0:T(8,128)S(1)}, u32[]{:S(2)}, u32[]{:S(2)}) %collective-permute-start.21) | collective-permute-done | bytes 360480 | tf_op jit(solution)/shard_map/ppermute | solution.py:26
  119.1 2.1 %collective-permute-start.30 = (f32[2,336,256]{2,1,0:T(8,128)S(1)}, f32[2,336,256]{2,1,0:T(8,128)S(1)}, u32[]{:S(2)}, u32[]{:S(2)}) collective-permute-start(f32[2,336,256]{2,1,0:T(8,128)S(1)} %pad_maximum_fusion.2), channel_id=1, source_target_pairs={{0,48},{16,32},{32,16},{48,0},{64,112},{80,96},{96,80},{112,64},{1... | collective-permute-start | bytes 2064392 | tf_op jit(solution)/shard_map/ppermute | solution.py:26
  121.1 2.5 %collective-permute-start.31 = (f32[2,352,256]{2,1,0:T(8,128)S(1)}, f32[2,352,256]{2,1,0:T(8,128)S(1)}, u32[]{:S(2)}, u32[]{:S(2)}) collective-permute-start(f32[2,352,256]{2,1,0:T(8,128)S(1)} %pad_maximum_fusion.1), channel_id=1, source_target_pairs={{0,16},{16,0},{32,48},{48,32},{64,80},{80,64},{96,112},{112,96},{1... | collective-permute-start | bytes 2162696 | tf_op jit(solution)/shard_map/ppermute | solution.py:26
  123.7 6.0 %collective-permute-done.24.refs_8_ = f32[2,336,256]{2,1,0:T(8,128)S(1)} collective-permute-done((f32[2,336,256]{2,1,0:T(8,128)S(1)}, f32[2,336,256]{2,1,0:T(8,128)S(1)}, u32[]{:S(2)}, u32[]{:S(2)}) %collective-permute-start.24) | collective-permute-done | bytes 688160 | tf_op jit(solution)/shard_map/ppermute | solution.py:26
  129.7 8.1 %collective-permute-done.25.refs_7_ = f32[2,352,256]{2,1,0:T(8,128)S(1)} collective-permute-done((f32[2,352,256]{2,1,0:T(8,128)S(1)}, f32[2,352,256]{2,1,0:T(8,128)S(1)}, u32[]{:S(2)}, u32[]{:S(2)}) %collective-permute-start.25) | collective-permute-done | bytes 720928 | tf_op jit(solution)/shard_map/ppermute | solution.py:26
  137.8 1.8 %collective-permute-start.32 = (f32[2,336,256]{2,1,0:T(8,128)S(1)}, f32[2,336,256]{2,1,0:T(8,128)S(1)}, u32[]{:S(2)}, u32[]{:S(2)}) collective-permute-start(f32[2,336,256]{2,1,0:T(8,128)S(1)} %pad_maximum_fusion.3), channel_id=1, source_target_pairs={{0,64},{16,80},{32,96},{48,112},{64,0},{80,16},{96,32},{112,48},{1... | collective-permute-start | bytes 2064392 | tf_op jit(solution)/shard_map/ppermute | solution.py:26
  139.7 1.7 %collective-permute-start.29 = (f32[2,336,256]{2,1,0:T(8,128)S(1)}, f32[2,336,256]{2,1,0:T(8,128)S(1)}, u32[]{:S(2)}, u32[]{:S(2)}) collective-permute-start(f32[2,336,256]{2,1,0:T(8,128)S(1)} %collective-permute-done.28.refs_9_), channel_id=1, source_target_pairs={{0,64},{16,80},{32,96},{48,112},{64,0},{80,16},{96,32},{112,48},{1... | collective-permute-start | bytes 2064392 | tf_op jit(solution)/shard_map/ppermute | solution.py:26
  141.4 8.6 %collective-permute-done.30.refs_11_.refs_5_ = f32[2,336,256]{2,1,0:T(8,128)S(1)} collective-permute-done((f32[2,336,256]{2,1,0:T(8,128)S(1)}, f32[2,336,256]{2,1,0:T(8,128)S(1)}, u32[]{:S(2)}, u32[]{:S(2)}) %collective-permute-start.30) | collective-permute-done | bytes 688160 | tf_op jit(solution)/shard_map/ppermute | solution.py:26
  149.9 1.0 pad_maximum_fusion
  151.1 1.3 collective-permute-done.32.refs_12_
  152.4 6.4 %apply.2 = (f32[1024,2048]{1,0:T(8,128)}, f32[1024,256]{1,0:T(8,128)}) custom-call(f32[1024,2048]{1,0:T(8,128)} %bitcast.42, f32[352,256]{1,0:T(8,128)S(1)} %get-tuple-element.56.refs_1_, f32[336,256]{1,0:T(8,128)S(1)} %get-tuple-element.58.refs_2_, f32[336,256]{1,0:T(8,128)S(1)} %get-tuple-element.61.refs_3_, ...), custom_call_target="tpu_custom_call" | custom-call | flops 1622016 | bytes 19464192 | tf_op jit(solution)/shard_map/apply/pallas_call | solution.py:197
  158.8 1.0 collective-permute-done.29.refs_3_
  159.8 1.1 collective-permute-done.27.refs_2_
  160.9 2.8 %apply.3 = (f32[1024,2048]{1,0:T(8,128)}, f32[1024,256]{1,0:T(8,128)}) custom-call(f32[1024,2048]{1,0:T(8,128)} %bitcast.43, f32[2,352,256]{2,1,0:T(8,128)S(1)} %collective-permute-done.26.refs_1_, f32[2,336,256]{2,1,0:T(8,128)S(1)} %collective-permute-done.27.refs_2_, ...), custom_call_target="tpu_custom_call", output_to_operand_aliasing={{0}: (7, {}), {1}: (8, {})} | custom-call | flops 540672 | bytes 6488064 | tf_op jit(solution)/shard_map/apply/pallas_call | solution.py:197
  (32 shorter events, 0.7 us)
Async XLA Ops:
  2.9 19.9 %collective-permute-start.9 = (f32[2,336,256]{2,1,0:T(8,128)S(1)}, f32[2,336,256]{2,1,0:T(8,128)S(1)}, u32[]{:S(2)}, u32[]{:S(2)}) collective-permute-start(f32[2,336,256]{2,1,0:T(8,128)S(1)} %get-tuple-element.34), channel_id=1, source_target_pairs={{0,64},{16,80},{32,96},{48,112},{64,0},{80,16},{96,32},{112,48},{1... | collective-permute-start | bytes 2064392 | tf_op jit(solution)/shard_map/ppermute | solution.py:26
  6.1 18.4 %collective-permute-start.5 = (f32[2,336,256]{2,1,0:T(8,128)S(1)}, f32[2,336,256]{2,1,0:T(8,128)S(1)}, u32[]{:S(2)}, u32[]{:S(2)}) collective-permute-start(f32[2,336,256]{2,1,0:T(8,128)S(1)} %get-tuple-element.31), channel_id=1, source_target_pairs={{0,48},{16,32},{32,16},{48,0},{64,112},{80,96},{96,80},{112,64},{1... | collective-permute-start | bytes 2064392 | tf_op jit(solution)/shard_map/ppermute | solution.py:26
  6.7 20.3 %collective-permute-start.1 = (f32[2,352,256]{2,1,0:T(8,128)S(1)}, f32[2,352,256]{2,1,0:T(8,128)S(1)}, u32[]{:S(2)}, u32[]{:S(2)}) collective-permute-start(f32[2,352,256]{2,1,0:T(8,128)S(1)} %get-tuple-element.28), channel_id=1, source_target_pairs={{0,16},{16,0},{32,48},{48,32},{64,80},{80,64},{96,112},{112,96},{1... | collective-permute-start | bytes 2162696 | tf_op jit(solution)/shard_map/ppermute | solution.py:26
  10.0 45.9 %collective-permute-start.4 = (f32[2,336,256]{2,1,0:T(8,128)S(1)}, f32[2,336,256]{2,1,0:T(8,128)S(1)}, u32[]{:S(2)}, u32[]{:S(2)}) collective-permute-start(f32[2,336,256]{2,1,0:T(8,128)S(1)} %get-tuple-element.30), channel_id=1, source_target_pairs={{0,48},{16,32},{32,16},{48,0},{64,112},{80,96},{96,80},{112,64},{1... | collective-permute-start | bytes 2064392 | tf_op jit(solution)/shard_map/ppermute | solution.py:26
  12.3 25.2 %collective-permute-start.8 = (f32[2,336,256]{2,1,0:T(8,128)S(1)}, f32[2,336,256]{2,1,0:T(8,128)S(1)}, u32[]{:S(2)}, u32[]{:S(2)}) collective-permute-start(f32[2,336,256]{2,1,0:T(8,128)S(1)} %get-tuple-element.33), channel_id=1, source_target_pairs={{0,64},{16,80},{32,96},{48,112},{64,0},{80,16},{96,32},{112,48},{1... | collective-permute-start | bytes 2064392 | tf_op jit(solution)/shard_map/ppermute | solution.py:26
  22.8 35.6 %collective-permute-start = (f32[2,352,256]{2,1,0:T(8,128)S(1)}, f32[2,352,256]{2,1,0:T(8,128)S(1)}, u32[]{:S(2)}, u32[]{:S(2)}) collective-permute-start(f32[2,352,256]{2,1,0:T(8,128)S(1)} %get-tuple-element.27), channel_id=1, source_target_pairs={{0,16},{16,0},{32,48},{48,32},{64,80},{80,64},{96,112},{112,96},{1... | collective-permute-start | bytes 2162696 | tf_op jit(solution)/shard_map/ppermute | solution.py:26
  24.5 29.7 %collective-permute-start.10 = (f32[2,336,256]{2,1,0:T(8,128)S(1)}, f32[2,336,256]{2,1,0:T(8,128)S(1)}, u32[]{:S(2)}, u32[]{:S(2)}) collective-permute-start(f32[2,336,256]{2,1,0:T(8,128)S(1)} %slice_add_fusion.1), channel_id=1, source_target_pairs={{0,16},{16,0},{32,48},{48,32},{64,80},{80,64},{96,112},{112,96},{1... | collective-permute-start | bytes 2064392 | tf_op jit(solution)/shard_map/ppermute | solution.py:26
  27.0 28.9 %collective-permute-start.6 = (f32[2,336,256]{2,1,0:T(8,128)S(1)}, f32[2,336,256]{2,1,0:T(8,128)S(1)}, u32[]{:S(2)}, u32[]{:S(2)}) collective-permute-start(f32[2,336,256]{2,1,0:T(8,128)S(1)} %slice_add_fusion.2), channel_id=1, source_target_pairs={{0,64},{16,80},{32,96},{48,112},{64,0},{80,16},{96,32},{112,48},{1... | collective-permute-start | bytes 2064392 | tf_op jit(solution)/shard_map/ppermute | solution.py:26
  37.5 20.9 %collective-permute-start.2 = (f32[2,352,256]{2,1,0:T(8,128)S(1)}, f32[2,352,256]{2,1,0:T(8,128)S(1)}, u32[]{:S(2)}, u32[]{:S(2)}) collective-permute-start(f32[2,352,256]{2,1,0:T(8,128)S(1)} %slice_add_fusion), channel_id=1, source_target_pairs={{0,48},{16,32},{32,16},{48,0},{64,112},{80,96},{96,80},{112,64},{1... | collective-permute-start | bytes 2162696 | tf_op jit(solution)/shard_map/ppermute | solution.py:26
  54.3 8.3 %collective-permute-start.11 = (f32[336,256]{1,0:T(8,128)S(1)}, f32[336,256]{1,0:T(8,128)S(1)}, u32[]{:S(2)}, u32[]{:S(2)}) collective-permute-start(f32[336,256]{1,0:T(8,128)S(1)} %fusion.3), channel_id=1, source_target_pairs={{0,48},{16,32},{32,16},{48,0},{64,112},{80,96},{96,80},{112,64},{1... | collective-permute-start | bytes 1032200 | tf_op jit(solution)/shard_map/ppermute | solution.py:26
  56.0 8.7 %collective-permute-start.7 = (f32[336,256]{1,0:T(8,128)S(1)}, f32[336,256]{1,0:T(8,128)S(1)}, u32[]{:S(2)}, u32[]{:S(2)}) collective-permute-start(f32[336,256]{1,0:T(8,128)S(1)} %fusion.6), channel_id=1, source_target_pairs={{0,16},{16,0},{32,48},{48,32},{64,80},{80,64},{96,112},{112,96},{1... | collective-permute-start | bytes 1032200 | tf_op jit(solution)/shard_map/ppermute | solution.py:26
  58.5 9.8 %collective-permute-start.3 = (f32[352,256]{1,0:T(8,128)S(1)}, f32[352,256]{1,0:T(8,128)S(1)}, u32[]{:S(2)}, u32[]{:S(2)}) collective-permute-start(f32[352,256]{1,0:T(8,128)S(1)} %fusion), channel_id=1, source_target_pairs={{0,64},{16,80},{32,96},{48,112},{64,0},{80,16},{96,32},{112,48},{1... | collective-permute-start | bytes 1081352 | tf_op jit(solution)/shard_map/ppermute | solution.py:26
  62.6 14.6 %copy-start = (f32[2,512,256]{2,1,0:T(8,128)S(1)}, f32[2,512,256]{2,1,0:T(8,128)}, u32[]{:S(2)}) copy-start(f32[2,512,256]{2,1,0:T(8,128)} %param.5) | copy-start | bytes 3145732
  68.4 3.7 %collective-permute-start.12 = (f32[8,256]{1,0:T(8,128)S(1)}, f32[8,256]{1,0:T(8,128)S(1)}, u32[]{:S(2)}, u32[]{:S(2)}) collective-permute-start(f32[8,256]{1,0:T(8,128)S(1)} %broadcast_in_dim.3), channel_id=1, source_target_pairs={{0,8},{1,9},{2,10},{3,11},{4,12},{5,13},{6,14},{7,15},{8,0},{9,1},... | collective-permute-start | bytes 24584 | tf_op jit(solution)/shard_map/ppermute | solution.py:26
  72.1 5.2 %collective-permute-start.13 = (f32[8,256]{1,0:T(8,128)S(1)}, f32[8,256]{1,0:T(8,128)S(1)}, u32[]{:S(2)}, u32[]{:S(2)}) collective-permute-start(f32[8,256]{1,0:T(8,128)S(1)} %broadcast_add_fusion), channel_id=1, source_target_pairs={{0,64},{16,80},{32,96},{48,112},{64,0},{80,16},{96,32},{112,48},{1... | collective-permute-start | bytes 24584 | tf_op jit(solution)/shard_map/ppermute | solution.py:26
  77.3 25.1 %collective-permute-start.20 = (f32[1024,256]{1,0:T(8,128)S(1)}, f32[1024,256]{1,0:T(8,128)S(1)}, u32[]{:S(2)}, u32[]{:S(2)}) collective-permute-start(f32[1024,256]{1,0:T(8,128)S(1)} %bitcast.49), channel_id=1, source_target_pairs={{0,16},{16,32},{32,48},{48,64},{64,80},{80,96},{96,112},{112,0},{1... | collective-permute-start | bytes 3145736 | tf_op jit(solution)/shard_map/ppermute | solution.py:250
  77.7 3.7 %collective-permute-start.14 = (f32[8,256]{1,0:T(8,128)S(1)}, f32[8,256]{1,0:T(8,128)S(1)}, u32[]{:S(2)}, u32[]{:S(2)}) collective-permute-start(f32[8,256]{1,0:T(8,128)S(1)} %fusion.14), channel_id=1, source_target_pairs={{0,2},{1,3},{2,0},{3,1},{4,6},{5,7},{6,4},{7,5},{8,10},{9,11},{10,... | collective-permute-start | bytes 24584 | tf_op jit(solution)/shard_map/ppermute | solution.py:26
  81.3 5.7 %collective-permute-start.15 = (f32[8,256]{1,0:T(8,128)S(1)}, f32[8,256]{1,0:T(8,128)S(1)}, u32[]{:S(2)}, u32[]{:S(2)}) collective-permute-start(f32[8,256]{1,0:T(8,128)S(1)} %add.157), channel_id=1, source_target_pairs={{0,6},{1,7},{2,4},{3,5},{4,2},{5,3},{6,0},{7,1},{8,14},{9,15},{10,... | collective-permute-start | bytes 24584 | tf_op jit(solution)/shard_map/ppermute | solution.py:26
  87.0 1.2 collective-permute-start.16
  88.2 3.7 %collective-permute-start.17 = (f32[8,256]{1,0:T(8,128)S(1)}, f32[8,256]{1,0:T(8,128)S(1)}, u32[]{:S(2)}, u32[]{:S(2)}) collective-permute-start(f32[8,256]{1,0:T(8,128)S(1)} %add.159), channel_id=1, source_target_pairs={{0,48},{16,0},{32,16},{48,32},{64,112},{80,64},{96,80},{112,96},{1... | collective-permute-start | bytes 24584 | tf_op jit(solution)/shard_map/ppermute | solution.py:255
  91.8 4.4 %collective-permute-start.18 = (f32[8,256]{1,0:T(8,128)S(1)}, f32[8,256]{1,0:T(8,128)S(1)}, u32[]{:S(2)}, u32[]{:S(2)}) collective-permute-start(f32[8,256]{1,0:T(8,128)S(1)} %collective-permute-done.17), channel_id=1, source_target_pairs={{0,48},{16,0},{32,16},{48,32},{64,112},{80,64},{96,80},{112,96},{1... | collective-permute-start | bytes 24584 | tf_op jit(solution)/shard_map/ppermute | solution.py:255
  96.2 4.9 %collective-permute-start.19 = (f32[8,256]{1,0:T(8,128)S(1)}, f32[8,256]{1,0:T(8,128)S(1)}, u32[]{:S(2)}, u32[]{:S(2)}) collective-permute-start(f32[8,256]{1,0:T(8,128)S(1)} %collective-permute-done.18), channel_id=1, source_target_pairs={{0,48},{16,0},{32,16},{48,32},{64,112},{80,64},{96,80},{112,96},{1... | collective-permute-start | bytes 24584 | tf_op jit(solution)/shard_map/ppermute | solution.py:255
  102.6 8.5 %collective-permute-start.22 = (f32[336,256]{1,0:T(8,128)S(1)}, f32[336,256]{1,0:T(8,128)S(1)}, u32[]{:S(2)}, u32[]{:S(2)}) collective-permute-start(f32[336,256]{1,0:T(8,128)S(1)} %get-tuple-element.58.refs_2_), channel_id=1, source_target_pairs={{0,16},{16,0},{32,48},{48,32},{64,80},{80,64},{96,112},{112,96},{1... | collective-permute-start | bytes 1032200 | tf_op jit(solution)/shard_map/ppermute | solution.py:26
  106.0 12.8 %collective-permute-start.21 = (f32[352,256]{1,0:T(8,128)S(1)}, f32[352,256]{1,0:T(8,128)S(1)}, u32[]{:S(2)}, u32[]{:S(2)}) collective-permute-start(f32[352,256]{1,0:T(8,128)S(1)} %get-tuple-element.56.refs_1_), channel_id=1, source_target_pairs={{0,64},{16,80},{32,96},{48,112},{64,0},{80,16},{96,32},{112,48},{1... | collective-permute-start | bytes 1081352 | tf_op jit(solution)/shard_map/ppermute | solution.py:26
  107.8 11.1 %collective-permute-start.23 = (f32[336,256]{1,0:T(8,128)S(1)}, f32[336,256]{1,0:T(8,128)S(1)}, u32[]{:S(2)}, u32[]{:S(2)}) collective-permute-start(f32[336,256]{1,0:T(8,128)S(1)} %get-tuple-element.61.refs_3_), channel_id=1, source_target_pairs={{0,48},{16,32},{32,16},{48,0},{64,112},{80,96},{96,80},{112,64},{1... | collective-permute-start | bytes 1032200 | tf_op jit(solution)/shard_map/ppermute | solution.py:26
  111.2 18.6 %collective-permute-start.24 = (f32[2,336,256]{2,1,0:T(8,128)S(1)}, f32[2,336,256]{2,1,0:T(8,128)S(1)}, u32[]{:S(2)}, u32[]{:S(2)}) collective-permute-start(f32[2,336,256]{2,1,0:T(8,128)S(1)} %pad_maximum_fusion.2), channel_id=1, source_target_pairs={{0,64},{16,80},{32,96},{48,112},{64,0},{80,16},{96,32},{112,48},{1... | collective-permute-start | bytes 2064392 | tf_op jit(solution)/shard_map/ppermute | solution.py:26
  118.8 19.0 %collective-permute-start.25 = (f32[2,352,256]{2,1,0:T(8,128)S(1)}, f32[2,352,256]{2,1,0:T(8,128)S(1)}, u32[]{:S(2)}, u32[]{:S(2)}) collective-permute-start(f32[2,352,256]{2,1,0:T(8,128)S(1)} %pad_maximum_fusion.1), channel_id=1, source_target_pairs={{0,48},{16,32},{32,16},{48,0},{64,112},{80,96},{96,80},{112,64},{1... | collective-permute-start | bytes 2162696 | tf_op jit(solution)/shard_map/ppermute | solution.py:26
  119.0 20.7 %collective-permute-start.28 = (f32[2,336,256]{2,1,0:T(8,128)S(1)}, f32[2,336,256]{2,1,0:T(8,128)S(1)}, u32[]{:S(2)}, u32[]{:S(2)}) collective-permute-start(f32[2,336,256]{2,1,0:T(8,128)S(1)} %pad_maximum_fusion.3), channel_id=1, source_target_pairs={{0,16},{16,0},{32,48},{48,32},{64,80},{80,64},{96,112},{112,96},{1... | collective-permute-start | bytes 2064392 | tf_op jit(solution)/shard_map/ppermute | solution.py:26
  119.1 30.9 %collective-permute-start.30 = (f32[2,336,256]{2,1,0:T(8,128)S(1)}, f32[2,336,256]{2,1,0:T(8,128)S(1)}, u32[]{:S(2)}, u32[]{:S(2)}) collective-permute-start(f32[2,336,256]{2,1,0:T(8,128)S(1)} %pad_maximum_fusion.2), channel_id=1, source_target_pairs={{0,48},{16,32},{32,16},{48,0},{64,112},{80,96},{96,80},{112,64},{1... | collective-permute-start | bytes 2064392 | tf_op jit(solution)/shard_map/ppermute | solution.py:26
  121.1 29.9 %collective-permute-start.31 = (f32[2,352,256]{2,1,0:T(8,128)S(1)}, f32[2,352,256]{2,1,0:T(8,128)S(1)}, u32[]{:S(2)}, u32[]{:S(2)}) collective-permute-start(f32[2,352,256]{2,1,0:T(8,128)S(1)} %pad_maximum_fusion.1), channel_id=1, source_target_pairs={{0,16},{16,0},{32,48},{48,32},{64,80},{80,64},{96,112},{112,96},{1... | collective-permute-start | bytes 2162696 | tf_op jit(solution)/shard_map/ppermute | solution.py:26
  137.8 23.0 %collective-permute-start.26 = (f32[2,352,256]{2,1,0:T(8,128)S(1)}, f32[2,352,256]{2,1,0:T(8,128)S(1)}, u32[]{:S(2)}, u32[]{:S(2)}) collective-permute-start(f32[2,352,256]{2,1,0:T(8,128)S(1)} %collective-permute-done.25.refs_7_), channel_id=1, source_target_pairs={{0,16},{16,0},{32,48},{48,32},{64,80},{80,64},{96,112},{112,96},{1... | collective-permute-start | bytes 2162696 | tf_op jit(solution)/shard_map/ppermute | solution.py:26
  137.8 14.6 %collective-permute-start.32 = (f32[2,336,256]{2,1,0:T(8,128)S(1)}, f32[2,336,256]{2,1,0:T(8,128)S(1)}, u32[]{:S(2)}, u32[]{:S(2)}) collective-permute-start(f32[2,336,256]{2,1,0:T(8,128)S(1)} %pad_maximum_fusion.3), channel_id=1, source_target_pairs={{0,64},{16,80},{32,96},{48,112},{64,0},{80,16},{96,32},{112,48},{1... | collective-permute-start | bytes 2064392 | tf_op jit(solution)/shard_map/ppermute | solution.py:26
  139.7 20.1 %collective-permute-start.29 = (f32[2,336,256]{2,1,0:T(8,128)S(1)}, f32[2,336,256]{2,1,0:T(8,128)S(1)}, u32[]{:S(2)}, u32[]{:S(2)}) collective-permute-start(f32[2,336,256]{2,1,0:T(8,128)S(1)} %collective-permute-done.28.refs_9_), channel_id=1, source_target_pairs={{0,64},{16,80},{32,96},{48,112},{64,0},{80,16},{96,32},{112,48},{1... | collective-permute-start | bytes 2064392 | tf_op jit(solution)/shard_map/ppermute | solution.py:26
  149.9 10.9 %collective-permute-start.27 = (f32[2,336,256]{2,1,0:T(8,128)S(1)}, f32[2,336,256]{2,1,0:T(8,128)S(1)}, u32[]{:S(2)}, u32[]{:S(2)}) collective-permute-start(f32[2,336,256]{2,1,0:T(8,128)S(1)} %collective-permute-done.24.refs_8_), channel_id=1, source_target_pairs={{0,48},{16,32},{32,16},{48,0},{64,112},{80,96},{96,80},{112,64},{1... | collective-permute-start | bytes 2064392 | tf_op jit(solution)/shard_map/ppermute | solution.py:26

commit v3 on v2

--- a/solution.py
+++ b/solution.py
@@ -24,6 +24,11 @@
 
 def exchange(value, flip, axis, size):
     return lax.ppermute(value, axis, [(i, i ^ flip) for i in range(size)])
+
+
+def exchange_two(value, replica_flip, shard_flip):
+    pairs = [(r * 16 + s, (r ^ replica_flip) * 16 + (s ^ shard_flip)) for r in range(8) for s in range(16)]
+    return lax.ppermute(value, ("replica", "shard"), pairs)
 
 
 def tie(*values):
@@ -244,8 +249,8 @@
     grads = [(kept[k][0] + got2[k][0] + got3[k][0] + got4[k]) / replicas for k in parts]
 
     squares = jnp.broadcast_to(sum(jnp.sum(p * p, axis=0) for p in grads), (8, block_cols))
-    squares = squares + exchange(squares, 8, "shard", 16)
-    squares = squares + exchange(squares, 4, "replica", replicas)
+    over_y = [exchange_two(squares, a, b) for a, b in ((0, 8), (4, 0), (4, 8))]
+    squares = (squares + over_y[0]) + (over_y[1] + over_y[2])
     squares, m = tie(squares, m)
     prior_m = lax.ppermute(m, "replica", [(i, (i + 1) % replicas) for i in range(replicas)])
     for flip in (2, 6, 1):
@@ -282,11 +287,17 @@
     late_at = [((1, 1, 0), 0, 0), ((1, 1, 1), 0, 1)]
     early_items = [(k, flips(k, *bits), (at + k, j)) for bits, at, j in early_at for k in parts]
     late_items = [(k, flips(k, *bits), (at + k, j)) for bits, at, j in late_at for k in parts]
-    early_priors = [(k, [(f, w) for kk, f, w in early_items if kk == k and f in (1, 3, 7)]) for k in (0, 2)]
-    late_priors = [(1, [(f, w) for kk, f, w in late_items if kk == 1 and f in (1, 3, 7)])]
-    for i, (f, w) in enumerate([(f, w) for kk, f, w in early_items if kk == 1 and f in (1, 3, 7)]):
-        late_priors[0][1].append((f, (3 + i, w[1])))
-    extra = [early[w[0]] for kk, f, w in early_items if kk == 1 and f in (1, 3, 7)]
+    near = (1, 3, 7)
+    late_parts = sorted({k for k, f, _ in late_items if f in near})
+    early_priors = [(k, [(f, w) for kk, f, w in early_items if kk == k and f in near]) for k in parts if k not in late_parts]
+    extra, late_priors = [], []
+    for k in late_parts:
+        wheres = [(f, w) for kk, f, w in late_items if kk == k and f in near]
+        for kk, f, (at, j) in early_items:
+            if kk == k and f in near:
+                wheres.append((f, (3 + len(extra), j)))
+                extra.append(early[at])
+        late_priors.append((k, wheres))
     outs = apply(g, early, prior_m, spans, block_cols, early_items, early_priors)
     params, backup = apply(g, [*got_ab, *extra], prior_m, spans, block_cols, late_items, late_priors, outs)
     return (

time: 164 us -> 162 us (0.988)
  waiting for transfers between devices: 97.9 us -> 91.4 us
  starting transfers between devices: 44.4 us -> 48.5 us
    ppermute x29 -> x27, waiting for transfers between devices: 89.3 us -> 80.3 us  [exchange(): return lax.ppermute(value, axis, [(i, i ^ flip) for i in range(size)])]
    ppermute x0 -> x3, starting transfers between devices: none -> 3.57 us  [exchange_two(): return lax.ppermute(value, ('replica', 'shard'), pairs)]
    ppermute x0 -> x3, waiting for transfers between devices: none -> 3.51 us  [exchange_two(): return lax.ppermute(value, ('replica', 'shard'), pairs)]
    ppermute x29 -> x27, starting transfers between devices: 39.7 us -> 39.7 us  [exchange(): return lax.ppermute(value, axis, [(i, i ^ flip) for i in range(size)])]
  transfers between devices with their start and end apart: 33 -> 34, of which waited for: 24 -> 24; matrix products, arithmetic and copies ran while one was open for 2% -> 2% of each run, Pallas kernels for 7% -> 7%
where the time goes in v3:
time: 162 us; the launch traced here: 161 us
  waiting for transfers between devices  91.4 us (56%)
  starting transfers between devices  48.5 us (30%)
  Pallas kernels  17 us (10%)
  other arithmetic  2.85 us (2%)
  between operations  1.65 us (1%)
    ppermute x27, waiting for transfers between devices, exchange(): return lax.ppermute(value, axis, [(i, i ^ flip) for i in range(size)])  80.3 us
    ppermute x27, starting transfers between devices, exchange(): return lax.ppermute(value, axis, [(i, i ^ flip) for i in range(size)])  39.7 us
    pallas_call x2, Pallas kernels, apply(): pl.pallas_call(functools.partial(apply_kernel, spans, block_cols, items,...  9.23 us
    pallas_call x3, Pallas kernels, drift(): pl.pallas_call(functools.partial(drift_kernel, spans, block_cols, items,...  7.81 us
    ppermute x3, waiting for transfers between devices, per_device(): lax.ppermute(around[-1], 'replica', [(i, i // 4 * 4 + (i + 3) % 4) for i...  7.53 us
    ppermute x3, starting transfers between devices, per_device(): lax.ppermute(around[-1], 'replica', [(i, i // 4 * 4 + (i + 3) % 4) for i...  4.89 us
    ppermute x3, starting transfers between devices, exchange_two(): return lax.ppermute(value, ('replica', 'shard'), pairs)  3.57 us
    ppermute x3, waiting for transfers between devices, exchange_two(): return lax.ppermute(value, ('replica', 'shard'), pairs)  3.51 us
  transfers between devices with their start and end apart: 34, of which 24 were waited for; matrix products, arithmetic and copies ran while one was open for 2% of the time, Pallas kernels for 7%

profile of v3, /device:TPU:4, one launch (start us, length us, event | category | flops | bytes accessed | tf_op | source)
XLA Modules:
  0.0 161.5 jit_solution(2605348114644769804)
XLA Ops:
  0.6 2.2 %drift.5 = (f32[2,352,256]{2,1,0:T(8,128)S(1)}, f32[2,336,256]{2,1,0:T(8,128)S(1)}, f32[2,336,256]{2,1,0:T(8,128)S(1)}) custom-call(f32[1024,2048]{1,0:T(8,128)} %bitcast.39, bf16[1024,2048]{1,0:T(8,128)(2,1)} %bitcast.44), custom_call_target="tpu_custom_call" | custom-call | flops 540672 | bytes 5406720 | tf_op jit(solution)/shard_map/drift/pallas_call | solution.py:110
  2.9 3.3 %collective-permute-start.9 = (f32[2,336,256]{2,1,0:T(8,128)S(1)}, f32[2,336,256]{2,1,0:T(8,128)S(1)}, u32[]{:S(2)}, u32[]{:S(2)}) collective-permute-start(f32[2,336,256]{2,1,0:T(8,128)S(1)} %get-tuple-element.34), channel_id=1, source_target_pairs={{0,64},{16,80},{32,96},{48,112},{64,0},{80,16},{96,32},{112,48},{1... | collective-permute-start | bytes 2064392 | tf_op jit(solution)/shard_map/ppermute | solution.py:26
  6.1 0.5 collective-permute-start.5
  6.7 1.1 collective-permute-start.1
  7.8 2.2 %drift.4 = (f32[2,352,256]{2,1,0:T(8,128)S(1)}, f32[2,336,256]{2,1,0:T(8,128)S(1)}, f32[2,336,256]{2,1,0:T(8,128)S(1)}) custom-call(f32[1024,2048]{1,0:T(8,128)} %bitcast.40, bf16[1024,2048]{1,0:T(8,128)(2,1)} %bitcast.45), custom_call_target="tpu_custom_call" | custom-call | flops 540672 | bytes 5406720 | tf_op jit(solution)/shard_map/drift/pallas_call | solution.py:110
  10.0 2.2 %collective-permute-start.4 = (f32[2,336,256]{2,1,0:T(8,128)S(1)}, f32[2,336,256]{2,1,0:T(8,128)S(1)}, u32[]{:S(2)}, u32[]{:S(2)}) collective-permute-start(f32[2,336,256]{2,1,0:T(8,128)S(1)} %get-tuple-element.30), channel_id=1, source_target_pairs={{0,48},{16,32},{32,16},{48,0},{64,112},{80,96},{96,80},{112,64},{1... | collective-permute-start | bytes 2064392 | tf_op jit(solution)/shard_map/ppermute | solution.py:26
  12.3 0.3 collective-permute-start.8
  12.6 3.4 %drift.3 = (f32[4,352,256]{2,1,0:T(8,128)S(1)}, f32[4,336,256]{2,1,0:T(8,128)S(1)}, f32[4,336,256]{2,1,0:T(8,128)S(1)}) custom-call(f32[1024,2048]{1,0:T(8,128)} %bitcast.41, bf16[1024,2048]{1,0:T(8,128)(2,1)} %bitcast.46), custom_call_target="tpu_custom_call" | custom-call | flops 1081344 | bytes 10813440 | tf_op jit(solution)/shard_map/drift/pallas_call | solution.py:110
  16.0 6.8 %collective-permute-done.9 = f32[2,336,256]{2,1,0:T(8,128)S(1)} collective-permute-done((f32[2,336,256]{2,1,0:T(8,128)S(1)}, f32[2,336,256]{2,1,0:T(8,128)S(1)}, u32[]{:S(2)}, u32[]{:S(2)}) %collective-permute-start.9) | collective-permute-done | bytes 688160 | tf_op jit(solution)/shard_map/ppermute | solution.py:26
  22.8 1.2 collective-permute-start
  24.1 0.4 collective-permute-done.5
  24.5 2.4 %collective-permute-start.10 = (f32[2,336,256]{2,1,0:T(8,128)S(1)}, f32[2,336,256]{2,1,0:T(8,128)S(1)}, u32[]{:S(2)}, u32[]{:S(2)}) collective-permute-start(f32[2,336,256]{2,1,0:T(8,128)S(1)} %slice_add_fusion.1), channel_id=1, source_target_pairs={{0,16},{16,0},{32,48},{48,32},{64,80},{80,64},{96,112},{112,96},{1... | collective-permute-start | bytes 2064392 | tf_op jit(solution)/shard_map/ppermute | solution.py:26
  27.0 1.3 collective-permute-start.6
  28.4 0.1 slice_add_fusion
  28.4 9.1 %collective-permute-done.8 = f32[2,336,256]{2,1,0:T(8,128)S(1)} collective-permute-done((f32[2,336,256]{2,1,0:T(8,128)S(1)}, f32[2,336,256]{2,1,0:T(8,128)S(1)}, u32[]{:S(2)}, u32[]{:S(2)}) %collective-permute-start.8) | collective-permute-done | bytes 688160 | tf_op jit(solution)/shard_map/ppermute | solution.py:26
  37.5 0.5 collective-permute-start.2
  38.0 16.1 %collective-permute-done.10 = f32[2,336,256]{2,1,0:T(8,128)S(1)} collective-permute-done((f32[2,336,256]{2,1,0:T(8,128)S(1)}, f32[2,336,256]{2,1,0:T(8,128)S(1)}, u32[]{:S(2)}, u32[]{:S(2)}) %collective-permute-start.10) | collective-permute-done | bytes 688160 | tf_op jit(solution)/shard_map/ppermute | solution.py:26
  54.3 1.6 %collective-permute-start.11 = (f32[336,256]{1,0:T(8,128)S(1)}, f32[336,256]{1,0:T(8,128)S(1)}, u32[]{:S(2)}, u32[]{:S(2)}) collective-permute-start(f32[336,256]{1,0:T(8,128)S(1)} %fusion.3), channel_id=1, source_target_pairs={{0,48},{16,32},{32,16},{48,0},{64,112},{80,96},{96,80},{112,64},{1... | collective-permute-start | bytes 1032200 | tf_op jit(solution)/shard_map/ppermute | solution.py:26
  56.0 2.4 %collective-permute-start.7 = (f32[336,256]{1,0:T(8,128)S(1)}, f32[336,256]{1,0:T(8,128)S(1)}, u32[]{:S(2)}, u32[]{:S(2)}) collective-permute-start(f32[336,256]{1,0:T(8,128)S(1)} %fusion.6), channel_id=1, source_target_pairs={{0,16},{16,0},{32,48},{48,32},{64,80},{80,64},{96,112},{112,96},{1... | collective-permute-start | bytes 1032200 | tf_op jit(solution)/shard_map/ppermute | solution.py:26
  58.5 0.5 collective-permute-start.3
  58.9 3.6 %collective-permute-done.11 = f32[336,256]{1,0:T(8,128)S(1)} collective-permute-done((f32[336,256]{1,0:T(8,128)S(1)}, f32[336,256]{1,0:T(8,128)S(1)}, u32[]{:S(2)}, u32[]{:S(2)}) %collective-permute-start.11) | collective-permute-done | bytes 344096 | tf_op jit(solution)/shard_map/ppermute | solution.py:26
  62.5 0.1 multiply_reduce_fusion.1
  62.6 2.1 %collective-permute-done.7 = f32[336,256]{1,0:T(8,128)S(1)} collective-permute-done((f32[336,256]{1,0:T(8,128)S(1)}, f32[336,256]{1,0:T(8,128)S(1)}, u32[]{:S(2)}, u32[]{:S(2)}) %collective-permute-start.7) | collective-permute-done | bytes 344096 | tf_op jit(solution)/shard_map/ppermute | solution.py:26
  64.7 0.1 multiply_reduce_fusion.2
  64.8 3.4 %collective-permute-done.3 = f32[352,256]{1,0:T(8,128)S(1)} collective-permute-done((f32[352,256]{1,0:T(8,128)S(1)}, f32[352,256]{1,0:T(8,128)S(1)}, u32[]{:S(2)}, u32[]{:S(2)}) %collective-permute-start.3) | collective-permute-done | bytes 360480 | tf_op jit(solution)/shard_map/ppermute | solution.py:26
  68.2 0.1 multiply_reduce_fusion
  68.3 0.4 collective-permute-start.13
  68.7 3.1 %collective-permute-start.14 = (f32[8,256]{1,0:T(8,128)S(1)}, f32[8,256]{1,0:T(8,128)S(1)}, u32[]{:S(2)}, u32[]{:S(2)}) collective-permute-start(f32[8,256]{1,0:T(8,128)S(1)} %broadcast_in_dim.3), channel_id=1, source_target_pairs={{0,72},{1,73},{2,74},{3,75},{4,76},{5,77},{6,78},{7,79},{8,64},{9,... | collective-permute-start | bytes 24584 | tf_op jit(solution)/shard_map/ppermute | solution.py:31
  71.7 0.1 collective-permute-start.12
  71.9 1.7 %collective-permute-done.13 = f32[8,256]{1,0:T(8,128)S(1)} collective-permute-done((f32[8,256]{1,0:T(8,128)S(1)}, f32[8,256]{1,0:T(8,128)S(1)}, u32[]{:S(2)}, u32[]{:S(2)}) %collective-permute-start.13) | collective-permute-done | bytes 8224 | tf_op jit(solution)/shard_map/ppermute | solution.py:31
  73.6 1.8 %collective-permute-done.12 = f32[8,256]{1,0:T(8,128)S(1)} collective-permute-done((f32[8,256]{1,0:T(8,128)S(1)}, f32[8,256]{1,0:T(8,128)S(1)}, u32[]{:S(2)}, u32[]{:S(2)}) %collective-permute-start.12) | collective-permute-done | bytes 8224 | tf_op jit(solution)/shard_map/ppermute | solution.py:31
  75.4 0.4 collective-permute-start.21
  75.8 1.9 %collective-permute-start.15 = (f32[8,256]{1,0:T(8,128)S(1)}, f32[8,256]{1,0:T(8,128)S(1)}, u32[]{:S(2)}, u32[]{:S(2)}) collective-permute-start(f32[8,256]{1,0:T(8,128)S(1)} %add_add_fusion), channel_id=1, source_target_pairs={{0,2},{1,3},{2,0},{3,1},{4,6},{5,7},{6,4},{7,5},{8,10},{9,11},{10,... | collective-permute-start | bytes 24584 | tf_op jit(solution)/shard_map/ppermute | solution.py:26
  77.7 1.7 %collective-permute-done.15 = f32[8,256]{1,0:T(8,128)S(1)} collective-permute-done((f32[8,256]{1,0:T(8,128)S(1)}, f32[8,256]{1,0:T(8,128)S(1)}, u32[]{:S(2)}, u32[]{:S(2)}) %collective-permute-start.15) | collective-permute-done | bytes 8224 | tf_op jit(solution)/shard_map/ppermute | solution.py:26
  79.4 4.0 %collective-permute-start.16 = (f32[8,256]{1,0:T(8,128)S(1)}, f32[8,256]{1,0:T(8,128)S(1)}, u32[]{:S(2)}, u32[]{:S(2)}) collective-permute-start(f32[8,256]{1,0:T(8,128)S(1)} %add.161), channel_id=1, source_target_pairs={{0,6},{1,7},{2,4},{3,5},{4,2},{5,3},{6,0},{7,1},{8,14},{9,15},{10,... | collective-permute-start | bytes 24584 | tf_op jit(solution)/shard_map/ppermute | solution.py:26
  83.5 1.6 %collective-permute-done.16 = f32[8,256]{1,0:T(8,128)S(1)} collective-permute-done((f32[8,256]{1,0:T(8,128)S(1)}, f32[8,256]{1,0:T(8,128)S(1)}, u32[]{:S(2)}, u32[]{:S(2)}) %collective-permute-start.16) | collective-permute-done | bytes 8224 | tf_op jit(solution)/shard_map/ppermute | solution.py:26
  85.1 1.2 collective-permute-done.17
  86.3 1.7 %collective-permute-start.18 = (f32[8,256]{1,0:T(8,128)S(1)}, f32[8,256]{1,0:T(8,128)S(1)}, u32[]{:S(2)}, u32[]{:S(2)}) collective-permute-start(f32[8,256]{1,0:T(8,128)S(1)} %add.163), channel_id=1, source_target_pairs={{0,48},{16,0},{32,16},{48,32},{64,112},{80,64},{96,80},{112,96},{1... | collective-permute-start | bytes 24584 | tf_op jit(solution)/shard_map/ppermute | solution.py:260
  88.0 1.9 %collective-permute-done.18 = f32[8,256]{1,0:T(8,128)S(1)} collective-permute-done((f32[8,256]{1,0:T(8,128)S(1)}, f32[8,256]{1,0:T(8,128)S(1)}, u32[]{:S(2)}, u32[]{:S(2)}) %collective-permute-start.18) | collective-permute-done | bytes 8224 | tf_op jit(solution)/shard_map/ppermute | solution.py:260
  89.9 1.7 %collective-permute-start.19 = (f32[8,256]{1,0:T(8,128)S(1)}, f32[8,256]{1,0:T(8,128)S(1)}, u32[]{:S(2)}, u32[]{:S(2)}) collective-permute-start(f32[8,256]{1,0:T(8,128)S(1)} %collective-permute-done.18), channel_id=1, source_target_pairs={{0,48},{16,0},{32,16},{48,32},{64,112},{80,64},{96,80},{112,96},{1... | collective-permute-start | bytes 24584 | tf_op jit(solution)/shard_map/ppermute | solution.py:260
  91.6 2.2 %collective-permute-done.19 = f32[8,256]{1,0:T(8,128)S(1)} collective-permute-done((f32[8,256]{1,0:T(8,128)S(1)}, f32[8,256]{1,0:T(8,128)S(1)}, u32[]{:S(2)}, u32[]{:S(2)}) %collective-permute-start.19) | collective-permute-done | bytes 8224 | tf_op jit(solution)/shard_map/ppermute | solution.py:260
  93.8 1.5 collective-permute-start.20
  95.3 3.4 %collective-permute-done.20 = f32[8,256]{1,0:T(8,128)S(1)} collective-permute-done((f32[8,256]{1,0:T(8,128)S(1)}, f32[8,256]{1,0:T(8,128)S(1)}, u32[]{:S(2)}, u32[]{:S(2)}) %collective-permute-start.20) | collective-permute-done | bytes 8224 | tf_op jit(solution)/shard_map/ppermute | solution.py:260
  98.7 0.6 fusion.10
  100.0 0.2 multiply_add_fusion.3
  100.2 3.3 %collective-permute-start.23 = (f32[336,256]{1,0:T(8,128)S(1)}, f32[336,256]{1,0:T(8,128)S(1)}, u32[]{:S(2)}, u32[]{:S(2)}) collective-permute-start(f32[336,256]{1,0:T(8,128)S(1)} %get-tuple-element.58.refs_2_), channel_id=1, source_target_pairs={{0,16},{16,0},{32,48},{48,32},{64,80},{80,64},{96,112},{112,96},{1... | collective-permute-start | bytes 1032200 | tf_op jit(solution)/shard_map/ppermute | solution.py:26
  103.6 2.3 %collective-permute-start.22 = (f32[352,256]{1,0:T(8,128)S(1)}, f32[352,256]{1,0:T(8,128)S(1)}, u32[]{:S(2)}, u32[]{:S(2)}) collective-permute-start(f32[352,256]{1,0:T(8,128)S(1)} %get-tuple-element.56.refs_1_), channel_id=1, source_target_pairs={{0,64},{16,80},{32,96},{48,112},{64,0},{80,16},{96,32},{112,48},{1... | collective-permute-start | bytes 1081352 | tf_op jit(solution)/shard_map/ppermute | solution.py:26
  105.9 2.9 %collective-permute-done.23.refs_5_.refs_4_ = f32[336,256]{1,0:T(8,128)S(1)} collective-permute-done((f32[336,256]{1,0:T(8,128)S(1)}, f32[336,256]{1,0:T(8,128)S(1)}, u32[]{:S(2)}, u32[]{:S(2)}) %collective-permute-start.23) | collective-permute-done | bytes 344096 | tf_op jit(solution)/shard_map/ppermute | solution.py:26
  108.8 2.3 %collective-permute-start.25 = (f32[2,336,256]{2,1,0:T(8,128)S(1)}, f32[2,336,256]{2,1,0:T(8,128)S(1)}, u32[]{:S(2)}, u32[]{:S(2)}) collective-permute-start(f32[2,336,256]{2,1,0:T(8,128)S(1)} %pad_maximum_fusion.2), channel_id=1, source_target_pairs={{0,64},{16,80},{32,96},{48,112},{64,0},{80,16},{96,32},{112,48},{1... | collective-permute-start | bytes 2064392 | tf_op jit(solution)/shard_map/ppermute | solution.py:26
  111.0 5.3 %collective-permute-done.22.refs_4_ = f32[352,256]{1,0:T(8,128)S(1)} collective-permute-done((f32[352,256]{1,0:T(8,128)S(1)}, f32[352,256]{1,0:T(8,128)S(1)}, u32[]{:S(2)}, u32[]{:S(2)}) %collective-permute-start.22) | collective-permute-done | bytes 360480 | tf_op jit(solution)/shard_map/ppermute | solution.py:26
  116.7 2.1 %collective-permute-start.31 = (f32[2,336,256]{2,1,0:T(8,128)S(1)}, f32[2,336,256]{2,1,0:T(8,128)S(1)}, u32[]{:S(2)}, u32[]{:S(2)}) collective-permute-start(f32[2,336,256]{2,1,0:T(8,128)S(1)} %pad_maximum_fusion.2), channel_id=1, source_target_pairs={{0,48},{16,32},{32,16},{48,0},{64,112},{80,96},{96,80},{112,64},{1... | collective-permute-start | bytes 2064392 | tf_op jit(solution)/shard_map/ppermute | solution.py:26
  118.7 2.5 %collective-permute-start.32 = (f32[2,352,256]{2,1,0:T(8,128)S(1)}, f32[2,352,256]{2,1,0:T(8,128)S(1)}, u32[]{:S(2)}, u32[]{:S(2)}) collective-permute-start(f32[2,352,256]{2,1,0:T(8,128)S(1)} %pad_maximum_fusion.1), channel_id=1, source_target_pairs={{0,16},{16,0},{32,48},{48,32},{64,80},{80,64},{96,112},{112,96},{1... | collective-permute-start | bytes 2162696 | tf_op jit(solution)/shard_map/ppermute | solution.py:26
  121.3 6.0 %collective-permute-done.25.refs_8_ = f32[2,336,256]{2,1,0:T(8,128)S(1)} collective-permute-done((f32[2,336,256]{2,1,0:T(8,128)S(1)}, f32[2,336,256]{2,1,0:T(8,128)S(1)}, u32[]{:S(2)}, u32[]{:S(2)}) %collective-permute-start.25) | collective-permute-done | bytes 688160 | tf_op jit(solution)/shard_map/ppermute | solution.py:26
  127.3 8.2 %collective-permute-done.26.refs_7_ = f32[2,352,256]{2,1,0:T(8,128)S(1)} collective-permute-done((f32[2,352,256]{2,1,0:T(8,128)S(1)}, f32[2,352,256]{2,1,0:T(8,128)S(1)}, u32[]{:S(2)}, u32[]{:S(2)}) %collective-permute-start.26) | collective-permute-done | bytes 720928 | tf_op jit(solution)/shard_map/ppermute | solution.py:26
  135.6 1.7 %collective-permute-start.33 = (f32[2,336,256]{2,1,0:T(8,128)S(1)}, f32[2,336,256]{2,1,0:T(8,128)S(1)}, u32[]{:S(2)}, u32[]{:S(2)}) collective-permute-start(f32[2,336,256]{2,1,0:T(8,128)S(1)} %pad_maximum_fusion.3), channel_id=1, source_target_pairs={{0,64},{16,80},{32,96},{48,112},{64,0},{80,16},{96,32},{112,48},{1... | collective-permute-start | bytes 2064392 | tf_op jit(solution)/shard_map/ppermute | solution.py:26
  137.3 1.9 %collective-permute-start.30 = (f32[2,336,256]{2,1,0:T(8,128)S(1)}, f32[2,336,256]{2,1,0:T(8,128)S(1)}, u32[]{:S(2)}, u32[]{:S(2)}) collective-permute-start(f32[2,336,256]{2,1,0:T(8,128)S(1)} %collective-permute-done.29.refs_9_), channel_id=1, source_target_pairs={{0,64},{16,80},{32,96},{48,112},{64,0},{80,16},{96,32},{112,48},{1... | collective-permute-start | bytes 2064392 | tf_op jit(solution)/shard_map/ppermute | solution.py:26
  139.1 8.4 %collective-permute-done.31.refs_11_.refs_5_ = f32[2,336,256]{2,1,0:T(8,128)S(1)} collective-permute-done((f32[2,336,256]{2,1,0:T(8,128)S(1)}, f32[2,336,256]{2,1,0:T(8,128)S(1)}, u32[]{:S(2)}, u32[]{:S(2)}) %collective-permute-start.31) | collective-permute-done | bytes 688160 | tf_op jit(solution)/shard_map/ppermute | solution.py:26
  147.5 1.0 pad_maximum_fusion
  148.6 0.5 collective-permute-done.32.refs_10_
  149.0 1.6 collective-permute-done.33.refs_12_
  150.6 6.4 %apply.2 = (f32[1024,2048]{1,0:T(8,128)}, f32[1024,256]{1,0:T(8,128)}) custom-call(f32[1024,2048]{1,0:T(8,128)} %bitcast.42, f32[352,256]{1,0:T(8,128)S(1)} %get-tuple-element.56.refs_1_, f32[336,256]{1,0:T(8,128)S(1)} %get-tuple-element.58.refs_2_, f32[336,256]{1,0:T(8,128)S(1)} %get-tuple-element.61.refs_3_, ...), custom_call_target="tpu_custom_call" | custom-call | flops 1622016 | bytes 19464192 | tf_op jit(solution)/shard_map/apply/pallas_call | solution.py:202
  157.0 1.0 collective-permute-done.30.refs_3_
  158.0 0.5 collective-permute-done.28.refs_2_
  158.5 2.8 %apply.3 = (f32[1024,2048]{1,0:T(8,128)}, f32[1024,256]{1,0:T(8,128)}) custom-call(f32[1024,2048]{1,0:T(8,128)} %bitcast.43, f32[2,352,256]{2,1,0:T(8,128)S(1)} %collective-permute-done.27.refs_1_, f32[2,336,256]{2,1,0:T(8,128)S(1)} %collective-permute-done.28.refs_2_, ...), custom_call_target="tpu_custom_call", output_to_operand_aliasing={{0}: (7, {}), {1}: (8, {})} | custom-call | flops 540672 | bytes 6488064 | tf_op jit(solution)/shard_map/apply/pallas_call | solution.py:202
  (33 shorter events, 0.8 us)
Async XLA Ops:
  2.9 19.9 %collective-permute-start.9 = (f32[2,336,256]{2,1,0:T(8,128)S(1)}, f32[2,336,256]{2,1,0:T(8,128)S(1)}, u32[]{:S(2)}, u32[]{:S(2)}) collective-permute-start(f32[2,336,256]{2,1,0:T(8,128)S(1)} %get-tuple-element.34), channel_id=1, source_target_pairs={{0,64},{16,80},{32,96},{48,112},{64,0},{80,16},{96,32},{112,48},{1... | collective-permute-start | bytes 2064392 | tf_op jit(solution)/shard_map/ppermute | solution.py:26
  6.1 18.4 %collective-permute-start.5 = (f32[2,336,256]{2,1,0:T(8,128)S(1)}, f32[2,336,256]{2,1,0:T(8,128)S(1)}, u32[]{:S(2)}, u32[]{:S(2)}) collective-permute-start(f32[2,336,256]{2,1,0:T(8,128)S(1)} %get-tuple-element.31), channel_id=1, source_target_pairs={{0,48},{16,32},{32,16},{48,0},{64,112},{80,96},{96,80},{112,64},{1... | collective-permute-start | bytes 2064392 | tf_op jit(solution)/shard_map/ppermute | solution.py:26
  6.7 20.3 %collective-permute-start.1 = (f32[2,352,256]{2,1,0:T(8,128)S(1)}, f32[2,352,256]{2,1,0:T(8,128)S(1)}, u32[]{:S(2)}, u32[]{:S(2)}) collective-permute-start(f32[2,352,256]{2,1,0:T(8,128)S(1)} %get-tuple-element.28), channel_id=1, source_target_pairs={{0,16},{16,0},{32,48},{48,32},{64,80},{80,64},{96,112},{112,96},{1... | collective-permute-start | bytes 2162696 | tf_op jit(solution)/shard_map/ppermute | solution.py:26
  10.0 45.9 %collective-permute-start.4 = (f32[2,336,256]{2,1,0:T(8,128)S(1)}, f32[2,336,256]{2,1,0:T(8,128)S(1)}, u32[]{:S(2)}, u32[]{:S(2)}) collective-permute-start(f32[2,336,256]{2,1,0:T(8,128)S(1)} %get-tuple-element.30), channel_id=1, source_target_pairs={{0,48},{16,32},{32,16},{48,0},{64,112},{80,96},{96,80},{112,64},{1... | collective-permute-start | bytes 2064392 | tf_op jit(solution)/shard_map/ppermute | solution.py:26
  12.3 25.2 %collective-permute-start.8 = (f32[2,336,256]{2,1,0:T(8,128)S(1)}, f32[2,336,256]{2,1,0:T(8,128)S(1)}, u32[]{:S(2)}, u32[]{:S(2)}) collective-permute-start(f32[2,336,256]{2,1,0:T(8,128)S(1)} %get-tuple-element.33), channel_id=1, source_target_pairs={{0,64},{16,80},{32,96},{48,112},{64,0},{80,16},{96,32},{112,48},{1... | collective-permute-start | bytes 2064392 | tf_op jit(solution)/shard_map/ppermute | solution.py:26
  22.8 35.6 %collective-permute-start = (f32[2,352,256]{2,1,0:T(8,128)S(1)}, f32[2,352,256]{2,1,0:T(8,128)S(1)}, u32[]{:S(2)}, u32[]{:S(2)}) collective-permute-start(f32[2,352,256]{2,1,0:T(8,128)S(1)} %get-tuple-element.27), channel_id=1, source_target_pairs={{0,16},{16,0},{32,48},{48,32},{64,80},{80,64},{96,112},{112,96},{1... | collective-permute-start | bytes 2162696 | tf_op jit(solution)/shard_map/ppermute | solution.py:26
  24.5 29.7 %collective-permute-start.10 = (f32[2,336,256]{2,1,0:T(8,128)S(1)}, f32[2,336,256]{2,1,0:T(8,128)S(1)}, u32[]{:S(2)}, u32[]{:S(2)}) collective-permute-start(f32[2,336,256]{2,1,0:T(8,128)S(1)} %slice_add_fusion.1), channel_id=1, source_target_pairs={{0,16},{16,0},{32,48},{48,32},{64,80},{80,64},{96,112},{112,96},{1... | collective-permute-start | bytes 2064392 | tf_op jit(solution)/shard_map/ppermute | solution.py:26
  27.0 28.9 %collective-permute-start.6 = (f32[2,336,256]{2,1,0:T(8,128)S(1)}, f32[2,336,256]{2,1,0:T(8,128)S(1)}, u32[]{:S(2)}, u32[]{:S(2)}) collective-permute-start(f32[2,336,256]{2,1,0:T(8,128)S(1)} %slice_add_fusion.2), channel_id=1, source_target_pairs={{0,64},{16,80},{32,96},{48,112},{64,0},{80,16},{96,32},{112,48},{1... | collective-permute-start | bytes 2064392 | tf_op jit(solution)/shard_map/ppermute | solution.py:26
  37.5 20.9 %collective-permute-start.2 = (f32[2,352,256]{2,1,0:T(8,128)S(1)}, f32[2,352,256]{2,1,0:T(8,128)S(1)}, u32[]{:S(2)}, u32[]{:S(2)}) collective-permute-start(f32[2,352,256]{2,1,0:T(8,128)S(1)} %slice_add_fusion), channel_id=1, source_target_pairs={{0,48},{16,32},{32,16},{48,0},{64,112},{80,96},{96,80},{112,64},{1... | collective-permute-start | bytes 2162696 | tf_op jit(solution)/shard_map/ppermute | solution.py:26
  54.3 8.3 %collective-permute-start.11 = (f32[336,256]{1,0:T(8,128)S(1)}, f32[336,256]{1,0:T(8,128)S(1)}, u32[]{:S(2)}, u32[]{:S(2)}) collective-permute-start(f32[336,256]{1,0:T(8,128)S(1)} %fusion.3), channel_id=1, source_target_pairs={{0,48},{16,32},{32,16},{48,0},{64,112},{80,96},{96,80},{112,64},{1... | collective-permute-start | bytes 1032200 | tf_op jit(solution)/shard_map/ppermute | solution.py:26
  56.0 8.7 %collective-permute-start.7 = (f32[336,256]{1,0:T(8,128)S(1)}, f32[336,256]{1,0:T(8,128)S(1)}, u32[]{:S(2)}, u32[]{:S(2)}) collective-permute-start(f32[336,256]{1,0:T(8,128)S(1)} %fusion.6), channel_id=1, source_target_pairs={{0,16},{16,0},{32,48},{48,32},{64,80},{80,64},{96,112},{112,96},{1... | collective-permute-start | bytes 1032200 | tf_op jit(solution)/shard_map/ppermute | solution.py:26
  58.5 9.7 %collective-permute-start.3 = (f32[352,256]{1,0:T(8,128)S(1)}, f32[352,256]{1,0:T(8,128)S(1)}, u32[]{:S(2)}, u32[]{:S(2)}) collective-permute-start(f32[352,256]{1,0:T(8,128)S(1)} %fusion), channel_id=1, source_target_pairs={{0,64},{16,80},{32,96},{48,112},{64,0},{80,16},{96,32},{112,48},{1... | collective-permute-start | bytes 1081352 | tf_op jit(solution)/shard_map/ppermute | solution.py:26
  62.6 12.8 %copy-start = (f32[2,512,256]{2,1,0:T(8,128)S(1)}, f32[2,512,256]{2,1,0:T(8,128)}, u32[]{:S(2)}) copy-start(f32[2,512,256]{2,1,0:T(8,128)} %param.5) | copy-start | bytes 3145732
  68.3 5.3 %collective-permute-start.13 = (f32[8,256]{1,0:T(8,128)S(1)}, f32[8,256]{1,0:T(8,128)S(1)}, u32[]{:S(2)}, u32[]{:S(2)}) collective-permute-start(f32[8,256]{1,0:T(8,128)S(1)} %broadcast_in_dim.3), channel_id=1, source_target_pairs={{0,64},{1,65},{2,66},{3,67},{4,68},{5,69},{6,70},{7,71},{8,72},{9,... | collective-permute-start | bytes 24584 | tf_op jit(solution)/shard_map/ppermute | solution.py:31
  68.7 5.0 %collective-permute-start.14 = (f32[8,256]{1,0:T(8,128)S(1)}, f32[8,256]{1,0:T(8,128)S(1)}, u32[]{:S(2)}, u32[]{:S(2)}) collective-permute-start(f32[8,256]{1,0:T(8,128)S(1)} %broadcast_in_dim.3), channel_id=1, source_target_pairs={{0,72},{1,73},{2,74},{3,75},{4,76},{5,77},{6,78},{7,79},{8,64},{9,... | collective-permute-start | bytes 24584 | tf_op jit(solution)/shard_map/ppermute | solution.py:31
  71.7 3.7 %collective-permute-start.12 = (f32[8,256]{1,0:T(8,128)S(1)}, f32[8,256]{1,0:T(8,128)S(1)}, u32[]{:S(2)}, u32[]{:S(2)}) collective-permute-start(f32[8,256]{1,0:T(8,128)S(1)} %broadcast_in_dim.3), channel_id=1, source_target_pairs={{0,8},{1,9},{2,10},{3,11},{4,12},{5,13},{6,14},{7,15},{8,0},{9,1},... | collective-permute-start | bytes 24584 | tf_op jit(solution)/shard_map/ppermute | solution.py:31
  75.4 24.6 %collective-permute-start.21 = (f32[1024,256]{1,0:T(8,128)S(1)}, f32[1024,256]{1,0:T(8,128)S(1)}, u32[]{:S(2)}, u32[]{:S(2)}) collective-permute-start(f32[1024,256]{1,0:T(8,128)S(1)} %bitcast.49), channel_id=1, source_target_pairs={{0,16},{16,32},{32,48},{48,64},{64,80},{80,96},{96,112},{112,0},{1... | collective-permute-start | bytes 3145736 | tf_op jit(solution)/shard_map/ppermute | solution.py:255
  75.8 3.7 %collective-permute-start.15 = (f32[8,256]{1,0:T(8,128)S(1)}, f32[8,256]{1,0:T(8,128)S(1)}, u32[]{:S(2)}, u32[]{:S(2)}) collective-permute-start(f32[8,256]{1,0:T(8,128)S(1)} %add_add_fusion), channel_id=1, source_target_pairs={{0,2},{1,3},{2,0},{3,1},{4,6},{5,7},{6,4},{7,5},{8,10},{9,11},{10,... | collective-permute-start | bytes 24584 | tf_op jit(solution)/shard_map/ppermute | solution.py:26
  79.4 5.7 %collective-permute-start.16 = (f32[8,256]{1,0:T(8,128)S(1)}, f32[8,256]{1,0:T(8,128)S(1)}, u32[]{:S(2)}, u32[]{:S(2)}) collective-permute-start(f32[8,256]{1,0:T(8,128)S(1)} %add.161), channel_id=1, source_target_pairs={{0,6},{1,7},{2,4},{3,5},{4,2},{5,3},{6,0},{7,1},{8,14},{9,15},{10,... | collective-permute-start | bytes 24584 | tf_op jit(solution)/shard_map/ppermute | solution.py:26
  85.1 1.2 collective-permute-start.17
  86.3 3.7 %collective-permute-start.18 = (f32[8,256]{1,0:T(8,128)S(1)}, f32[8,256]{1,0:T(8,128)S(1)}, u32[]{:S(2)}, u32[]{:S(2)}) collective-permute-start(f32[8,256]{1,0:T(8,128)S(1)} %add.163), channel_id=1, source_target_pairs={{0,48},{16,0},{32,16},{48,32},{64,112},{80,64},{96,80},{112,96},{1... | collective-permute-start | bytes 24584 | tf_op jit(solution)/shard_map/ppermute | solution.py:260
  89.9 3.9 %collective-permute-start.19 = (f32[8,256]{1,0:T(8,128)S(1)}, f32[8,256]{1,0:T(8,128)S(1)}, u32[]{:S(2)}, u32[]{:S(2)}) collective-permute-start(f32[8,256]{1,0:T(8,128)S(1)} %collective-permute-done.18), channel_id=1, source_target_pairs={{0,48},{16,0},{32,16},{48,32},{64,112},{80,64},{96,80},{112,96},{1... | collective-permute-start | bytes 24584 | tf_op jit(solution)/shard_map/ppermute | solution.py:260
  93.8 4.9 %collective-permute-start.20 = (f32[8,256]{1,0:T(8,128)S(1)}, f32[8,256]{1,0:T(8,128)S(1)}, u32[]{:S(2)}, u32[]{:S(2)}) collective-permute-start(f32[8,256]{1,0:T(8,128)S(1)} %collective-permute-done.19), channel_id=1, source_target_pairs={{0,48},{16,0},{32,16},{48,32},{64,112},{80,64},{96,80},{112,96},{1... | collective-permute-start | bytes 24584 | tf_op jit(solution)/shard_map/ppermute | solution.py:260
  100.2 8.5 %collective-permute-start.23 = (f32[336,256]{1,0:T(8,128)S(1)}, f32[336,256]{1,0:T(8,128)S(1)}, u32[]{:S(2)}, u32[]{:S(2)}) collective-permute-start(f32[336,256]{1,0:T(8,128)S(1)} %get-tuple-element.58.refs_2_), channel_id=1, source_target_pairs={{0,16},{16,0},{32,48},{48,32},{64,80},{80,64},{96,112},{112,96},{1... | collective-permute-start | bytes 1032200 | tf_op jit(solution)/shard_map/ppermute | solution.py:26
  103.6 12.8 %collective-permute-start.22 = (f32[352,256]{1,0:T(8,128)S(1)}, f32[352,256]{1,0:T(8,128)S(1)}, u32[]{:S(2)}, u32[]{:S(2)}) collective-permute-start(f32[352,256]{1,0:T(8,128)S(1)} %get-tuple-element.56.refs_1_), channel_id=1, source_target_pairs={{0,64},{16,80},{32,96},{48,112},{64,0},{80,16},{96,32},{112,48},{1... | collective-permute-start | bytes 1081352 | tf_op jit(solution)/shard_map/ppermute | solution.py:26
  105.9 10.7 %collective-permute-start.24 = (f32[336,256]{1,0:T(8,128)S(1)}, f32[336,256]{1,0:T(8,128)S(1)}, u32[]{:S(2)}, u32[]{:S(2)}) collective-permute-start(f32[336,256]{1,0:T(8,128)S(1)} %get-tuple-element.61.refs_3_), channel_id=1, source_target_pairs={{0,48},{16,32},{32,16},{48,0},{64,112},{80,96},{96,80},{112,64},{1... | collective-permute-start | bytes 1032200 | tf_op jit(solution)/shard_map/ppermute | solution.py:26
  108.8 18.6 %collective-permute-start.25 = (f32[2,336,256]{2,1,0:T(8,128)S(1)}, f32[2,336,256]{2,1,0:T(8,128)S(1)}, u32[]{:S(2)}, u32[]{:S(2)}) collective-permute-start(f32[2,336,256]{2,1,0:T(8,128)S(1)} %pad_maximum_fusion.2), channel_id=1, source_target_pairs={{0,64},{16,80},{32,96},{48,112},{64,0},{80,16},{96,32},{112,48},{1... | collective-permute-start | bytes 2064392 | tf_op jit(solution)/shard_map/ppermute | solution.py:26
  116.4 19.2 %collective-permute-start.26 = (f32[2,352,256]{2,1,0:T(8,128)S(1)}, f32[2,352,256]{2,1,0:T(8,128)S(1)}, u32[]{:S(2)}, u32[]{:S(2)}) collective-permute-start(f32[2,352,256]{2,1,0:T(8,128)S(1)} %pad_maximum_fusion.1), channel_id=1, source_target_pairs={{0,48},{16,32},{32,16},{48,0},{64,112},{80,96},{96,80},{112,64},{1... | collective-permute-start | bytes 2162696 | tf_op jit(solution)/shard_map/ppermute | solution.py:26
  116.6 20.7 %collective-permute-start.29 = (f32[2,336,256]{2,1,0:T(8,128)S(1)}, f32[2,336,256]{2,1,0:T(8,128)S(1)}, u32[]{:S(2)}, u32[]{:S(2)}) collective-permute-start(f32[2,336,256]{2,1,0:T(8,128)S(1)} %pad_maximum_fusion.3), channel_id=1, source_target_pairs={{0,16},{16,0},{32,48},{48,32},{64,80},{80,64},{96,112},{112,96},{1... | collective-permute-start | bytes 2064392 | tf_op jit(solution)/shard_map/ppermute | solution.py:26
  116.7 30.9 %collective-permute-start.31 = (f32[2,336,256]{2,1,0:T(8,128)S(1)}, f32[2,336,256]{2,1,0:T(8,128)S(1)}, u32[]{:S(2)}, u32[]{:S(2)}) collective-permute-start(f32[2,336,256]{2,1,0:T(8,128)S(1)} %pad_maximum_fusion.2), channel_id=1, source_target_pairs={{0,48},{16,32},{32,16},{48,0},{64,112},{80,96},{96,80},{112,64},{1... | collective-permute-start | bytes 2064392 | tf_op jit(solution)/shard_map/ppermute | solution.py:26
  118.7 30.3 %collective-permute-start.32 = (f32[2,352,256]{2,1,0:T(8,128)S(1)}, f32[2,352,256]{2,1,0:T(8,128)S(1)}, u32[]{:S(2)}, u32[]{:S(2)}) collective-permute-start(f32[2,352,256]{2,1,0:T(8,128)S(1)} %pad_maximum_fusion.1), channel_id=1, source_target_pairs={{0,16},{16,0},{32,48},{48,32},{64,80},{80,64},{96,112},{112,96},{1... | collective-permute-start | bytes 2162696 | tf_op jit(solution)/shard_map/ppermute | solution.py:26
  135.6 22.9 %collective-permute-start.27 = (f32[2,352,256]{2,1,0:T(8,128)S(1)}, f32[2,352,256]{2,1,0:T(8,128)S(1)}, u32[]{:S(2)}, u32[]{:S(2)}) collective-permute-start(f32[2,352,256]{2,1,0:T(8,128)S(1)} %collective-permute-done.26.refs_7_), channel_id=1, source_target_pairs={{0,16},{16,0},{32,48},{48,32},{64,80},{80,64},{96,112},{112,96},{1... | collective-permute-start | bytes 2162696 | tf_op jit(solution)/shard_map/ppermute | solution.py:26
  135.6 15.0 %collective-permute-start.33 = (f32[2,336,256]{2,1,0:T(8,128)S(1)}, f32[2,336,256]{2,1,0:T(8,128)S(1)}, u32[]{:S(2)}, u32[]{:S(2)}) collective-permute-start(f32[2,336,256]{2,1,0:T(8,128)S(1)} %pad_maximum_fusion.3), channel_id=1, source_target_pairs={{0,64},{16,80},{32,96},{48,112},{64,0},{80,16},{96,32},{112,48},{1... | collective-permute-start | bytes 2064392 | tf_op jit(solution)/shard_map/ppermute | solution.py:26
  137.3 20.7 %collective-permute-start.30 = (f32[2,336,256]{2,1,0:T(8,128)S(1)}, f32[2,336,256]{2,1,0:T(8,128)S(1)}, u32[]{:S(2)}, u32[]{:S(2)}) collective-permute-start(f32[2,336,256]{2,1,0:T(8,128)S(1)} %collective-permute-done.29.refs_9_), channel_id=1, source_target_pairs={{0,64},{16,80},{32,96},{48,112},{64,0},{80,16},{96,32},{112,48},{1... | collective-permute-start | bytes 2064392 | tf_op jit(solution)/shard_map/ppermute | solution.py:26
  147.5 10.9 %collective-permute-start.28 = (f32[2,336,256]{2,1,0:T(8,128)S(1)}, f32[2,336,256]{2,1,0:T(8,128)S(1)}, u32[]{:S(2)}, u32[]{:S(2)}) collective-permute-start(f32[2,336,256]{2,1,0:T(8,128)S(1)} %collective-permute-done.25.refs_8_), channel_id=1, source_target_pairs={{0,48},{16,32},{32,16},{48,0},{64,112},{80,96},{96,80},{112,64},{1... | collective-permute-start | bytes 2064392 | tf_op jit(solution)/shard_map/ppermute | solution.py:26

commit v4 on v3

--- a/solution.py
+++ b/solution.py
@@ -119,7 +119,7 @@
             pltpu.SemaphoreType.DMA((n,)),
             pltpu.SemaphoreType.DMA((n,)),
         ],
-        compiler_params=pltpu.CompilerParams(vmem_limit_bytes=16 * 1024 * 1024),
+        compiler_params=pltpu.CompilerParams(vmem_limit_bytes=10 * 1024 * 1024),
         cost_estimate=pl.CostEstimate(flops=n * most * block_cols, bytes_accessed=10 * n * most * block_cols, transcendentals=0),
         name="drift",
     )(in_hbm(g), in_hbm(r))
@@ -212,7 +212,7 @@
             pltpu.VMEM((p, most, block_cols), jnp.float32),
             *[pltpu.SemaphoreType.DMA((count,)) for count in (n, n, p, p, n, p)],
         ],
-        compiler_params=pltpu.CompilerParams(vmem_limit_bytes=20 * 1024 * 1024),
+        compiler_params=pltpu.CompilerParams(vmem_limit_bytes=16 * 1024 * 1024),
         cost_estimate=pl.CostEstimate(flops=n * most * block_cols, bytes_accessed=12 * n * most * block_cols, transcendentals=0),
         name="apply",
     )(*operands)
@@ -259,7 +259,7 @@
     for _ in range(3):
         around.append(lax.ppermute(around[-1], "replica", [(i, i // 4 * 4 + (i + 3) % 4) for i in range(replicas)]))
     squares = (around[0] + around[2]) + (around[1] + around[3])
-    factor = clip_factor(jnp.sum(squares[0]))
+    factor = clip_factor(jnp.broadcast_to(jnp.sum(squares, axis=1, keepdims=True), squares.shape))[:1]
     factor, prior_m = lax.optimization_barrier((factor, prior_m))
 
     clipped = [p * factor for p in grads]

time: 162 us -> 161 us (level)
  transfers between devices with their start and end apart: 34 -> 34, of which waited for: 24 -> 24; matrix products, arithmetic and copies ran while one was open for 2% -> 1% of each run, Pallas kernels for 7% -> 7%
where the time goes in v4:
time: 161 us; the launch traced here: 160 us
  waiting for transfers between devices  91.4 us (57%)
  starting transfers between devices  48.5 us (30%)
  Pallas kernels  17 us (11%)
  other arithmetic  2.38 us (1%)
    ppermute x27, waiting for transfers between devices, exchange(): return lax.ppermute(value, axis, [(i, i ^ flip) for i in range(size)])  80.3 us
    ppermute x27, starting transfers between devices, exchange(): return lax.ppermute(value, axis, [(i, i ^ flip) for i in range(size)])  39.7 us
    pallas_call x2, Pallas kernels, apply(): pl.pallas_call(functools.partial(apply_kernel, spans, block_cols, items,...  9.23 us
    pallas_call x3, Pallas kernels, drift(): pl.pallas_call(functools.partial(drift_kernel, spans, block_cols, items,...  7.81 us
    ppermute x3, waiting for transfers between devices, per_device(): lax.ppermute(around[-1], 'replica', [(i, i // 4 * 4 + (i + 3) % 4) for i...  7.53 us
    ppermute x3, starting transfers between devices, per_device(): lax.ppermute(around[-1], 'replica', [(i, i // 4 * 4 + (i + 3) % 4) for i...  4.89 us
    ppermute x3, starting transfers between devices, exchange_two(): return lax.ppermute(value, ('replica', 'shard'), pairs)  3.57 us
    ppermute x3, waiting for transfers between devices, exchange_two(): return lax.ppermute(value, ('replica', 'shard'), pairs)  3.51 us
  transfers between devices with their start and end apart: 34, of which 24 were waited for; matrix products, arithmetic and copies ran while one was open for 1% of the time, Pallas kernels for 7%

profile of v4, /device:TPU:4, one launch (start us, length us, event | category | flops | bytes accessed | tf_op | source)
XLA Modules:
  0.0 160.3 jit_solution(12670507467332818061)
XLA Ops:
  0.6 2.2 %drift.5 = (f32[2,352,256]{2,1,0:T(8,128)S(1)}, f32[2,336,256]{2,1,0:T(8,128)S(1)}, f32[2,336,256]{2,1,0:T(8,128)S(1)}) custom-call(f32[1024,2048]{1,0:T(8,128)} %bitcast.42, bf16[1024,2048]{1,0:T(8,128)(2,1)} %bitcast.47), custom_call_target="tpu_custom_call" | custom-call | flops 540672 | bytes 5406720 | tf_op jit(solution)/shard_map/drift/pallas_call | solution.py:110
  2.9 3.3 %collective-permute-start.9 = (f32[2,336,256]{2,1,0:T(8,128)S(1)}, f32[2,336,256]{2,1,0:T(8,128)S(1)}, u32[]{:S(2)}, u32[]{:S(2)}) collective-permute-start(f32[2,336,256]{2,1,0:T(8,128)S(1)} %get-tuple-element.34), channel_id=1, source_target_pairs={{0,64},{16,80},{32,96},{48,112},{64,0},{80,16},{96,32},{112,48},{1... | collective-permute-start | bytes 2064392 | tf_op jit(solution)/shard_map/ppermute | solution.py:26
  6.1 0.5 collective-permute-start.5
  6.7 1.1 collective-permute-start.1
  7.8 2.2 %drift.4 = (f32[2,352,256]{2,1,0:T(8,128)S(1)}, f32[2,336,256]{2,1,0:T(8,128)S(1)}, f32[2,336,256]{2,1,0:T(8,128)S(1)}) custom-call(f32[1024,2048]{1,0:T(8,128)} %bitcast.43, bf16[1024,2048]{1,0:T(8,128)(2,1)} %bitcast.48), custom_call_target="tpu_custom_call" | custom-call | flops 540672 | bytes 5406720 | tf_op jit(solution)/shard_map/drift/pallas_call | solution.py:110
  10.0 2.2 %collective-permute-start.4 = (f32[2,336,256]{2,1,0:T(8,128)S(1)}, f32[2,336,256]{2,1,0:T(8,128)S(1)}, u32[]{:S(2)}, u32[]{:S(2)}) collective-permute-start(f32[2,336,256]{2,1,0:T(8,128)S(1)} %get-tuple-element.30), channel_id=1, source_target_pairs={{0,48},{16,32},{32,16},{48,0},{64,112},{80,96},{96,80},{112,64},{1... | collective-permute-start | bytes 2064392 | tf_op jit(solution)/shard_map/ppermute | solution.py:26
  12.3 0.3 collective-permute-start.8
  12.6 3.4 %drift.3 = (f32[4,352,256]{2,1,0:T(8,128)S(1)}, f32[4,336,256]{2,1,0:T(8,128)S(1)}, f32[4,336,256]{2,1,0:T(8,128)S(1)}) custom-call(f32[1024,2048]{1,0:T(8,128)} %bitcast.44, bf16[1024,2048]{1,0:T(8,128)(2,1)} %bitcast.49), custom_call_target="tpu_custom_call" | custom-call | flops 1081344 | bytes 10813440 | tf_op jit(solution)/shard_map/drift/pallas_call | solution.py:110
  16.0 6.8 %collective-permute-done.9 = f32[2,336,256]{2,1,0:T(8,128)S(1)} collective-permute-done((f32[2,336,256]{2,1,0:T(8,128)S(1)}, f32[2,336,256]{2,1,0:T(8,128)S(1)}, u32[]{:S(2)}, u32[]{:S(2)}) %collective-permute-start.9) | collective-permute-done | bytes 688160 | tf_op jit(solution)/shard_map/ppermute | solution.py:26
  22.8 1.2 collective-permute-start
  24.1 0.4 collective-permute-done.5
  24.5 2.4 %collective-permute-start.10 = (f32[2,336,256]{2,1,0:T(8,128)S(1)}, f32[2,336,256]{2,1,0:T(8,128)S(1)}, u32[]{:S(2)}, u32[]{:S(2)}) collective-permute-start(f32[2,336,256]{2,1,0:T(8,128)S(1)} %slice_add_fusion.1), channel_id=1, source_target_pairs={{0,16},{16,0},{32,48},{48,32},{64,80},{80,64},{96,112},{112,96},{1... | collective-permute-start | bytes 2064392 | tf_op jit(solution)/shard_map/ppermute | solution.py:26
  27.0 1.3 collective-permute-start.6
  28.4 0.1 slice_add_fusion
  28.4 9.1 %collective-permute-done.8 = f32[2,336,256]{2,1,0:T(8,128)S(1)} collective-permute-done((f32[2,336,256]{2,1,0:T(8,128)S(1)}, f32[2,336,256]{2,1,0:T(8,128)S(1)}, u32[]{:S(2)}, u32[]{:S(2)}) %collective-permute-start.8) | collective-permute-done | bytes 688160 | tf_op jit(solution)/shard_map/ppermute | solution.py:26
  37.5 0.5 collective-permute-start.2
  38.0 16.1 %collective-permute-done.10 = f32[2,336,256]{2,1,0:T(8,128)S(1)} collective-permute-done((f32[2,336,256]{2,1,0:T(8,128)S(1)}, f32[2,336,256]{2,1,0:T(8,128)S(1)}, u32[]{:S(2)}, u32[]{:S(2)}) %collective-permute-start.10) | collective-permute-done | bytes 688160 | tf_op jit(solution)/shard_map/ppermute | solution.py:26
  54.3 1.6 %collective-permute-start.11 = (f32[336,256]{1,0:T(8,128)S(1)}, f32[336,256]{1,0:T(8,128)S(1)}, u32[]{:S(2)}, u32[]{:S(2)}) collective-permute-start(f32[336,256]{1,0:T(8,128)S(1)} %fusion.3), channel_id=1, source_target_pairs={{0,48},{16,32},{32,16},{48,0},{64,112},{80,96},{96,80},{112,64},{1... | collective-permute-start | bytes 1032200 | tf_op jit(solution)/shard_map/ppermute | solution.py:26
  56.0 2.4 %collective-permute-start.7 = (f32[336,256]{1,0:T(8,128)S(1)}, f32[336,256]{1,0:T(8,128)S(1)}, u32[]{:S(2)}, u32[]{:S(2)}) collective-permute-start(f32[336,256]{1,0:T(8,128)S(1)} %fusion.6), channel_id=1, source_target_pairs={{0,16},{16,0},{32,48},{48,32},{64,80},{80,64},{96,112},{112,96},{1... | collective-permute-start | bytes 1032200 | tf_op jit(solution)/shard_map/ppermute | solution.py:26
  58.5 0.5 collective-permute-start.3
  58.9 3.6 %collective-permute-done.11 = f32[336,256]{1,0:T(8,128)S(1)} collective-permute-done((f32[336,256]{1,0:T(8,128)S(1)}, f32[336,256]{1,0:T(8,128)S(1)}, u32[]{:S(2)}, u32[]{:S(2)}) %collective-permute-start.11) | collective-permute-done | bytes 344096 | tf_op jit(solution)/shard_map/ppermute | solution.py:26
  62.5 0.1 multiply_reduce_fusion.1
  62.6 2.1 %collective-permute-done.7 = f32[336,256]{1,0:T(8,128)S(1)} collective-permute-done((f32[336,256]{1,0:T(8,128)S(1)}, f32[336,256]{1,0:T(8,128)S(1)}, u32[]{:S(2)}, u32[]{:S(2)}) %collective-permute-start.7) | collective-permute-done | bytes 344096 | tf_op jit(solution)/shard_map/ppermute | solution.py:26
  64.7 0.1 multiply_reduce_fusion.2
  64.8 3.4 %collective-permute-done.3 = f32[352,256]{1,0:T(8,128)S(1)} collective-permute-done((f32[352,256]{1,0:T(8,128)S(1)}, f32[352,256]{1,0:T(8,128)S(1)}, u32[]{:S(2)}, u32[]{:S(2)}) %collective-permute-start.3) | collective-permute-done | bytes 360480 | tf_op jit(solution)/shard_map/ppermute | solution.py:26
  68.2 0.1 multiply_reduce_fusion
  68.3 0.4 collective-permute-start.13
  68.7 3.1 %collective-permute-start.14 = (f32[8,256]{1,0:T(8,128)S(1)}, f32[8,256]{1,0:T(8,128)S(1)}, u32[]{:S(2)}, u32[]{:S(2)}) collective-permute-start(f32[8,256]{1,0:T(8,128)S(1)} %broadcast_in_dim.4), channel_id=1, source_target_pairs={{0,72},{1,73},{2,74},{3,75},{4,76},{5,77},{6,78},{7,79},{8,64},{9,... | collective-permute-start | bytes 24584 | tf_op jit(solution)/shard_map/ppermute | solution.py:31
  71.7 0.1 collective-permute-start.12
  71.9 1.7 %collective-permute-done.13 = f32[8,256]{1,0:T(8,128)S(1)} collective-permute-done((f32[8,256]{1,0:T(8,128)S(1)}, f32[8,256]{1,0:T(8,128)S(1)}, u32[]{:S(2)}, u32[]{:S(2)}) %collective-permute-start.13) | collective-permute-done | bytes 8224 | tf_op jit(solution)/shard_map/ppermute | solution.py:31
  73.6 1.8 %collective-permute-done.12 = f32[8,256]{1,0:T(8,128)S(1)} collective-permute-done((f32[8,256]{1,0:T(8,128)S(1)}, f32[8,256]{1,0:T(8,128)S(1)}, u32[]{:S(2)}, u32[]{:S(2)}) %collective-permute-start.12) | collective-permute-done | bytes 8224 | tf_op jit(solution)/shard_map/ppermute | solution.py:31
  75.4 0.4 collective-permute-start.21
  75.8 1.9 %collective-permute-start.15 = (f32[8,256]{1,0:T(8,128)S(1)}, f32[8,256]{1,0:T(8,128)S(1)}, u32[]{:S(2)}, u32[]{:S(2)}) collective-permute-start(f32[8,256]{1,0:T(8,128)S(1)} %add_add_fusion), channel_id=1, source_target_pairs={{0,2},{1,3},{2,0},{3,1},{4,6},{5,7},{6,4},{7,5},{8,10},{9,11},{10,... | collective-permute-start | bytes 24584 | tf_op jit(solution)/shard_map/ppermute | solution.py:26
  77.7 1.7 %collective-permute-done.15 = f32[8,256]{1,0:T(8,128)S(1)} collective-permute-done((f32[8,256]{1,0:T(8,128)S(1)}, f32[8,256]{1,0:T(8,128)S(1)}, u32[]{:S(2)}, u32[]{:S(2)}) %collective-permute-start.15) | collective-permute-done | bytes 8224 | tf_op jit(solution)/shard_map/ppermute | solution.py:26
  79.4 4.0 %collective-permute-start.16 = (f32[8,256]{1,0:T(8,128)S(1)}, f32[8,256]{1,0:T(8,128)S(1)}, u32[]{:S(2)}, u32[]{:S(2)}) collective-permute-start(f32[8,256]{1,0:T(8,128)S(1)} %add.165), channel_id=1, source_target_pairs={{0,6},{1,7},{2,4},{3,5},{4,2},{5,3},{6,0},{7,1},{8,14},{9,15},{10,... | collective-permute-start | bytes 24584 | tf_op jit(solution)/shard_map/ppermute | solution.py:26
  83.5 1.6 %collective-permute-done.16 = f32[8,256]{1,0:T(8,128)S(1)} collective-permute-done((f32[8,256]{1,0:T(8,128)S(1)}, f32[8,256]{1,0:T(8,128)S(1)}, u32[]{:S(2)}, u32[]{:S(2)}) %collective-permute-start.16) | collective-permute-done | bytes 8224 | tf_op jit(solution)/shard_map/ppermute | solution.py:26
  85.1 1.2 collective-permute-done.17
  86.3 1.7 %collective-permute-start.18 = (f32[8,256]{1,0:T(8,128)S(1)}, f32[8,256]{1,0:T(8,128)S(1)}, u32[]{:S(2)}, u32[]{:S(2)}) collective-permute-start(f32[8,256]{1,0:T(8,128)S(1)} %add.167), channel_id=1, source_target_pairs={{0,48},{16,0},{32,16},{48,32},{64,112},{80,64},{96,80},{112,96},{1... | collective-permute-start | bytes 24584 | tf_op jit(solution)/shard_map/ppermute | solution.py:260
  88.0 1.9 %collective-permute-done.18 = f32[8,256]{1,0:T(8,128)S(1)} collective-permute-done((f32[8,256]{1,0:T(8,128)S(1)}, f32[8,256]{1,0:T(8,128)S(1)}, u32[]{:S(2)}, u32[]{:S(2)}) %collective-permute-start.18) | collective-permute-done | bytes 8224 | tf_op jit(solution)/shard_map/ppermute | solution.py:260
  89.9 1.7 %collective-permute-start.19 = (f32[8,256]{1,0:T(8,128)S(1)}, f32[8,256]{1,0:T(8,128)S(1)}, u32[]{:S(2)}, u32[]{:S(2)}) collective-permute-start(f32[8,256]{1,0:T(8,128)S(1)} %collective-permute-done.18), channel_id=1, source_target_pairs={{0,48},{16,0},{32,16},{48,32},{64,112},{80,64},{96,80},{112,96},{1... | collective-permute-start | bytes 24584 | tf_op jit(solution)/shard_map/ppermute | solution.py:260
  91.6 2.2 %collective-permute-done.19 = f32[8,256]{1,0:T(8,128)S(1)} collective-permute-done((f32[8,256]{1,0:T(8,128)S(1)}, f32[8,256]{1,0:T(8,128)S(1)}, u32[]{:S(2)}, u32[]{:S(2)}) %collective-permute-start.19) | collective-permute-done | bytes 8224 | tf_op jit(solution)/shard_map/ppermute | solution.py:260
  93.8 1.5 collective-permute-start.20
  95.3 3.4 %collective-permute-done.20 = f32[8,256]{1,0:T(8,128)S(1)} collective-permute-done((f32[8,256]{1,0:T(8,128)S(1)}, f32[8,256]{1,0:T(8,128)S(1)}, u32[]{:S(2)}, u32[]{:S(2)}) %collective-permute-start.20) | collective-permute-done | bytes 8224 | tf_op jit(solution)/shard_map/ppermute | solution.py:260
  98.7 0.1 add_reduce_fusion
  98.9 0.2 multiply_add_fusion.3
  99.0 3.3 %collective-permute-start.23 = (f32[336,256]{1,0:T(8,128)S(1)}, f32[336,256]{1,0:T(8,128)S(1)}, u32[]{:S(2)}, u32[]{:S(2)}) collective-permute-start(f32[336,256]{1,0:T(8,128)S(1)} %get-tuple-element.58.refs_2_), channel_id=1, source_target_pairs={{0,16},{16,0},{32,48},{48,32},{64,80},{80,64},{96,112},{112,96},{1... | collective-permute-start | bytes 1032200 | tf_op jit(solution)/shard_map/ppermute | solution.py:26
  102.4 2.3 %collective-permute-start.22 = (f32[352,256]{1,0:T(8,128)S(1)}, f32[352,256]{1,0:T(8,128)S(1)}, u32[]{:S(2)}, u32[]{:S(2)}) collective-permute-start(f32[352,256]{1,0:T(8,128)S(1)} %get-tuple-element.56.refs_1_), channel_id=1, source_target_pairs={{0,64},{16,80},{32,96},{48,112},{64,0},{80,16},{96,32},{112,48},{1... | collective-permute-start | bytes 1081352 | tf_op jit(solution)/shard_map/ppermute | solution.py:26
  104.7 2.9 %collective-permute-done.23.refs_5_.refs_4_ = f32[336,256]{1,0:T(8,128)S(1)} collective-permute-done((f32[336,256]{1,0:T(8,128)S(1)}, f32[336,256]{1,0:T(8,128)S(1)}, u32[]{:S(2)}, u32[]{:S(2)}) %collective-permute-start.23) | collective-permute-done | bytes 344096 | tf_op jit(solution)/shard_map/ppermute | solution.py:26
  107.6 2.3 %collective-permute-start.25 = (f32[2,336,256]{2,1,0:T(8,128)S(1)}, f32[2,336,256]{2,1,0:T(8,128)S(1)}, u32[]{:S(2)}, u32[]{:S(2)}) collective-permute-start(f32[2,336,256]{2,1,0:T(8,128)S(1)} %pad_maximum_fusion.2), channel_id=1, source_target_pairs={{0,64},{16,80},{32,96},{48,112},{64,0},{80,16},{96,32},{112,48},{1... | collective-permute-start | bytes 2064392 | tf_op jit(solution)/shard_map/ppermute | solution.py:26
  109.9 5.3 %collective-permute-done.22.refs_4_ = f32[352,256]{1,0:T(8,128)S(1)} collective-permute-done((f32[352,256]{1,0:T(8,128)S(1)}, f32[352,256]{1,0:T(8,128)S(1)}, u32[]{:S(2)}, u32[]{:S(2)}) %collective-permute-start.22) | collective-permute-done | bytes 360480 | tf_op jit(solution)/shard_map/ppermute | solution.py:26
  115.5 2.1 %collective-permute-start.31 = (f32[2,336,256]{2,1,0:T(8,128)S(1)}, f32[2,336,256]{2,1,0:T(8,128)S(1)}, u32[]{:S(2)}, u32[]{:S(2)}) collective-permute-start(f32[2,336,256]{2,1,0:T(8,128)S(1)} %pad_maximum_fusion.2), channel_id=1, source_target_pairs={{0,48},{16,32},{32,16},{48,0},{64,112},{80,96},{96,80},{112,64},{1... | collective-permute-start | bytes 2064392 | tf_op jit(solution)/shard_map/ppermute | solution.py:26
  117.6 2.5 %collective-permute-start.32 = (f32[2,352,256]{2,1,0:T(8,128)S(1)}, f32[2,352,256]{2,1,0:T(8,128)S(1)}, u32[]{:S(2)}, u32[]{:S(2)}) collective-permute-start(f32[2,352,256]{2,1,0:T(8,128)S(1)} %pad_maximum_fusion.1), channel_id=1, source_target_pairs={{0,16},{16,0},{32,48},{48,32},{64,80},{80,64},{96,112},{112,96},{1... | collective-permute-start | bytes 2162696 | tf_op jit(solution)/shard_map/ppermute | solution.py:26
  120.2 6.0 %collective-permute-done.25.refs_8_ = f32[2,336,256]{2,1,0:T(8,128)S(1)} collective-permute-done((f32[2,336,256]{2,1,0:T(8,128)S(1)}, f32[2,336,256]{2,1,0:T(8,128)S(1)}, u32[]{:S(2)}, u32[]{:S(2)}) %collective-permute-start.25) | collective-permute-done | bytes 688160 | tf_op jit(solution)/shard_map/ppermute | solution.py:26
  126.2 8.2 %collective-permute-done.26.refs_7_ = f32[2,352,256]{2,1,0:T(8,128)S(1)} collective-permute-done((f32[2,352,256]{2,1,0:T(8,128)S(1)}, f32[2,352,256]{2,1,0:T(8,128)S(1)}, u32[]{:S(2)}, u32[]{:S(2)}) %collective-permute-start.26) | collective-permute-done | bytes 720928 | tf_op jit(solution)/shard_map/ppermute | solution.py:26
  134.5 1.7 %collective-permute-start.33 = (f32[2,336,256]{2,1,0:T(8,128)S(1)}, f32[2,336,256]{2,1,0:T(8,128)S(1)}, u32[]{:S(2)}, u32[]{:S(2)}) collective-permute-start(f32[2,336,256]{2,1,0:T(8,128)S(1)} %pad_maximum_fusion.3), channel_id=1, source_target_pairs={{0,64},{16,80},{32,96},{48,112},{64,0},{80,16},{96,32},{112,48},{1... | collective-permute-start | bytes 2064392 | tf_op jit(solution)/shard_map/ppermute | solution.py:26
  136.1 1.9 %collective-permute-start.30 = (f32[2,336,256]{2,1,0:T(8,128)S(1)}, f32[2,336,256]{2,1,0:T(8,128)S(1)}, u32[]{:S(2)}, u32[]{:S(2)}) collective-permute-start(f32[2,336,256]{2,1,0:T(8,128)S(1)} %collective-permute-done.29.refs_9_), channel_id=1, source_target_pairs={{0,64},{16,80},{32,96},{48,112},{64,0},{80,16},{96,32},{112,48},{1... | collective-permute-start | bytes 2064392 | tf_op jit(solution)/shard_map/ppermute | solution.py:26
  138.0 8.4 %collective-permute-done.31.refs_11_.refs_5_ = f32[2,336,256]{2,1,0:T(8,128)S(1)} collective-permute-done((f32[2,336,256]{2,1,0:T(8,128)S(1)}, f32[2,336,256]{2,1,0:T(8,128)S(1)}, u32[]{:S(2)}, u32[]{:S(2)}) %collective-permute-start.31) | collective-permute-done | bytes 688160 | tf_op jit(solution)/shard_map/ppermute | solution.py:26
  146.4 1.0 pad_maximum_fusion
  147.5 0.5 collective-permute-done.32.refs_10_
  147.9 1.6 collective-permute-done.33.refs_12_
  149.5 6.4 %apply.2 = (f32[1024,2048]{1,0:T(8,128)}, f32[1024,256]{1,0:T(8,128)}) custom-call(f32[1024,2048]{1,0:T(8,128)} %bitcast.45, f32[352,256]{1,0:T(8,128)S(1)} %get-tuple-element.56.refs_1_, f32[336,256]{1,0:T(8,128)S(1)} %get-tuple-element.58.refs_2_, f32[336,256]{1,0:T(8,128)S(1)} %get-tuple-element.61.refs_3_, ...), custom_call_target="tpu_custom_call" | custom-call | flops 1622016 | bytes 19464192 | tf_op jit(solution)/shard_map/apply/pallas_call | solution.py:202
  155.9 1.0 collective-permute-done.30.refs_3_
  156.9 0.5 collective-permute-done.28.refs_2_
  157.4 2.8 %apply.3 = (f32[1024,2048]{1,0:T(8,128)}, f32[1024,256]{1,0:T(8,128)}) custom-call(f32[1024,2048]{1,0:T(8,128)} %bitcast.46, f32[2,352,256]{2,1,0:T(8,128)S(1)} %collective-permute-done.27.refs_1_, f32[2,336,256]{2,1,0:T(8,128)S(1)} %collective-permute-done.28.refs_2_, ...), custom_call_target="tpu_custom_call", output_to_operand_aliasing={{0}: (7, {}), {1}: (8, {})} | custom-call | flops 540672 | bytes 6488064 | tf_op jit(solution)/shard_map/apply/pallas_call | solution.py:202
  (36 shorter events, 0.9 us)
Async XLA Ops:
  2.9 19.9 %collective-permute-start.9 = (f32[2,336,256]{2,1,0:T(8,128)S(1)}, f32[2,336,256]{2,1,0:T(8,128)S(1)}, u32[]{:S(2)}, u32[]{:S(2)}) collective-permute-start(f32[2,336,256]{2,1,0:T(8,128)S(1)} %get-tuple-element.34), channel_id=1, source_target_pairs={{0,64},{16,80},{32,96},{48,112},{64,0},{80,16},{96,32},{112,48},{1... | collective-permute-start | bytes 2064392 | tf_op jit(solution)/shard_map/ppermute | solution.py:26
  6.1 18.4 %collective-permute-start.5 = (f32[2,336,256]{2,1,0:T(8,128)S(1)}, f32[2,336,256]{2,1,0:T(8,128)S(1)}, u32[]{:S(2)}, u32[]{:S(2)}) collective-permute-start(f32[2,336,256]{2,1,0:T(8,128)S(1)} %get-tuple-element.31), channel_id=1, source_target_pairs={{0,48},{16,32},{32,16},{48,0},{64,112},{80,96},{96,80},{112,64},{1... | collective-permute-start | bytes 2064392 | tf_op jit(solution)/shard_map/ppermute | solution.py:26
  6.7 20.3 %collective-permute-start.1 = (f32[2,352,256]{2,1,0:T(8,128)S(1)}, f32[2,352,256]{2,1,0:T(8,128)S(1)}, u32[]{:S(2)}, u32[]{:S(2)}) collective-permute-start(f32[2,352,256]{2,1,0:T(8,128)S(1)} %get-tuple-element.28), channel_id=1, source_target_pairs={{0,16},{16,0},{32,48},{48,32},{64,80},{80,64},{96,112},{112,96},{1... | collective-permute-start | bytes 2162696 | tf_op jit(solution)/shard_map/ppermute | solution.py:26
  10.0 45.9 %collective-permute-start.4 = (f32[2,336,256]{2,1,0:T(8,128)S(1)}, f32[2,336,256]{2,1,0:T(8,128)S(1)}, u32[]{:S(2)}, u32[]{:S(2)}) collective-permute-start(f32[2,336,256]{2,1,0:T(8,128)S(1)} %get-tuple-element.30), channel_id=1, source_target_pairs={{0,48},{16,32},{32,16},{48,0},{64,112},{80,96},{96,80},{112,64},{1... | collective-permute-start | bytes 2064392 | tf_op jit(solution)/shard_map/ppermute | solution.py:26
  12.3 25.2 %collective-permute-start.8 = (f32[2,336,256]{2,1,0:T(8,128)S(1)}, f32[2,336,256]{2,1,0:T(8,128)S(1)}, u32[]{:S(2)}, u32[]{:S(2)}) collective-permute-start(f32[2,336,256]{2,1,0:T(8,128)S(1)} %get-tuple-element.33), channel_id=1, source_target_pairs={{0,64},{16,80},{32,96},{48,112},{64,0},{80,16},{96,32},{112,48},{1... | collective-permute-start | bytes 2064392 | tf_op jit(solution)/shard_map/ppermute | solution.py:26
  22.8 35.6 %collective-permute-start = (f32[2,352,256]{2,1,0:T(8,128)S(1)}, f32[2,352,256]{2,1,0:T(8,128)S(1)}, u32[]{:S(2)}, u32[]{:S(2)}) collective-permute-start(f32[2,352,256]{2,1,0:T(8,128)S(1)} %get-tuple-element.27), channel_id=1, source_target_pairs={{0,16},{16,0},{32,48},{48,32},{64,80},{80,64},{96,112},{112,96},{1... | collective-permute-start | bytes 2162696 | tf_op jit(solution)/shard_map/ppermute | solution.py:26
  24.5 29.7 %collective-permute-start.10 = (f32[2,336,256]{2,1,0:T(8,128)S(1)}, f32[2,336,256]{2,1,0:T(8,128)S(1)}, u32[]{:S(2)}, u32[]{:S(2)}) collective-permute-start(f32[2,336,256]{2,1,0:T(8,128)S(1)} %slice_add_fusion.1), channel_id=1, source_target_pairs={{0,16},{16,0},{32,48},{48,32},{64,80},{80,64},{96,112},{112,96},{1... | collective-permute-start | bytes 2064392 | tf_op jit(solution)/shard_map/ppermute | solution.py:26
  27.0 28.9 %collective-permute-start.6 = (f32[2,336,256]{2,1,0:T(8,128)S(1)}, f32[2,336,256]{2,1,0:T(8,128)S(1)}, u32[]{:S(2)}, u32[]{:S(2)}) collective-permute-start(f32[2,336,256]{2,1,0:T(8,128)S(1)} %slice_add_fusion.2), channel_id=1, source_target_pairs={{0,64},{16,80},{32,96},{48,112},{64,0},{80,16},{96,32},{112,48},{1... | collective-permute-start | bytes 2064392 | tf_op jit(solution)/shard_map/ppermute | solution.py:26
  37.5 20.9 %collective-permute-start.2 = (f32[2,352,256]{2,1,0:T(8,128)S(1)}, f32[2,352,256]{2,1,0:T(8,128)S(1)}, u32[]{:S(2)}, u32[]{:S(2)}) collective-permute-start(f32[2,352,256]{2,1,0:T(8,128)S(1)} %slice_add_fusion), channel_id=1, source_target_pairs={{0,48},{16,32},{32,16},{48,0},{64,112},{80,96},{96,80},{112,64},{1... | collective-permute-start | bytes 2162696 | tf_op jit(solution)/shard_map/ppermute | solution.py:26
  54.3 8.3 %collective-permute-start.11 = (f32[336,256]{1,0:T(8,128)S(1)}, f32[336,256]{1,0:T(8,128)S(1)}, u32[]{:S(2)}, u32[]{:S(2)}) collective-permute-start(f32[336,256]{1,0:T(8,128)S(1)} %fusion.3), channel_id=1, source_target_pairs={{0,48},{16,32},{32,16},{48,0},{64,112},{80,96},{96,80},{112,64},{1... | collective-permute-start | bytes 1032200 | tf_op jit(solution)/shard_map/ppermute | solution.py:26
  56.0 8.7 %collective-permute-start.7 = (f32[336,256]{1,0:T(8,128)S(1)}, f32[336,256]{1,0:T(8,128)S(1)}, u32[]{:S(2)}, u32[]{:S(2)}) collective-permute-start(f32[336,256]{1,0:T(8,128)S(1)} %fusion.6), channel_id=1, source_target_pairs={{0,16},{16,0},{32,48},{48,32},{64,80},{80,64},{96,112},{112,96},{1... | collective-permute-start | bytes 1032200 | tf_op jit(solution)/shard_map/ppermute | solution.py:26
  58.5 9.7 %collective-permute-start.3 = (f32[352,256]{1,0:T(8,128)S(1)}, f32[352,256]{1,0:T(8,128)S(1)}, u32[]{:S(2)}, u32[]{:S(2)}) collective-permute-start(f32[352,256]{1,0:T(8,128)S(1)} %fusion), channel_id=1, source_target_pairs={{0,64},{16,80},{32,96},{48,112},{64,0},{80,16},{96,32},{112,48},{1... | collective-permute-start | bytes 1081352 | tf_op jit(solution)/shard_map/ppermute | solution.py:26
  62.6 12.8 %copy-start = (f32[2,512,256]{2,1,0:T(8,128)S(1)}, f32[2,512,256]{2,1,0:T(8,128)}, u32[]{:S(2)}) copy-start(f32[2,512,256]{2,1,0:T(8,128)} %param.5) | copy-start | bytes 3145732
  68.3 5.3 %collective-permute-start.13 = (f32[8,256]{1,0:T(8,128)S(1)}, f32[8,256]{1,0:T(8,128)S(1)}, u32[]{:S(2)}, u32[]{:S(2)}) collective-permute-start(f32[8,256]{1,0:T(8,128)S(1)} %broadcast_in_dim.4), channel_id=1, source_target_pairs={{0,64},{1,65},{2,66},{3,67},{4,68},{5,69},{6,70},{7,71},{8,72},{9,... | collective-permute-start | bytes 24584 | tf_op jit(solution)/shard_map/ppermute | solution.py:31
  68.7 5.0 %collective-permute-start.14 = (f32[8,256]{1,0:T(8,128)S(1)}, f32[8,256]{1,0:T(8,128)S(1)}, u32[]{:S(2)}, u32[]{:S(2)}) collective-permute-start(f32[8,256]{1,0:T(8,128)S(1)} %broadcast_in_dim.4), channel_id=1, source_target_pairs={{0,72},{1,73},{2,74},{3,75},{4,76},{5,77},{6,78},{7,79},{8,64},{9,... | collective-permute-start | bytes 24584 | tf_op jit(solution)/shard_map/ppermute | solution.py:31
  71.7 3.7 %collective-permute-start.12 = (f32[8,256]{1,0:T(8,128)S(1)}, f32[8,256]{1,0:T(8,128)S(1)}, u32[]{:S(2)}, u32[]{:S(2)}) collective-permute-start(f32[8,256]{1,0:T(8,128)S(1)} %broadcast_in_dim.4), channel_id=1, source_target_pairs={{0,8},{1,9},{2,10},{3,11},{4,12},{5,13},{6,14},{7,15},{8,0},{9,1},... | collective-permute-start | bytes 24584 | tf_op jit(solution)/shard_map/ppermute | solution.py:31
  75.4 23.4 %collective-permute-start.21 = (f32[1024,256]{1,0:T(8,128)S(1)}, f32[1024,256]{1,0:T(8,128)S(1)}, u32[]{:S(2)}, u32[]{:S(2)}) collective-permute-start(f32[1024,256]{1,0:T(8,128)S(1)} %bitcast.52), channel_id=1, source_target_pairs={{0,16},{16,32},{32,48},{48,64},{64,80},{80,96},{96,112},{112,0},{1... | collective-permute-start | bytes 3145736 | tf_op jit(solution)/shard_map/ppermute | solution.py:255
  75.8 3.7 %collective-permute-start.15 = (f32[8,256]{1,0:T(8,128)S(1)}, f32[8,256]{1,0:T(8,128)S(1)}, u32[]{:S(2)}, u32[]{:S(2)}) collective-permute-start(f32[8,256]{1,0:T(8,128)S(1)} %add_add_fusion), channel_id=1, source_target_pairs={{0,2},{1,3},{2,0},{3,1},{4,6},{5,7},{6,4},{7,5},{8,10},{9,11},{10,... | collective-permute-start | bytes 24584 | tf_op jit(solution)/shard_map/ppermute | solution.py:26
  79.4 5.7 %collective-permute-start.16 = (f32[8,256]{1,0:T(8,128)S(1)}, f32[8,256]{1,0:T(8,128)S(1)}, u32[]{:S(2)}, u32[]{:S(2)}) collective-permute-start(f32[8,256]{1,0:T(8,128)S(1)} %add.165), channel_id=1, source_target_pairs={{0,6},{1,7},{2,4},{3,5},{4,2},{5,3},{6,0},{7,1},{8,14},{9,15},{10,... | collective-permute-start | bytes 24584 | tf_op jit(solution)/shard_map/ppermute | solution.py:26
  85.1 1.2 collective-permute-start.17
  86.3 3.7 %collective-permute-start.18 = (f32[8,256]{1,0:T(8,128)S(1)}, f32[8,256]{1,0:T(8,128)S(1)}, u32[]{:S(2)}, u32[]{:S(2)}) collective-permute-start(f32[8,256]{1,0:T(8,128)S(1)} %add.167), channel_id=1, source_target_pairs={{0,48},{16,0},{32,16},{48,32},{64,112},{80,64},{96,80},{112,96},{1... | collective-permute-start | bytes 24584 | tf_op jit(solution)/shard_map/ppermute | solution.py:260
  89.9 3.9 %collective-permute-start.19 = (f32[8,256]{1,0:T(8,128)S(1)}, f32[8,256]{1,0:T(8,128)S(1)}, u32[]{:S(2)}, u32[]{:S(2)}) collective-permute-start(f32[8,256]{1,0:T(8,128)S(1)} %collective-permute-done.18), channel_id=1, source_target_pairs={{0,48},{16,0},{32,16},{48,32},{64,112},{80,64},{96,80},{112,96},{1... | collective-permute-start | bytes 24584 | tf_op jit(solution)/shard_map/ppermute | solution.py:260
  93.8 4.9 %collective-permute-start.20 = (f32[8,256]{1,0:T(8,128)S(1)}, f32[8,256]{1,0:T(8,128)S(1)}, u32[]{:S(2)}, u32[]{:S(2)}) collective-permute-start(f32[8,256]{1,0:T(8,128)S(1)} %collective-permute-done.19), channel_id=1, source_target_pairs={{0,48},{16,0},{32,16},{48,32},{64,112},{80,64},{96,80},{112,96},{1... | collective-permute-start | bytes 24584 | tf_op jit(solution)/shard_map/ppermute | solution.py:260
  99.0 8.5 %collective-permute-start.23 = (f32[336,256]{1,0:T(8,128)S(1)}, f32[336,256]{1,0:T(8,128)S(1)}, u32[]{:S(2)}, u32[]{:S(2)}) collective-permute-start(f32[336,256]{1,0:T(8,128)S(1)} %get-tuple-element.58.refs_2_), channel_id=1, source_target_pairs={{0,16},{16,0},{32,48},{48,32},{64,80},{80,64},{96,112},{112,96},{1... | collective-permute-start | bytes 1032200 | tf_op jit(solution)/shard_map/ppermute | solution.py:26
  102.4 12.8 %collective-permute-start.22 = (f32[352,256]{1,0:T(8,128)S(1)}, f32[352,256]{1,0:T(8,128)S(1)}, u32[]{:S(2)}, u32[]{:S(2)}) collective-permute-start(f32[352,256]{1,0:T(8,128)S(1)} %get-tuple-element.56.refs_1_), channel_id=1, source_target_pairs={{0,64},{16,80},{32,96},{48,112},{64,0},{80,16},{96,32},{112,48},{1... | collective-permute-start | bytes 1081352 | tf_op jit(solution)/shard_map/ppermute | solution.py:26
  104.7 10.7 %collective-permute-start.24 = (f32[336,256]{1,0:T(8,128)S(1)}, f32[336,256]{1,0:T(8,128)S(1)}, u32[]{:S(2)}, u32[]{:S(2)}) collective-permute-start(f32[336,256]{1,0:T(8,128)S(1)} %get-tuple-element.61.refs_3_), channel_id=1, source_target_pairs={{0,48},{16,32},{32,16},{48,0},{64,112},{80,96},{96,80},{112,64},{1... | collective-permute-start | bytes 1032200 | tf_op jit(solution)/shard_map/ppermute | solution.py:26
  107.6 18.6 %collective-permute-start.25 = (f32[2,336,256]{2,1,0:T(8,128)S(1)}, f32[2,336,256]{2,1,0:T(8,128)S(1)}, u32[]{:S(2)}, u32[]{:S(2)}) collective-permute-start(f32[2,336,256]{2,1,0:T(8,128)S(1)} %pad_maximum_fusion.2), channel_id=1, source_target_pairs={{0,64},{16,80},{32,96},{48,112},{64,0},{80,16},{96,32},{112,48},{1... | collective-permute-start | bytes 2064392 | tf_op jit(solution)/shard_map/ppermute | solution.py:26
  115.3 19.2 %collective-permute-start.26 = (f32[2,352,256]{2,1,0:T(8,128)S(1)}, f32[2,352,256]{2,1,0:T(8,128)S(1)}, u32[]{:S(2)}, u32[]{:S(2)}) collective-permute-start(f32[2,352,256]{2,1,0:T(8,128)S(1)} %pad_maximum_fusion.1), channel_id=1, source_target_pairs={{0,48},{16,32},{32,16},{48,0},{64,112},{80,96},{96,80},{112,64},{1... | collective-permute-start | bytes 2162696 | tf_op jit(solution)/shard_map/ppermute | solution.py:26
  115.5 20.7 %collective-permute-start.29 = (f32[2,336,256]{2,1,0:T(8,128)S(1)}, f32[2,336,256]{2,1,0:T(8,128)S(1)}, u32[]{:S(2)}, u32[]{:S(2)}) collective-permute-start(f32[2,336,256]{2,1,0:T(8,128)S(1)} %pad_maximum_fusion.3), channel_id=1, source_target_pairs={{0,16},{16,0},{32,48},{48,32},{64,80},{80,64},{96,112},{112,96},{1... | collective-permute-start | bytes 2064392 | tf_op jit(solution)/shard_map/ppermute | solution.py:26
  115.5 30.9 %collective-permute-start.31 = (f32[2,336,256]{2,1,0:T(8,128)S(1)}, f32[2,336,256]{2,1,0:T(8,128)S(1)}, u32[]{:S(2)}, u32[]{:S(2)}) collective-permute-start(f32[2,336,256]{2,1,0:T(8,128)S(1)} %pad_maximum_fusion.2), channel_id=1, source_target_pairs={{0,48},{16,32},{32,16},{48,0},{64,112},{80,96},{96,80},{112,64},{1... | collective-permute-start | bytes 2064392 | tf_op jit(solution)/shard_map/ppermute | solution.py:26
  117.6 30.3 %collective-permute-start.32 = (f32[2,352,256]{2,1,0:T(8,128)S(1)}, f32[2,352,256]{2,1,0:T(8,128)S(1)}, u32[]{:S(2)}, u32[]{:S(2)}) collective-permute-start(f32[2,352,256]{2,1,0:T(8,128)S(1)} %pad_maximum_fusion.1), channel_id=1, source_target_pairs={{0,16},{16,0},{32,48},{48,32},{64,80},{80,64},{96,112},{112,96},{1... | collective-permute-start | bytes 2162696 | tf_op jit(solution)/shard_map/ppermute | solution.py:26
  134.4 22.9 %collective-permute-start.27 = (f32[2,352,256]{2,1,0:T(8,128)S(1)}, f32[2,352,256]{2,1,0:T(8,128)S(1)}, u32[]{:S(2)}, u32[]{:S(2)}) collective-permute-start(f32[2,352,256]{2,1,0:T(8,128)S(1)} %collective-permute-done.26.refs_7_), channel_id=1, source_target_pairs={{0,16},{16,0},{32,48},{48,32},{64,80},{80,64},{96,112},{112,96},{1... | collective-permute-start | bytes 2162696 | tf_op jit(solution)/shard_map/ppermute | solution.py:26
  134.5 15.0 %collective-permute-start.33 = (f32[2,336,256]{2,1,0:T(8,128)S(1)}, f32[2,336,256]{2,1,0:T(8,128)S(1)}, u32[]{:S(2)}, u32[]{:S(2)}) collective-permute-start(f32[2,336,256]{2,1,0:T(8,128)S(1)} %pad_maximum_fusion.3), channel_id=1, source_target_pairs={{0,64},{16,80},{32,96},{48,112},{64,0},{80,16},{96,32},{112,48},{1... | collective-permute-start | bytes 2064392 | tf_op jit(solution)/shard_map/ppermute | solution.py:26
  136.1 20.7 %collective-permute-start.30 = (f32[2,336,256]{2,1,0:T(8,128)S(1)}, f32[2,336,256]{2,1,0:T(8,128)S(1)}, u32[]{:S(2)}, u32[]{:S(2)}) collective-permute-start(f32[2,336,256]{2,1,0:T(8,128)S(1)} %collective-permute-done.29.refs_9_), channel_id=1, source_target_pairs={{0,64},{16,80},{32,96},{48,112},{64,0},{80,16},{96,32},{112,48},{1... | collective-permute-start | bytes 2064392 | tf_op jit(solution)/shard_map/ppermute | solution.py:26
  146.4 10.9 %collective-permute-start.28 = (f32[2,336,256]{2,1,0:T(8,128)S(1)}, f32[2,336,256]{2,1,0:T(8,128)S(1)}, u32[]{:S(2)}, u32[]{:S(2)}) collective-permute-start(f32[2,336,256]{2,1,0:T(8,128)S(1)} %collective-permute-done.25.refs_8_), channel_id=1, source_target_pairs={{0,48},{16,32},{32,16},{48,0},{64,112},{80,96},{96,80},{112,64},{1... | collective-permute-start | bytes 2064392 | tf_op jit(solution)/shard_map/ppermute | solution.py:26

commit v5 on v4

--- a/solution.py
+++ b/solution.py
@@ -248,7 +248,8 @@
     got4 = [cross(k, 2, fourth[k]) for k in parts]
     grads = [(kept[k][0] + got2[k][0] + got3[k][0] + got4[k]) / replicas for k in parts]
 
-    squares = jnp.broadcast_to(sum(jnp.sum(p * p, axis=0) for p in grads), (8, block_cols))
+    squares = sum(jnp.sum(p * p, axis=0) for p in grads)
+    squares = jnp.broadcast_to(squares[:128] + squares[128:], (8, 128))
     over_y = [exchange_two(squares, a, b) for a, b in ((0, 8), (4, 0), (4, 8))]
     squares = (squares + over_y[0]) + (over_y[1] + over_y[2])
     squares, m = tie(squares, m)
@@ -259,7 +260,7 @@
     for _ in range(3):
         around.append(lax.ppermute(around[-1], "replica", [(i, i // 4 * 4 + (i + 3) % 4) for i in range(replicas)]))
     squares = (around[0] + around[2]) + (around[1] + around[3])
-    factor = clip_factor(jnp.broadcast_to(jnp.sum(squares, axis=1, keepdims=True), squares.shape))[:1]
+    factor = clip_factor(jnp.broadcast_to(jnp.sum(squares, axis=1, keepdims=True), (8, block_cols)))[:1]
     factor, prior_m = lax.optimization_barrier((factor, prior_m))
 
     clipped = [p * factor for p in grads]

time: 161 us -> 160 us (level)
  no operation moved by 1% of the time
where the time goes in v5:
time: 160 us
  waiting for transfers between devices  90.9 us (57%)
  starting transfers between devices  48.7 us (30%)
  Pallas kernels  17 us (11%)
  other arithmetic  2.38 us (1%)
    ppermute x27, waiting for transfers between devices, exchange(): return lax.ppermute(value, axis, [(i, i ^ flip) for i in range(size)])  80.2 us
    ppermute x27, starting transfers between devices, exchange(): return lax.ppermute(value, axis, [(i, i ^ flip) for i in range(size)])  39.8 us
    pallas_call x2, Pallas kernels, apply(): pl.pallas_call(functools.partial(apply_kernel, spans, block_cols, items,...  9.23 us
    pallas_call x3, Pallas kernels, drift(): pl.pallas_call(functools.partial(drift_kernel, spans, block_cols, items,...  7.81 us
    ppermute x3, waiting for transfers between devices, per_device(): lax.ppermute(around[-1], 'replica', [(i, i // 4 * 4 + (i + 3) % 4) for i...  7.31 us
    ppermute x3, starting transfers between devices, per_device(): lax.ppermute(around[-1], 'replica', [(i, i // 4 * 4 + (i + 3) % 4) for i...  4.93 us
    ppermute x3, starting transfers between devices, exchange_two(): return lax.ppermute(value, ('replica', 'shard'), pairs)  3.57 us
    ppermute x3, waiting for transfers between devices, exchange_two(): return lax.ppermute(value, ('replica', 'shard'), pairs)  3.47 us
  transfers between devices with their start and end apart: 34, of which 24 were waited for; matrix products, arithmetic and copies ran while one was open for 1% of the time, Pallas kernels for 7%

profile of v5, /device:TPU:4, one launch (start us, length us, event | category | flops | bytes accessed | tf_op | source)
XLA Modules:
  0.0 160.0 jit_solution(2171643378961149355)
XLA Ops:
  0.6 2.2 %drift.5 = (f32[2,352,256]{2,1,0:T(8,128)S(1)}, f32[2,336,256]{2,1,0:T(8,128)S(1)}, f32[2,336,256]{2,1,0:T(8,128)S(1)}) custom-call(f32[1024,2048]{1,0:T(8,128)} %bitcast.42, bf16[1024,2048]{1,0:T(8,128)(2,1)} %bitcast.47), custom_call_target="tpu_custom_call" | custom-call | flops 540672 | bytes 5406720 | tf_op jit(solution)/shard_map/drift/pallas_call | solution.py:110
  2.9 3.3 %collective-permute-start.9 = (f32[2,336,256]{2,1,0:T(8,128)S(1)}, f32[2,336,256]{2,1,0:T(8,128)S(1)}, u32[]{:S(2)}, u32[]{:S(2)}) collective-permute-start(f32[2,336,256]{2,1,0:T(8,128)S(1)} %get-tuple-element.34), channel_id=1, source_target_pairs={{0,64},{16,80},{32,96},{48,112},{64,0},{80,16},{96,32},{112,48},{1... | collective-permute-start | bytes 2064392 | tf_op jit(solution)/shard_map/ppermute | solution.py:26
  6.1 0.5 collective-permute-start.5
  6.7 1.1 collective-permute-start.1
  7.8 2.2 %drift.4 = (f32[2,352,256]{2,1,0:T(8,128)S(1)}, f32[2,336,256]{2,1,0:T(8,128)S(1)}, f32[2,336,256]{2,1,0:T(8,128)S(1)}) custom-call(f32[1024,2048]{1,0:T(8,128)} %bitcast.43, bf16[1024,2048]{1,0:T(8,128)(2,1)} %bitcast.48), custom_call_target="tpu_custom_call" | custom-call | flops 540672 | bytes 5406720 | tf_op jit(solution)/shard_map/drift/pallas_call | solution.py:110
  10.0 2.2 %collective-permute-start.4 = (f32[2,336,256]{2,1,0:T(8,128)S(1)}, f32[2,336,256]{2,1,0:T(8,128)S(1)}, u32[]{:S(2)}, u32[]{:S(2)}) collective-permute-start(f32[2,336,256]{2,1,0:T(8,128)S(1)} %get-tuple-element.30), channel_id=1, source_target_pairs={{0,48},{16,32},{32,16},{48,0},{64,112},{80,96},{96,80},{112,64},{1... | collective-permute-start | bytes 2064392 | tf_op jit(solution)/shard_map/ppermute | solution.py:26
  12.3 0.3 collective-permute-start.8
  12.6 3.4 %drift.3 = (f32[4,352,256]{2,1,0:T(8,128)S(1)}, f32[4,336,256]{2,1,0:T(8,128)S(1)}, f32[4,336,256]{2,1,0:T(8,128)S(1)}) custom-call(f32[1024,2048]{1,0:T(8,128)} %bitcast.44, bf16[1024,2048]{1,0:T(8,128)(2,1)} %bitcast.49), custom_call_target="tpu_custom_call" | custom-call | flops 1081344 | bytes 10813440 | tf_op jit(solution)/shard_map/drift/pallas_call | solution.py:110
  16.0 6.8 %collective-permute-done.9 = f32[2,336,256]{2,1,0:T(8,128)S(1)} collective-permute-done((f32[2,336,256]{2,1,0:T(8,128)S(1)}, f32[2,336,256]{2,1,0:T(8,128)S(1)}, u32[]{:S(2)}, u32[]{:S(2)}) %collective-permute-start.9) | collective-permute-done | bytes 688160 | tf_op jit(solution)/shard_map/ppermute | solution.py:26
  22.8 1.2 collective-permute-start
  24.1 0.4 collective-permute-done.5
  24.5 2.4 %collective-permute-start.10 = (f32[2,336,256]{2,1,0:T(8,128)S(1)}, f32[2,336,256]{2,1,0:T(8,128)S(1)}, u32[]{:S(2)}, u32[]{:S(2)}) collective-permute-start(f32[2,336,256]{2,1,0:T(8,128)S(1)} %slice_add_fusion.1), channel_id=1, source_target_pairs={{0,16},{16,0},{32,48},{48,32},{64,80},{80,64},{96,112},{112,96},{1... | collective-permute-start | bytes 2064392 | tf_op jit(solution)/shard_map/ppermute | solution.py:26
  27.0 1.3 collective-permute-start.6
  28.4 0.1 slice_add_fusion
  28.4 9.1 %collective-permute-done.8 = f32[2,336,256]{2,1,0:T(8,128)S(1)} collective-permute-done((f32[2,336,256]{2,1,0:T(8,128)S(1)}, f32[2,336,256]{2,1,0:T(8,128)S(1)}, u32[]{:S(2)}, u32[]{:S(2)}) %collective-permute-start.8) | collective-permute-done | bytes 688160 | tf_op jit(solution)/shard_map/ppermute | solution.py:26
  37.5 0.5 collective-permute-start.2
  38.0 16.1 %collective-permute-done.10 = f32[2,336,256]{2,1,0:T(8,128)S(1)} collective-permute-done((f32[2,336,256]{2,1,0:T(8,128)S(1)}, f32[2,336,256]{2,1,0:T(8,128)S(1)}, u32[]{:S(2)}, u32[]{:S(2)}) %collective-permute-start.10) | collective-permute-done | bytes 688160 | tf_op jit(solution)/shard_map/ppermute | solution.py:26
  54.3 1.6 %collective-permute-start.11 = (f32[336,256]{1,0:T(8,128)S(1)}, f32[336,256]{1,0:T(8,128)S(1)}, u32[]{:S(2)}, u32[]{:S(2)}) collective-permute-start(f32[336,256]{1,0:T(8,128)S(1)} %fusion.3), channel_id=1, source_target_pairs={{0,48},{16,32},{32,16},{48,0},{64,112},{80,96},{96,80},{112,64},{1... | collective-permute-start | bytes 1032200 | tf_op jit(solution)/shard_map/ppermute | solution.py:26
  56.0 2.4 %collective-permute-start.7 = (f32[336,256]{1,0:T(8,128)S(1)}, f32[336,256]{1,0:T(8,128)S(1)}, u32[]{:S(2)}, u32[]{:S(2)}) collective-permute-start(f32[336,256]{1,0:T(8,128)S(1)} %fusion.6), channel_id=1, source_target_pairs={{0,16},{16,0},{32,48},{48,32},{64,80},{80,64},{96,112},{112,96},{1... | collective-permute-start | bytes 1032200 | tf_op jit(solution)/shard_map/ppermute | solution.py:26
  58.5 0.5 collective-permute-start.3
  58.9 3.6 %collective-permute-done.11 = f32[336,256]{1,0:T(8,128)S(1)} collective-permute-done((f32[336,256]{1,0:T(8,128)S(1)}, f32[336,256]{1,0:T(8,128)S(1)}, u32[]{:S(2)}, u32[]{:S(2)}) %collective-permute-start.11) | collective-permute-done | bytes 344096 | tf_op jit(solution)/shard_map/ppermute | solution.py:26
  62.5 0.1 multiply_reduce_fusion.1
  62.6 2.1 %collective-permute-done.7 = f32[336,256]{1,0:T(8,128)S(1)} collective-permute-done((f32[336,256]{1,0:T(8,128)S(1)}, f32[336,256]{1,0:T(8,128)S(1)}, u32[]{:S(2)}, u32[]{:S(2)}) %collective-permute-start.7) | collective-permute-done | bytes 344096 | tf_op jit(solution)/shard_map/ppermute | solution.py:26
  64.7 0.1 multiply_reduce_fusion.2
  64.8 3.4 %collective-permute-done.3 = f32[352,256]{1,0:T(8,128)S(1)} collective-permute-done((f32[352,256]{1,0:T(8,128)S(1)}, f32[352,256]{1,0:T(8,128)S(1)}, u32[]{:S(2)}, u32[]{:S(2)}) %collective-permute-start.3) | collective-permute-done | bytes 360480 | tf_op jit(solution)/shard_map/ppermute | solution.py:26
  68.2 0.1 multiply_reduce_fusion
  68.3 0.4 collective-permute-start.13
  68.7 3.1 %collective-permute-start.14 = (f32[8,128]{1,0:T(8,128)S(1)}, f32[8,128]{1,0:T(8,128)S(1)}, u32[]{:S(2)}, u32[]{:S(2)}) collective-permute-start(f32[8,128]{1,0:T(8,128)S(1)} %broadcast_in_dim.4), channel_id=1, source_target_pairs={{0,72},{1,73},{2,74},{3,75},{4,76},{5,77},{6,78},{7,79},{8,64},{9,... | collective-permute-start | bytes 12296 | tf_op jit(solution)/shard_map/ppermute | solution.py:31
  71.7 0.1 collective-permute-start.12
  71.9 1.7 %collective-permute-done.13 = f32[8,128]{1,0:T(8,128)S(1)} collective-permute-done((f32[8,128]{1,0:T(8,128)S(1)}, f32[8,128]{1,0:T(8,128)S(1)}, u32[]{:S(2)}, u32[]{:S(2)}) %collective-permute-start.13) | collective-permute-done | bytes 4128 | tf_op jit(solution)/shard_map/ppermute | solution.py:31
  73.5 1.8 %collective-permute-done.12 = f32[8,128]{1,0:T(8,128)S(1)} collective-permute-done((f32[8,128]{1,0:T(8,128)S(1)}, f32[8,128]{1,0:T(8,128)S(1)}, u32[]{:S(2)}, u32[]{:S(2)}) %collective-permute-start.12) | collective-permute-done | bytes 4128 | tf_op jit(solution)/shard_map/ppermute | solution.py:31
  75.3 0.4 collective-permute-start.21
  75.7 1.9 %collective-permute-start.15 = (f32[8,128]{1,0:T(8,128)S(1)}, f32[8,128]{1,0:T(8,128)S(1)}, u32[]{:S(2)}, u32[]{:S(2)}) collective-permute-start(f32[8,128]{1,0:T(8,128)S(1)} %add_add_fusion), channel_id=1, source_target_pairs={{0,2},{1,3},{2,0},{3,1},{4,6},{5,7},{6,4},{7,5},{8,10},{9,11},{10,... | collective-permute-start | bytes 12296 | tf_op jit(solution)/shard_map/ppermute | solution.py:26
  77.6 1.7 %collective-permute-done.15 = f32[8,128]{1,0:T(8,128)S(1)} collective-permute-done((f32[8,128]{1,0:T(8,128)S(1)}, f32[8,128]{1,0:T(8,128)S(1)}, u32[]{:S(2)}, u32[]{:S(2)}) %collective-permute-start.15) | collective-permute-done | bytes 4128 | tf_op jit(solution)/shard_map/ppermute | solution.py:26
  79.3 4.0 %collective-permute-start.16 = (f32[8,128]{1,0:T(8,128)S(1)}, f32[8,128]{1,0:T(8,128)S(1)}, u32[]{:S(2)}, u32[]{:S(2)}) collective-permute-start(f32[8,128]{1,0:T(8,128)S(1)} %add.169), channel_id=1, source_target_pairs={{0,6},{1,7},{2,4},{3,5},{4,2},{5,3},{6,0},{7,1},{8,14},{9,15},{10,... | collective-permute-start | bytes 12296 | tf_op jit(solution)/shard_map/ppermute | solution.py:26
  83.4 1.6 collective-permute-done.16
  85.0 1.2 collective-permute-done.17
  86.1 1.7 %collective-permute-start.18 = (f32[8,128]{1,0:T(8,128)S(1)}, f32[8,128]{1,0:T(8,128)S(1)}, u32[]{:S(2)}, u32[]{:S(2)}) collective-permute-start(f32[8,128]{1,0:T(8,128)S(1)} %add.171), channel_id=1, source_target_pairs={{0,48},{16,0},{32,16},{48,32},{64,112},{80,64},{96,80},{112,96},{1... | collective-permute-start | bytes 12296 | tf_op jit(solution)/shard_map/ppermute | solution.py:261
  87.8 1.9 %collective-permute-done.18 = f32[8,128]{1,0:T(8,128)S(1)} collective-permute-done((f32[8,128]{1,0:T(8,128)S(1)}, f32[8,128]{1,0:T(8,128)S(1)}, u32[]{:S(2)}, u32[]{:S(2)}) %collective-permute-start.18) | collective-permute-done | bytes 4128 | tf_op jit(solution)/shard_map/ppermute | solution.py:261
  89.7 1.7 %collective-permute-start.19 = (f32[8,128]{1,0:T(8,128)S(1)}, f32[8,128]{1,0:T(8,128)S(1)}, u32[]{:S(2)}, u32[]{:S(2)}) collective-permute-start(f32[8,128]{1,0:T(8,128)S(1)} %collective-permute-done.18), channel_id=1, source_target_pairs={{0,48},{16,0},{32,16},{48,32},{64,112},{80,64},{96,80},{112,96},{1... | collective-permute-start | bytes 12296 | tf_op jit(solution)/shard_map/ppermute | solution.py:261
  91.5 2.1 %collective-permute-done.19 = f32[8,128]{1,0:T(8,128)S(1)} collective-permute-done((f32[8,128]{1,0:T(8,128)S(1)}, f32[8,128]{1,0:T(8,128)S(1)}, u32[]{:S(2)}, u32[]{:S(2)}) %collective-permute-start.19) | collective-permute-done | bytes 4128 | tf_op jit(solution)/shard_map/ppermute | solution.py:261
  93.6 1.5 collective-permute-start.20
  95.1 3.3 %collective-permute-done.20 = f32[8,128]{1,0:T(8,128)S(1)} collective-permute-done((f32[8,128]{1,0:T(8,128)S(1)}, f32[8,128]{1,0:T(8,128)S(1)}, u32[]{:S(2)}, u32[]{:S(2)}) %collective-permute-start.20) | collective-permute-done | bytes 4128 | tf_op jit(solution)/shard_map/ppermute | solution.py:261
  98.4 0.1 add_reduce_fusion
  98.6 0.2 multiply_add_fusion.3
  98.7 3.3 %collective-permute-start.23 = (f32[336,256]{1,0:T(8,128)S(1)}, f32[336,256]{1,0:T(8,128)S(1)}, u32[]{:S(2)}, u32[]{:S(2)}) collective-permute-start(f32[336,256]{1,0:T(8,128)S(1)} %get-tuple-element.58.refs_2_), channel_id=1, source_target_pairs={{0,16},{16,0},{32,48},{48,32},{64,80},{80,64},{96,112},{112,96},{1... | collective-permute-start | bytes 1032200 | tf_op jit(solution)/shard_map/ppermute | solution.py:26
  102.1 2.3 %collective-permute-start.22 = (f32[352,256]{1,0:T(8,128)S(1)}, f32[352,256]{1,0:T(8,128)S(1)}, u32[]{:S(2)}, u32[]{:S(2)}) collective-permute-start(f32[352,256]{1,0:T(8,128)S(1)} %get-tuple-element.56.refs_1_), channel_id=1, source_target_pairs={{0,64},{16,80},{32,96},{48,112},{64,0},{80,16},{96,32},{112,48},{1... | collective-permute-start | bytes 1081352 | tf_op jit(solution)/shard_map/ppermute | solution.py:26
  104.5 2.8 %collective-permute-done.23.refs_5_.refs_4_ = f32[336,256]{1,0:T(8,128)S(1)} collective-permute-done((f32[336,256]{1,0:T(8,128)S(1)}, f32[336,256]{1,0:T(8,128)S(1)}, u32[]{:S(2)}, u32[]{:S(2)}) %collective-permute-start.23) | collective-permute-done | bytes 344096 | tf_op jit(solution)/shard_map/ppermute | solution.py:26
  107.3 2.3 %collective-permute-start.25 = (f32[2,336,256]{2,1,0:T(8,128)S(1)}, f32[2,336,256]{2,1,0:T(8,128)S(1)}, u32[]{:S(2)}, u32[]{:S(2)}) collective-permute-start(f32[2,336,256]{2,1,0:T(8,128)S(1)} %pad_maximum_fusion.2), channel_id=1, source_target_pairs={{0,64},{16,80},{32,96},{48,112},{64,0},{80,16},{96,32},{112,48},{1... | collective-permute-start | bytes 2064392 | tf_op jit(solution)/shard_map/ppermute | solution.py:26
  109.7 5.3 %collective-permute-done.22.refs_4_ = f32[352,256]{1,0:T(8,128)S(1)} collective-permute-done((f32[352,256]{1,0:T(8,128)S(1)}, f32[352,256]{1,0:T(8,128)S(1)}, u32[]{:S(2)}, u32[]{:S(2)}) %collective-permute-start.22) | collective-permute-done | bytes 360480 | tf_op jit(solution)/shard_map/ppermute | solution.py:26
  115.2 2.1 %collective-permute-start.31 = (f32[2,336,256]{2,1,0:T(8,128)S(1)}, f32[2,336,256]{2,1,0:T(8,128)S(1)}, u32[]{:S(2)}, u32[]{:S(2)}) collective-permute-start(f32[2,336,256]{2,1,0:T(8,128)S(1)} %pad_maximum_fusion.2), channel_id=1, source_target_pairs={{0,48},{16,32},{32,16},{48,0},{64,112},{80,96},{96,80},{112,64},{1... | collective-permute-start | bytes 2064392 | tf_op jit(solution)/shard_map/ppermute | solution.py:26
  117.3 2.5 %collective-permute-start.32 = (f32[2,352,256]{2,1,0:T(8,128)S(1)}, f32[2,352,256]{2,1,0:T(8,128)S(1)}, u32[]{:S(2)}, u32[]{:S(2)}) collective-permute-start(f32[2,352,256]{2,1,0:T(8,128)S(1)} %pad_maximum_fusion.1), channel_id=1, source_target_pairs={{0,16},{16,0},{32,48},{48,32},{64,80},{80,64},{96,112},{112,96},{1... | collective-permute-start | bytes 2162696 | tf_op jit(solution)/shard_map/ppermute | solution.py:26
  119.9 6.0 %collective-permute-done.25.refs_8_ = f32[2,336,256]{2,1,0:T(8,128)S(1)} collective-permute-done((f32[2,336,256]{2,1,0:T(8,128)S(1)}, f32[2,336,256]{2,1,0:T(8,128)S(1)}, u32[]{:S(2)}, u32[]{:S(2)}) %collective-permute-start.25) | collective-permute-done | bytes 688160 | tf_op jit(solution)/shard_map/ppermute | solution.py:26
  125.9 8.2 %collective-permute-done.26.refs_7_ = f32[2,352,256]{2,1,0:T(8,128)S(1)} collective-permute-done((f32[2,352,256]{2,1,0:T(8,128)S(1)}, f32[2,352,256]{2,1,0:T(8,128)S(1)}, u32[]{:S(2)}, u32[]{:S(2)}) %collective-permute-start.26) | collective-permute-done | bytes 720928 | tf_op jit(solution)/shard_map/ppermute | solution.py:26
  134.1 1.7 %collective-permute-start.33 = (f32[2,336,256]{2,1,0:T(8,128)S(1)}, f32[2,336,256]{2,1,0:T(8,128)S(1)}, u32[]{:S(2)}, u32[]{:S(2)}) collective-permute-start(f32[2,336,256]{2,1,0:T(8,128)S(1)} %pad_maximum_fusion.3), channel_id=1, source_target_pairs={{0,64},{16,80},{32,96},{48,112},{64,0},{80,16},{96,32},{112,48},{1... | collective-permute-start | bytes 2064392 | tf_op jit(solution)/shard_map/ppermute | solution.py:26
  135.8 1.8 %collective-permute-start.30 = (f32[2,336,256]{2,1,0:T(8,128)S(1)}, f32[2,336,256]{2,1,0:T(8,128)S(1)}, u32[]{:S(2)}, u32[]{:S(2)}) collective-permute-start(f32[2,336,256]{2,1,0:T(8,128)S(1)} %collective-permute-done.29.refs_9_), channel_id=1, source_target_pairs={{0,64},{16,80},{32,96},{48,112},{64,0},{80,16},{96,32},{112,48},{1... | collective-permute-start | bytes 2064392 | tf_op jit(solution)/shard_map/ppermute | solution.py:26
  137.7 8.4 %collective-permute-done.31.refs_11_.refs_5_ = f32[2,336,256]{2,1,0:T(8,128)S(1)} collective-permute-done((f32[2,336,256]{2,1,0:T(8,128)S(1)}, f32[2,336,256]{2,1,0:T(8,128)S(1)}, u32[]{:S(2)}, u32[]{:S(2)}) %collective-permute-start.31) | collective-permute-done | bytes 688160 | tf_op jit(solution)/shard_map/ppermute | solution.py:26
  146.1 1.0 pad_maximum_fusion
  147.2 0.5 collective-permute-done.32.refs_10_
  147.7 1.6 %collective-permute-done.33.refs_12_ = f32[2,336,256]{2,1,0:T(8,128)S(1)} collective-permute-done((f32[2,336,256]{2,1,0:T(8,128)S(1)}, f32[2,336,256]{2,1,0:T(8,128)S(1)}, u32[]{:S(2)}, u32[]{:S(2)}) %collective-permute-start.33) | collective-permute-done | bytes 688160 | tf_op jit(solution)/shard_map/ppermute | solution.py:26
  149.3 6.4 %apply.2 = (f32[1024,2048]{1,0:T(8,128)}, f32[1024,256]{1,0:T(8,128)}) custom-call(f32[1024,2048]{1,0:T(8,128)} %bitcast.45, f32[352,256]{1,0:T(8,128)S(1)} %get-tuple-element.56.refs_1_, f32[336,256]{1,0:T(8,128)S(1)} %get-tuple-element.58.refs_2_, f32[336,256]{1,0:T(8,128)S(1)} %get-tuple-element.61.refs_3_, ...), custom_call_target="tpu_custom_call" | custom-call | flops 1622016 | bytes 19464192 | tf_op jit(solution)/shard_map/apply/pallas_call | solution.py:202
  155.7 1.0 collective-permute-done.30.refs_3_
  156.6 0.4 collective-permute-done.28.refs_2_
  157.1 2.8 %apply.3 = (f32[1024,2048]{1,0:T(8,128)}, f32[1024,256]{1,0:T(8,128)}) custom-call(f32[1024,2048]{1,0:T(8,128)} %bitcast.46, f32[2,352,256]{2,1,0:T(8,128)S(1)} %collective-permute-done.27.refs_1_, f32[2,336,256]{2,1,0:T(8,128)S(1)} %collective-permute-done.28.refs_2_, ...), custom_call_target="tpu_custom_call", output_to_operand_aliasing={{0}: (7, {}), {1}: (8, {})} | custom-call | flops 540672 | bytes 6488064 | tf_op jit(solution)/shard_map/apply/pallas_call | solution.py:202
  (37 shorter events, 0.9 us)
Async XLA Ops:
  2.9 19.9 %collective-permute-start.9 = (f32[2,336,256]{2,1,0:T(8,128)S(1)}, f32[2,336,256]{2,1,0:T(8,128)S(1)}, u32[]{:S(2)}, u32[]{:S(2)}) collective-permute-start(f32[2,336,256]{2,1,0:T(8,128)S(1)} %get-tuple-element.34), channel_id=1, source_target_pairs={{0,64},{16,80},{32,96},{48,112},{64,0},{80,16},{96,32},{112,48},{1... | collective-permute-start | bytes 2064392 | tf_op jit(solution)/shard_map/ppermute | solution.py:26
  6.1 18.4 %collective-permute-start.5 = (f32[2,336,256]{2,1,0:T(8,128)S(1)}, f32[2,336,256]{2,1,0:T(8,128)S(1)}, u32[]{:S(2)}, u32[]{:S(2)}) collective-permute-start(f32[2,336,256]{2,1,0:T(8,128)S(1)} %get-tuple-element.31), channel_id=1, source_target_pairs={{0,48},{16,32},{32,16},{48,0},{64,112},{80,96},{96,80},{112,64},{1... | collective-permute-start | bytes 2064392 | tf_op jit(solution)/shard_map/ppermute | solution.py:26
  6.7 20.3 %collective-permute-start.1 = (f32[2,352,256]{2,1,0:T(8,128)S(1)}, f32[2,352,256]{2,1,0:T(8,128)S(1)}, u32[]{:S(2)}, u32[]{:S(2)}) collective-permute-start(f32[2,352,256]{2,1,0:T(8,128)S(1)} %get-tuple-element.28), channel_id=1, source_target_pairs={{0,16},{16,0},{32,48},{48,32},{64,80},{80,64},{96,112},{112,96},{1... | collective-permute-start | bytes 2162696 | tf_op jit(solution)/shard_map/ppermute | solution.py:26
  10.0 45.9 %collective-permute-start.4 = (f32[2,336,256]{2,1,0:T(8,128)S(1)}, f32[2,336,256]{2,1,0:T(8,128)S(1)}, u32[]{:S(2)}, u32[]{:S(2)}) collective-permute-start(f32[2,336,256]{2,1,0:T(8,128)S(1)} %get-tuple-element.30), channel_id=1, source_target_pairs={{0,48},{16,32},{32,16},{48,0},{64,112},{80,96},{96,80},{112,64},{1... | collective-permute-start | bytes 2064392 | tf_op jit(solution)/shard_map/ppermute | solution.py:26
  12.3 25.2 %collective-permute-start.8 = (f32[2,336,256]{2,1,0:T(8,128)S(1)}, f32[2,336,256]{2,1,0:T(8,128)S(1)}, u32[]{:S(2)}, u32[]{:S(2)}) collective-permute-start(f32[2,336,256]{2,1,0:T(8,128)S(1)} %get-tuple-element.33), channel_id=1, source_target_pairs={{0,64},{16,80},{32,96},{48,112},{64,0},{80,16},{96,32},{112,48},{1... | collective-permute-start | bytes 2064392 | tf_op jit(solution)/shard_map/ppermute | solution.py:26
  22.8 35.6 %collective-permute-start = (f32[2,352,256]{2,1,0:T(8,128)S(1)}, f32[2,352,256]{2,1,0:T(8,128)S(1)}, u32[]{:S(2)}, u32[]{:S(2)}) collective-permute-start(f32[2,352,256]{2,1,0:T(8,128)S(1)} %get-tuple-element.27), channel_id=1, source_target_pairs={{0,16},{16,0},{32,48},{48,32},{64,80},{80,64},{96,112},{112,96},{1... | collective-permute-start | bytes 2162696 | tf_op jit(solution)/shard_map/ppermute | solution.py:26
  24.5 29.7 %collective-permute-start.10 = (f32[2,336,256]{2,1,0:T(8,128)S(1)}, f32[2,336,256]{2,1,0:T(8,128)S(1)}, u32[]{:S(2)}, u32[]{:S(2)}) collective-permute-start(f32[2,336,256]{2,1,0:T(8,128)S(1)} %slice_add_fusion.1), channel_id=1, source_target_pairs={{0,16},{16,0},{32,48},{48,32},{64,80},{80,64},{96,112},{112,96},{1... | collective-permute-start | bytes 2064392 | tf_op jit(solution)/shard_map/ppermute | solution.py:26
  27.0 28.9 %collective-permute-start.6 = (f32[2,336,256]{2,1,0:T(8,128)S(1)}, f32[2,336,256]{2,1,0:T(8,128)S(1)}, u32[]{:S(2)}, u32[]{:S(2)}) collective-permute-start(f32[2,336,256]{2,1,0:T(8,128)S(1)} %slice_add_fusion.2), channel_id=1, source_target_pairs={{0,64},{16,80},{32,96},{48,112},{64,0},{80,16},{96,32},{112,48},{1... | collective-permute-start | bytes 2064392 | tf_op jit(solution)/shard_map/ppermute | solution.py:26
  37.5 20.9 %collective-permute-start.2 = (f32[2,352,256]{2,1,0:T(8,128)S(1)}, f32[2,352,256]{2,1,0:T(8,128)S(1)}, u32[]{:S(2)}, u32[]{:S(2)}) collective-permute-start(f32[2,352,256]{2,1,0:T(8,128)S(1)} %slice_add_fusion), channel_id=1, source_target_pairs={{0,48},{16,32},{32,16},{48,0},{64,112},{80,96},{96,80},{112,64},{1... | collective-permute-start | bytes 2162696 | tf_op jit(solution)/shard_map/ppermute | solution.py:26
  54.3 8.3 %collective-permute-start.11 = (f32[336,256]{1,0:T(8,128)S(1)}, f32[336,256]{1,0:T(8,128)S(1)}, u32[]{:S(2)}, u32[]{:S(2)}) collective-permute-start(f32[336,256]{1,0:T(8,128)S(1)} %fusion.3), channel_id=1, source_target_pairs={{0,48},{16,32},{32,16},{48,0},{64,112},{80,96},{96,80},{112,64},{1... | collective-permute-start | bytes 1032200 | tf_op jit(solution)/shard_map/ppermute | solution.py:26
  56.0 8.7 %collective-permute-start.7 = (f32[336,256]{1,0:T(8,128)S(1)}, f32[336,256]{1,0:T(8,128)S(1)}, u32[]{:S(2)}, u32[]{:S(2)}) collective-permute-start(f32[336,256]{1,0:T(8,128)S(1)} %fusion.6), channel_id=1, source_target_pairs={{0,16},{16,0},{32,48},{48,32},{64,80},{80,64},{96,112},{112,96},{1... | collective-permute-start | bytes 1032200 | tf_op jit(solution)/shard_map/ppermute | solution.py:26
  58.5 9.7 %collective-permute-start.3 = (f32[352,256]{1,0:T(8,128)S(1)}, f32[352,256]{1,0:T(8,128)S(1)}, u32[]{:S(2)}, u32[]{:S(2)}) collective-permute-start(f32[352,256]{1,0:T(8,128)S(1)} %fusion), channel_id=1, source_target_pairs={{0,64},{16,80},{32,96},{48,112},{64,0},{80,16},{96,32},{112,48},{1... | collective-permute-start | bytes 1081352 | tf_op jit(solution)/shard_map/ppermute | solution.py:26
  62.6 12.7 %copy-start = (f32[2,512,256]{2,1,0:T(8,128)S(1)}, f32[2,512,256]{2,1,0:T(8,128)}, u32[]{:S(2)}) copy-start(f32[2,512,256]{2,1,0:T(8,128)} %param.5) | copy-start | bytes 3145732
  68.3 5.2 %collective-permute-start.13 = (f32[8,128]{1,0:T(8,128)S(1)}, f32[8,128]{1,0:T(8,128)S(1)}, u32[]{:S(2)}, u32[]{:S(2)}) collective-permute-start(f32[8,128]{1,0:T(8,128)S(1)} %broadcast_in_dim.4), channel_id=1, source_target_pairs={{0,64},{1,65},{2,66},{3,67},{4,68},{5,69},{6,70},{7,71},{8,72},{9,... | collective-permute-start | bytes 12296 | tf_op jit(solution)/shard_map/ppermute | solution.py:31
  68.7 4.9 %collective-permute-start.14 = (f32[8,128]{1,0:T(8,128)S(1)}, f32[8,128]{1,0:T(8,128)S(1)}, u32[]{:S(2)}, u32[]{:S(2)}) collective-permute-start(f32[8,128]{1,0:T(8,128)S(1)} %broadcast_in_dim.4), channel_id=1, source_target_pairs={{0,72},{1,73},{2,74},{3,75},{4,76},{5,77},{6,78},{7,79},{8,64},{9,... | collective-permute-start | bytes 12296 | tf_op jit(solution)/shard_map/ppermute | solution.py:31
  71.7 3.6 %collective-permute-start.12 = (f32[8,128]{1,0:T(8,128)S(1)}, f32[8,128]{1,0:T(8,128)S(1)}, u32[]{:S(2)}, u32[]{:S(2)}) collective-permute-start(f32[8,128]{1,0:T(8,128)S(1)} %broadcast_in_dim.4), channel_id=1, source_target_pairs={{0,8},{1,9},{2,10},{3,11},{4,12},{5,13},{6,14},{7,15},{8,0},{9,1},... | collective-permute-start | bytes 12296 | tf_op jit(solution)/shard_map/ppermute | solution.py:31
  75.3 23.2 %collective-permute-start.21 = (f32[1024,256]{1,0:T(8,128)S(1)}, f32[1024,256]{1,0:T(8,128)S(1)}, u32[]{:S(2)}, u32[]{:S(2)}) collective-permute-start(f32[1024,256]{1,0:T(8,128)S(1)} %bitcast.52), channel_id=1, source_target_pairs={{0,16},{16,32},{32,48},{48,64},{64,80},{80,96},{96,112},{112,0},{1... | collective-permute-start | bytes 3145736 | tf_op jit(solution)/shard_map/ppermute | solution.py:256
  75.7 3.6 %collective-permute-start.15 = (f32[8,128]{1,0:T(8,128)S(1)}, f32[8,128]{1,0:T(8,128)S(1)}, u32[]{:S(2)}, u32[]{:S(2)}) collective-permute-start(f32[8,128]{1,0:T(8,128)S(1)} %add_add_fusion), channel_id=1, source_target_pairs={{0,2},{1,3},{2,0},{3,1},{4,6},{5,7},{6,4},{7,5},{8,10},{9,11},{10,... | collective-permute-start | bytes 12296 | tf_op jit(solution)/shard_map/ppermute | solution.py:26
  79.3 5.6 %collective-permute-start.16 = (f32[8,128]{1,0:T(8,128)S(1)}, f32[8,128]{1,0:T(8,128)S(1)}, u32[]{:S(2)}, u32[]{:S(2)}) collective-permute-start(f32[8,128]{1,0:T(8,128)S(1)} %add.169), channel_id=1, source_target_pairs={{0,6},{1,7},{2,4},{3,5},{4,2},{5,3},{6,0},{7,1},{8,14},{9,15},{10,... | collective-permute-start | bytes 12296 | tf_op jit(solution)/shard_map/ppermute | solution.py:26
  85.0 1.2 collective-permute-start.17
  86.1 3.6 %collective-permute-start.18 = (f32[8,128]{1,0:T(8,128)S(1)}, f32[8,128]{1,0:T(8,128)S(1)}, u32[]{:S(2)}, u32[]{:S(2)}) collective-permute-start(f32[8,128]{1,0:T(8,128)S(1)} %add.171), channel_id=1, source_target_pairs={{0,48},{16,0},{32,16},{48,32},{64,112},{80,64},{96,80},{112,96},{1... | collective-permute-start | bytes 12296 | tf_op jit(solution)/shard_map/ppermute | solution.py:261
  89.7 3.8 %collective-permute-start.19 = (f32[8,128]{1,0:T(8,128)S(1)}, f32[8,128]{1,0:T(8,128)S(1)}, u32[]{:S(2)}, u32[]{:S(2)}) collective-permute-start(f32[8,128]{1,0:T(8,128)S(1)} %collective-permute-done.18), channel_id=1, source_target_pairs={{0,48},{16,0},{32,16},{48,32},{64,112},{80,64},{96,80},{112,96},{1... | collective-permute-start | bytes 12296 | tf_op jit(solution)/shard_map/ppermute | solution.py:261
  93.6 4.8 %collective-permute-start.20 = (f32[8,128]{1,0:T(8,128)S(1)}, f32[8,128]{1,0:T(8,128)S(1)}, u32[]{:S(2)}, u32[]{:S(2)}) collective-permute-start(f32[8,128]{1,0:T(8,128)S(1)} %collective-permute-done.19), channel_id=1, source_target_pairs={{0,48},{16,0},{32,16},{48,32},{64,112},{80,64},{96,80},{112,96},{1... | collective-permute-start | bytes 12296 | tf_op jit(solution)/shard_map/ppermute | solution.py:261
  98.7 8.5 %collective-permute-start.23 = (f32[336,256]{1,0:T(8,128)S(1)}, f32[336,256]{1,0:T(8,128)S(1)}, u32[]{:S(2)}, u32[]{:S(2)}) collective-permute-start(f32[336,256]{1,0:T(8,128)S(1)} %get-tuple-element.58.refs_2_), channel_id=1, source_target_pairs={{0,16},{16,0},{32,48},{48,32},{64,80},{80,64},{96,112},{112,96},{1... | collective-permute-start | bytes 1032200 | tf_op jit(solution)/shard_map/ppermute | solution.py:26
  102.1 12.8 %collective-permute-start.22 = (f32[352,256]{1,0:T(8,128)S(1)}, f32[352,256]{1,0:T(8,128)S(1)}, u32[]{:S(2)}, u32[]{:S(2)}) collective-permute-start(f32[352,256]{1,0:T(8,128)S(1)} %get-tuple-element.56.refs_1_), channel_id=1, source_target_pairs={{0,64},{16,80},{32,96},{48,112},{64,0},{80,16},{96,32},{112,48},{1... | collective-permute-start | bytes 1081352 | tf_op jit(solution)/shard_map/ppermute | solution.py:26
  104.5 10.6 %collective-permute-start.24 = (f32[336,256]{1,0:T(8,128)S(1)}, f32[336,256]{1,0:T(8,128)S(1)}, u32[]{:S(2)}, u32[]{:S(2)}) collective-permute-start(f32[336,256]{1,0:T(8,128)S(1)} %get-tuple-element.61.refs_3_), channel_id=1, source_target_pairs={{0,48},{16,32},{32,16},{48,0},{64,112},{80,96},{96,80},{112,64},{1... | collective-permute-start | bytes 1032200 | tf_op jit(solution)/shard_map/ppermute | solution.py:26
  107.3 18.6 %collective-permute-start.25 = (f32[2,336,256]{2,1,0:T(8,128)S(1)}, f32[2,336,256]{2,1,0:T(8,128)S(1)}, u32[]{:S(2)}, u32[]{:S(2)}) collective-permute-start(f32[2,336,256]{2,1,0:T(8,128)S(1)} %pad_maximum_fusion.2), channel_id=1, source_target_pairs={{0,64},{16,80},{32,96},{48,112},{64,0},{80,16},{96,32},{112,48},{1... | collective-permute-start | bytes 2064392 | tf_op jit(solution)/shard_map/ppermute | solution.py:26
  115.0 19.2 %collective-permute-start.26 = (f32[2,352,256]{2,1,0:T(8,128)S(1)}, f32[2,352,256]{2,1,0:T(8,128)S(1)}, u32[]{:S(2)}, u32[]{:S(2)}) collective-permute-start(f32[2,352,256]{2,1,0:T(8,128)S(1)} %pad_maximum_fusion.1), channel_id=1, source_target_pairs={{0,48},{16,32},{32,16},{48,0},{64,112},{80,96},{96,80},{112,64},{1... | collective-permute-start | bytes 2162696 | tf_op jit(solution)/shard_map/ppermute | solution.py:26
  115.1 20.7 %collective-permute-start.29 = (f32[2,336,256]{2,1,0:T(8,128)S(1)}, f32[2,336,256]{2,1,0:T(8,128)S(1)}, u32[]{:S(2)}, u32[]{:S(2)}) collective-permute-start(f32[2,336,256]{2,1,0:T(8,128)S(1)} %pad_maximum_fusion.3), channel_id=1, source_target_pairs={{0,16},{16,0},{32,48},{48,32},{64,80},{80,64},{96,112},{112,96},{1... | collective-permute-start | bytes 2064392 | tf_op jit(solution)/shard_map/ppermute | solution.py:26
  115.2 30.9 %collective-permute-start.31 = (f32[2,336,256]{2,1,0:T(8,128)S(1)}, f32[2,336,256]{2,1,0:T(8,128)S(1)}, u32[]{:S(2)}, u32[]{:S(2)}) collective-permute-start(f32[2,336,256]{2,1,0:T(8,128)S(1)} %pad_maximum_fusion.2), channel_id=1, source_target_pairs={{0,48},{16,32},{32,16},{48,0},{64,112},{80,96},{96,80},{112,64},{1... | collective-permute-start | bytes 2064392 | tf_op jit(solution)/shard_map/ppermute | solution.py:26
  117.3 30.4 %collective-permute-start.32 = (f32[2,352,256]{2,1,0:T(8,128)S(1)}, f32[2,352,256]{2,1,0:T(8,128)S(1)}, u32[]{:S(2)}, u32[]{:S(2)}) collective-permute-start(f32[2,352,256]{2,1,0:T(8,128)S(1)} %pad_maximum_fusion.1), channel_id=1, source_target_pairs={{0,16},{16,0},{32,48},{48,32},{64,80},{80,64},{96,112},{112,96},{1... | collective-permute-start | bytes 2162696 | tf_op jit(solution)/shard_map/ppermute | solution.py:26
  134.1 22.9 %collective-permute-start.27 = (f32[2,352,256]{2,1,0:T(8,128)S(1)}, f32[2,352,256]{2,1,0:T(8,128)S(1)}, u32[]{:S(2)}, u32[]{:S(2)}) collective-permute-start(f32[2,352,256]{2,1,0:T(8,128)S(1)} %collective-permute-done.26.refs_7_), channel_id=1, source_target_pairs={{0,16},{16,0},{32,48},{48,32},{64,80},{80,64},{96,112},{112,96},{1... | collective-permute-start | bytes 2162696 | tf_op jit(solution)/shard_map/ppermute | solution.py:26
  134.1 15.1 %collective-permute-start.33 = (f32[2,336,256]{2,1,0:T(8,128)S(1)}, f32[2,336,256]{2,1,0:T(8,128)S(1)}, u32[]{:S(2)}, u32[]{:S(2)}) collective-permute-start(f32[2,336,256]{2,1,0:T(8,128)S(1)} %pad_maximum_fusion.3), channel_id=1, source_target_pairs={{0,64},{16,80},{32,96},{48,112},{64,0},{80,16},{96,32},{112,48},{1... | collective-permute-start | bytes 2064392 | tf_op jit(solution)/shard_map/ppermute | solution.py:26
  135.8 20.8 %collective-permute-start.30 = (f32[2,336,256]{2,1,0:T(8,128)S(1)}, f32[2,336,256]{2,1,0:T(8,128)S(1)}, u32[]{:S(2)}, u32[]{:S(2)}) collective-permute-start(f32[2,336,256]{2,1,0:T(8,128)S(1)} %collective-permute-done.29.refs_9_), channel_id=1, source_target_pairs={{0,64},{16,80},{32,96},{48,112},{64,0},{80,16},{96,32},{112,48},{1... | collective-permute-start | bytes 2064392 | tf_op jit(solution)/shard_map/ppermute | solution.py:26
  146.1 10.9 %collective-permute-start.28 = (f32[2,336,256]{2,1,0:T(8,128)S(1)}, f32[2,336,256]{2,1,0:T(8,128)S(1)}, u32[]{:S(2)}, u32[]{:S(2)}) collective-permute-start(f32[2,336,256]{2,1,0:T(8,128)S(1)} %collective-permute-done.25.refs_8_), channel_id=1, source_target_pairs={{0,48},{16,32},{32,16},{48,0},{64,112},{80,96},{96,80},{112,64},{1... | collective-permute-start | bytes 2064392 | tf_op jit(solution)/shard_map/ppermute | solution.py:26

commit v6 on v5

--- a/solution.py
+++ b/solution.py
@@ -55,8 +55,8 @@
     return flip_of(ORDERS[k], bits)
 
 
-FIRST = ((1, 1, 0), (1, 1, 1))
-SECOND = ((1, 0, 0), (1, 0, 1))
+FIRST = ((1, 1, 0), (1, 1, 1), (1, 0, 1))
+SECOND = ((1, 0, 0),)
 KEPT = ((0, 0, 0), (0, 0, 1), (0, 1, 0), (0, 1, 1))
 
 
@@ -239,14 +239,13 @@
 
     (first,) = drift(g, r, spans, block_cols, [FIRST])
     got1 = [cross(k, 0, first[k]) for k in parts]
-    (second,) = drift(g, r, spans, block_cols, [SECOND])
-    got2 = [cross(k, 0, second[k]) for k in parts]
-    (kept,) = drift(g, r, spans, block_cols, [KEPT])
-    third = [kept[k][2:] + got1[k] for k in parts]
+    second, kept = drift(g, r, spans, block_cols, [SECOND, KEPT])
+    third = [kept[k][2:] + got1[k][:2] for k in parts]
     got3 = [cross(k, 1, third[k]) for k in parts]
-    fourth = [kept[k][1] + got2[k][1] + got3[k][1] for k in parts]
+    got2 = [cross(k, 0, second[k][0]) for k in parts]
+    fourth = [kept[k][1] + got1[k][2] + got3[k][1] for k in parts]
     got4 = [cross(k, 2, fourth[k]) for k in parts]
-    grads = [(kept[k][0] + got2[k][0] + got3[k][0] + got4[k]) / replicas for k in parts]
+    grads = [(kept[k][0] + got2[k] + got3[k][0] + got4[k]) / replicas for k in parts]
 
     squares = sum(jnp.sum(p * p, axis=0) for p in grads)
     squares = jnp.broadcast_to(squares[:128] + squares[128:], (8, 128))

time: 160 us -> 160 us (level)
    ppermute x3, waiting for transfers between devices: 7.31 us -> 11.5 us  [per_device(): lax.ppermute(around[-1], 'replica', [(i, i // 4 * 4 + (i + 3) % 4) for i...]
    ppermute x3, starting transfers between devices: 4.93 us -> 1.36 us  [per_device(): lax.ppermute(around[-1], 'replica', [(i, i // 4 * 4 + (i + 3) % 4) for i...]
    ppermute x27, waiting for transfers between devices: 80.2 us -> 77 us  [exchange(): return lax.ppermute(value, axis, [(i, i ^ flip) for i in range(size)])]
    ppermute x27, starting transfers between devices: 39.8 us -> 41.6 us  [exchange(): return lax.ppermute(value, axis, [(i, i ^ flip) for i in range(size)])]
    pallas_call x3 -> x2, Pallas kernels: 7.81 us -> 7.08 us  [drift(): pl.pallas_call(functools.partial(drift_kernel, spans, block_cols, items,...]
  transfers between devices with their start and end apart: 34 -> 34, of which waited for: 24 -> 22; matrix products, arithmetic and copies ran while one was open for 1% -> 1% of each run, Pallas kernels for 7% -> 7%
where the time goes in v6:
time: 160 us
  waiting for transfers between devices  92.2 us (58%)
  starting transfers between devices  48.3 us (30%)
  Pallas kernels  16.3 us (10%)
  other arithmetic  2.39 us (1%)
    ppermute x27, waiting for transfers between devices, exchange(): return lax.ppermute(value, axis, [(i, i ^ flip) for i in range(size)])  77 us
    ppermute x27, starting transfers between devices, exchange(): return lax.ppermute(value, axis, [(i, i ^ flip) for i in range(size)])  41.6 us
    ppermute x3, waiting for transfers between devices, per_device(): lax.ppermute(around[-1], 'replica', [(i, i // 4 * 4 + (i + 3) % 4) for i...  11.5 us
    pallas_call x2, Pallas kernels, apply(): pl.pallas_call(functools.partial(apply_kernel, spans, block_cols, items,...  9.23 us
    pallas_call x2, Pallas kernels, drift(): pl.pallas_call(functools.partial(drift_kernel, spans, block_cols, items,...  7.08 us
    ppermute x3, starting transfers between devices, exchange_two(): return lax.ppermute(value, ('replica', 'shard'), pairs)  3.98 us
    ppermute x3, waiting for transfers between devices, exchange_two(): return lax.ppermute(value, ('replica', 'shard'), pairs)  3.73 us
  transfers between devices with their start and end apart: 34, of which 22 were waited for; matrix products, arithmetic and copies ran while one was open for 1% of the time, Pallas kernels for 7%

profile of v6, /device:TPU:4, one launch (start us, length us, event | category | flops | bytes accessed | tf_op | source)
XLA Modules:
  0.0 160.3 jit_solution(11574310675701997141)
XLA Ops:
  0.6 2.9 %drift.3 = (f32[3,352,256]{2,1,0:T(8,128)S(1)}, f32[3,336,256]{2,1,0:T(8,128)S(1)}, f32[3,336,256]{2,1,0:T(8,128)S(1)}) custom-call(f32[1024,2048]{1,0:T(8,128)} %bitcast.69, bf16[1024,2048]{1,0:T(8,128)(2,1)} %bitcast.73), custom_call_target="tpu_custom_call" | custom-call | flops 811008 | bytes 8110080 | tf_op jit(solution)/shard_map/drift/pallas_call | solution.py:110
  3.5 3.3 %collective-permute-start.9 = (f32[3,336,256]{2,1,0:T(8,128)S(1)}, f32[3,336,256]{2,1,0:T(8,128)S(1)}, u32[]{:S(2)}, u32[]{:S(2)}) collective-permute-start(f32[3,336,256]{2,1,0:T(8,128)S(1)} %get-tuple-element.34), channel_id=1, source_target_pairs={{0,64},{16,80},{32,96},{48,112},{64,0},{80,16},{96,32},{112,48},{1... | collective-permute-start | bytes 3096584 | tf_op jit(solution)/shard_map/ppermute | solution.py:26
  6.8 0.5 collective-permute-start.5
  7.3 1.1 collective-permute-start.1
  8.4 4.2 %drift.2 = (f32[1,352,256]{2,1,0:T(8,128)S(1)}, f32[1,336,256]{2,1,0:T(8,128)S(1)}, f32[1,336,256]{2,1,0:T(8,128)S(1)}, f32[4,352,256]{2,1,0:T(8,128)S(1)}, f32[...) custom-call(f32[1024,2048]{1,0:T(8,128)} %bitcast.70, bf16[1024,2048]{1,0:T(8,128)(2,1)} %bitcast.74), custom_call_target="tpu_custom_call" | custom-call | flops 1351680 | bytes 13516800 | tf_op jit(solution)/shard_map/drift/pallas_call | solution.py:110
  12.7 17.0 %collective-permute-done.9 = f32[3,336,256]{2,1,0:T(8,128)S(1)} collective-permute-done((f32[3,336,256]{2,1,0:T(8,128)S(1)}, f32[3,336,256]{2,1,0:T(8,128)S(1)}, u32[]{:S(2)}, u32[]{:S(2)}) %collective-permute-start.9) | collective-permute-done | bytes 1032224 | tf_op jit(solution)/shard_map/ppermute | solution.py:26
  29.6 0.1 slice_add_fusion.1
  29.7 1.3 collective-permute-start.10
  31.0 0.1 slice_add_fusion.2
  31.1 3.3 %collective-permute-start.6 = (f32[2,336,256]{2,1,0:T(8,128)S(1)}, f32[2,336,256]{2,1,0:T(8,128)S(1)}, u32[]{:S(2)}, u32[]{:S(2)}) collective-permute-start(f32[2,336,256]{2,1,0:T(8,128)S(1)} %slice_add_fusion.2), channel_id=1, source_target_pairs={{0,64},{16,80},{32,96},{48,112},{64,0},{80,16},{96,32},{112,48},{1... | collective-permute-start | bytes 2064392 | tf_op jit(solution)/shard_map/ppermute | solution.py:26
  34.4 0.1 slice_add_fusion
  34.5 1.3 collective-permute-start.2
  35.8 0.8 collective-permute-start.4
  36.6 0.3 collective-permute-start.8
  36.9 10.1 %collective-permute-done.10 = f32[2,336,256]{2,1,0:T(8,128)S(1)} collective-permute-done((f32[2,336,256]{2,1,0:T(8,128)S(1)}, f32[2,336,256]{2,1,0:T(8,128)S(1)}, u32[]{:S(2)}, u32[]{:S(2)}) %collective-permute-start.10) | collective-permute-done | bytes 688160 | tf_op jit(solution)/shard_map/ppermute | solution.py:26
  47.1 1.1 collective-permute-start
  48.3 2.8 %collective-permute-done.6 = f32[2,336,256]{2,1,0:T(8,128)S(1)} collective-permute-done((f32[2,336,256]{2,1,0:T(8,128)S(1)}, f32[2,336,256]{2,1,0:T(8,128)S(1)}, u32[]{:S(2)}, u32[]{:S(2)}) %collective-permute-start.6) | collective-permute-done | bytes 688160 | tf_op jit(solution)/shard_map/ppermute | solution.py:26
  51.1 0.5 collective-permute-start.11
  51.7 2.0 %collective-permute-done.2 = f32[2,352,256]{2,1,0:T(8,128)S(1)} collective-permute-done((f32[2,352,256]{2,1,0:T(8,128)S(1)}, f32[2,352,256]{2,1,0:T(8,128)S(1)}, u32[]{:S(2)}, u32[]{:S(2)}) %collective-permute-start.2) | collective-permute-done | bytes 720928 | tf_op jit(solution)/shard_map/ppermute | solution.py:26
  53.6 2.0 %collective-permute-start.7 = (f32[336,256]{1,0:T(8,128)S(1)}, f32[336,256]{1,0:T(8,128)S(1)}, u32[]{:S(2)}, u32[]{:S(2)}) collective-permute-start(f32[336,256]{1,0:T(8,128)S(1)} %fusion.6), channel_id=1, source_target_pairs={{0,16},{16,0},{32,48},{48,32},{64,80},{80,64},{96,112},{112,96},{1... | collective-permute-start | bytes 1032200 | tf_op jit(solution)/shard_map/ppermute | solution.py:26
  55.7 0.3 collective-permute-done.8
  56.1 3.2 %collective-permute-start.3 = (f32[352,256]{1,0:T(8,128)S(1)}, f32[352,256]{1,0:T(8,128)S(1)}, u32[]{:S(2)}, u32[]{:S(2)}) collective-permute-start(f32[352,256]{1,0:T(8,128)S(1)} %fusion), channel_id=1, source_target_pairs={{0,64},{16,80},{32,96},{48,112},{64,0},{80,16},{96,32},{112,48},{1... | collective-permute-start | bytes 1081352 | tf_op jit(solution)/shard_map/ppermute | solution.py:26
  59.3 6.5 %collective-permute-done.11 = f32[336,256]{1,0:T(8,128)S(1)} collective-permute-done((f32[336,256]{1,0:T(8,128)S(1)}, f32[336,256]{1,0:T(8,128)S(1)}, u32[]{:S(2)}, u32[]{:S(2)}) %collective-permute-start.11) | collective-permute-done | bytes 344096 | tf_op jit(solution)/shard_map/ppermute | solution.py:26
  65.7 0.1 multiply_reduce_fusion.1
  65.9 0.1 multiply_reduce_fusion.2
  66.0 0.1 multiply_reduce_fusion
  66.1 2.9 %collective-permute-start.13 = (f32[8,128]{1,0:T(8,128)S(1)}, f32[8,128]{1,0:T(8,128)S(1)}, u32[]{:S(2)}, u32[]{:S(2)}) collective-permute-start(f32[8,128]{1,0:T(8,128)S(1)} %broadcast_in_dim.4), channel_id=1, source_target_pairs={{0,64},{1,65},{2,66},{3,67},{4,68},{5,69},{6,70},{7,71},{8,72},{9,... | collective-permute-start | bytes 12296 | tf_op jit(solution)/shard_map/ppermute | solution.py:31
  69.0 1.1 collective-permute-start.14
  70.1 1.2 collective-permute-done.13
  71.3 2.5 %collective-permute-done.14 = f32[8,128]{1,0:T(8,128)S(1)} collective-permute-done((f32[8,128]{1,0:T(8,128)S(1)}, f32[8,128]{1,0:T(8,128)S(1)}, u32[]{:S(2)}, u32[]{:S(2)}) %collective-permute-start.14) | collective-permute-done | bytes 4128 | tf_op jit(solution)/shard_map/ppermute | solution.py:31
  73.9 1.4 collective-permute-start.21
  75.3 1.9 %collective-permute-start.15 = (f32[8,128]{1,0:T(8,128)S(1)}, f32[8,128]{1,0:T(8,128)S(1)}, u32[]{:S(2)}, u32[]{:S(2)}) collective-permute-start(f32[8,128]{1,0:T(8,128)S(1)} %add_add_fusion), channel_id=1, source_target_pairs={{0,2},{1,3},{2,0},{3,1},{4,6},{5,7},{6,4},{7,5},{8,10},{9,11},{10,... | collective-permute-start | bytes 12296 | tf_op jit(solution)/shard_map/ppermute | solution.py:26
  77.2 1.7 %collective-permute-done.15 = f32[8,128]{1,0:T(8,128)S(1)} collective-permute-done((f32[8,128]{1,0:T(8,128)S(1)}, f32[8,128]{1,0:T(8,128)S(1)}, u32[]{:S(2)}, u32[]{:S(2)}) %collective-permute-start.15) | collective-permute-done | bytes 4128 | tf_op jit(solution)/shard_map/ppermute | solution.py:26
  78.9 4.0 %collective-permute-start.16 = (f32[8,128]{1,0:T(8,128)S(1)}, f32[8,128]{1,0:T(8,128)S(1)}, u32[]{:S(2)}, u32[]{:S(2)}) collective-permute-start(f32[8,128]{1,0:T(8,128)S(1)} %add.154), channel_id=1, source_target_pairs={{0,6},{1,7},{2,4},{3,5},{4,2},{5,3},{6,0},{7,1},{8,14},{9,15},{10,... | collective-permute-start | bytes 12296 | tf_op jit(solution)/shard_map/ppermute | solution.py:26
  82.9 1.6 collective-permute-done.16
  84.5 1.2 collective-permute-done.17
  85.7 0.7 collective-permute-start.18
  86.4 2.9 %collective-permute-done.18 = f32[8,128]{1,0:T(8,128)S(1)} collective-permute-done((f32[8,128]{1,0:T(8,128)S(1)}, f32[8,128]{1,0:T(8,128)S(1)}, u32[]{:S(2)}, u32[]{:S(2)}) %collective-permute-start.18) | collective-permute-done | bytes 4128 | tf_op jit(solution)/shard_map/ppermute | solution.py:260
  89.3 0.7 collective-permute-start.19
  90.0 3.7 %collective-permute-done.19 = f32[8,128]{1,0:T(8,128)S(1)} collective-permute-done((f32[8,128]{1,0:T(8,128)S(1)}, f32[8,128]{1,0:T(8,128)S(1)}, u32[]{:S(2)}, u32[]{:S(2)}) %collective-permute-start.19) | collective-permute-done | bytes 4128 | tf_op jit(solution)/shard_map/ppermute | solution.py:260
  93.7 4.8 %collective-permute-done.20 = f32[8,128]{1,0:T(8,128)S(1)} collective-permute-done((f32[8,128]{1,0:T(8,128)S(1)}, f32[8,128]{1,0:T(8,128)S(1)}, u32[]{:S(2)}, u32[]{:S(2)}) %collective-permute-start.20) | collective-permute-done | bytes 4128 | tf_op jit(solution)/shard_map/ppermute | solution.py:260
  98.5 0.1 add_reduce_fusion
  98.7 0.2 multiply_add_fusion.3
  98.9 3.3 %collective-permute-start.23 = (f32[336,256]{1,0:T(8,128)S(1)}, f32[336,256]{1,0:T(8,128)S(1)}, u32[]{:S(2)}, u32[]{:S(2)}) collective-permute-start(f32[336,256]{1,0:T(8,128)S(1)} %get-tuple-element.58.refs_2_), channel_id=1, source_target_pairs={{0,16},{16,0},{32,48},{48,32},{64,80},{80,64},{96,112},{112,96},{1... | collective-permute-start | bytes 1032200 | tf_op jit(solution)/shard_map/ppermute | solution.py:26
  102.2 0.1 multiply_add_fusion
  102.3 2.6 %collective-permute-start.22 = (f32[352,256]{1,0:T(8,128)S(1)}, f32[352,256]{1,0:T(8,128)S(1)}, u32[]{:S(2)}, u32[]{:S(2)}) collective-permute-start(f32[352,256]{1,0:T(8,128)S(1)} %get-tuple-element.56.refs_1_), channel_id=1, source_target_pairs={{0,64},{16,80},{32,96},{48,112},{64,0},{80,16},{96,32},{112,48},{1... | collective-permute-start | bytes 1081352 | tf_op jit(solution)/shard_map/ppermute | solution.py:26
  104.9 2.6 %collective-permute-done.23.refs_5_.refs_4_ = f32[336,256]{1,0:T(8,128)S(1)} collective-permute-done((f32[336,256]{1,0:T(8,128)S(1)}, f32[336,256]{1,0:T(8,128)S(1)}, u32[]{:S(2)}, u32[]{:S(2)}) %collective-permute-start.23) | collective-permute-done | bytes 344096 | tf_op jit(solution)/shard_map/ppermute | solution.py:26
  107.5 2.6 %collective-permute-start.25 = (f32[2,336,256]{2,1,0:T(8,128)S(1)}, f32[2,336,256]{2,1,0:T(8,128)S(1)}, u32[]{:S(2)}, u32[]{:S(2)}) collective-permute-start(f32[2,336,256]{2,1,0:T(8,128)S(1)} %pad_maximum_fusion.2), channel_id=1, source_target_pairs={{0,64},{16,80},{32,96},{48,112},{64,0},{80,16},{96,32},{112,48},{1... | collective-permute-start | bytes 2064392 | tf_op jit(solution)/shard_map/ppermute | solution.py:26
  110.1 5.0 %collective-permute-done.22.refs_4_ = f32[352,256]{1,0:T(8,128)S(1)} collective-permute-done((f32[352,256]{1,0:T(8,128)S(1)}, f32[352,256]{1,0:T(8,128)S(1)}, u32[]{:S(2)}, u32[]{:S(2)}) %collective-permute-start.22) | collective-permute-done | bytes 360480 | tf_op jit(solution)/shard_map/ppermute | solution.py:26
  115.1 0.1 collective-permute-start.26
  115.3 0.2 collective-permute-start.29
  115.5 2.0 %collective-permute-start.31 = (f32[2,336,256]{2,1,0:T(8,128)S(1)}, f32[2,336,256]{2,1,0:T(8,128)S(1)}, u32[]{:S(2)}, u32[]{:S(2)}) collective-permute-start(f32[2,336,256]{2,1,0:T(8,128)S(1)} %pad_maximum_fusion.2), channel_id=1, source_target_pairs={{0,48},{16,32},{32,16},{48,0},{64,112},{80,96},{96,80},{112,64},{1... | collective-permute-start | bytes 2064392 | tf_op jit(solution)/shard_map/ppermute | solution.py:26
  117.5 2.5 %collective-permute-start.32 = (f32[2,352,256]{2,1,0:T(8,128)S(1)}, f32[2,352,256]{2,1,0:T(8,128)S(1)}, u32[]{:S(2)}, u32[]{:S(2)}) collective-permute-start(f32[2,352,256]{2,1,0:T(8,128)S(1)} %pad_maximum_fusion.1), channel_id=1, source_target_pairs={{0,16},{16,0},{32,48},{48,32},{64,80},{80,64},{96,112},{112,96},{1... | collective-permute-start | bytes 2162696 | tf_op jit(solution)/shard_map/ppermute | solution.py:26
  120.0 6.0 %collective-permute-done.25.refs_8_ = f32[2,336,256]{2,1,0:T(8,128)S(1)} collective-permute-done((f32[2,336,256]{2,1,0:T(8,128)S(1)}, f32[2,336,256]{2,1,0:T(8,128)S(1)}, u32[]{:S(2)}, u32[]{:S(2)}) %collective-permute-start.25) | collective-permute-done | bytes 688160 | tf_op jit(solution)/shard_map/ppermute | solution.py:26
  126.0 8.2 %collective-permute-done.26.refs_7_ = f32[2,352,256]{2,1,0:T(8,128)S(1)} collective-permute-done((f32[2,352,256]{2,1,0:T(8,128)S(1)}, f32[2,352,256]{2,1,0:T(8,128)S(1)}, u32[]{:S(2)}, u32[]{:S(2)}) %collective-permute-start.26) | collective-permute-done | bytes 720928 | tf_op jit(solution)/shard_map/ppermute | solution.py:26
  134.3 1.9 %collective-permute-start.33 = (f32[2,336,256]{2,1,0:T(8,128)S(1)}, f32[2,336,256]{2,1,0:T(8,128)S(1)}, u32[]{:S(2)}, u32[]{:S(2)}) collective-permute-start(f32[2,336,256]{2,1,0:T(8,128)S(1)} %pad_maximum_fusion.3), channel_id=1, source_target_pairs={{0,64},{16,80},{32,96},{48,112},{64,0},{80,16},{96,32},{112,48},{1... | collective-permute-start | bytes 2064392 | tf_op jit(solution)/shard_map/ppermute | solution.py:26
  136.2 1.6 collective-permute-start.30
  137.8 8.4 %collective-permute-done.31.refs_11_.refs_5_ = f32[2,336,256]{2,1,0:T(8,128)S(1)} collective-permute-done((f32[2,336,256]{2,1,0:T(8,128)S(1)}, f32[2,336,256]{2,1,0:T(8,128)S(1)}, u32[]{:S(2)}, u32[]{:S(2)}) %collective-permute-start.31) | collective-permute-done | bytes 688160 | tf_op jit(solution)/shard_map/ppermute | solution.py:26
  146.3 1.0 pad_maximum_fusion
  147.3 0.8 collective-permute-done.32.refs_10_
  148.1 1.8 %collective-permute-done.33.refs_12_ = f32[2,336,256]{2,1,0:T(8,128)S(1)} collective-permute-done((f32[2,336,256]{2,1,0:T(8,128)S(1)}, f32[2,336,256]{2,1,0:T(8,128)S(1)}, u32[]{:S(2)}, u32[]{:S(2)}) %collective-permute-start.33) | collective-permute-done | bytes 688160 | tf_op jit(solution)/shard_map/ppermute | solution.py:26
  149.9 6.4 %apply.2 = (f32[1024,2048]{1,0:T(8,128)}, f32[1024,256]{1,0:T(8,128)}) custom-call(f32[1024,2048]{1,0:T(8,128)} %bitcast.71, f32[352,256]{1,0:T(8,128)S(1)} %get-tuple-element.56.refs_1_, f32[336,256]{1,0:T(8,128)S(1)} %get-tuple-element.58.refs_2_, f32[336,256]{1,0:T(8,128)S(1)} %get-tuple-element.61.refs_3_, ...), custom_call_target="tpu_custom_call" | custom-call | flops 1622016 | bytes 19464192 | tf_op jit(solution)/shard_map/apply/pallas_call | solution.py:202
  156.3 1.0 collective-permute-done.30.refs_3_
  157.3 2.8 %apply.3 = (f32[1024,2048]{1,0:T(8,128)}, f32[1024,256]{1,0:T(8,128)}) custom-call(f32[1024,2048]{1,0:T(8,128)} %bitcast.72, f32[2,352,256]{2,1,0:T(8,128)S(1)} %collective-permute-done.27.refs_1_, f32[2,336,256]{2,1,0:T(8,128)S(1)} %collective-permute-done.28.refs_2_, ...), custom_call_target="tpu_custom_call", output_to_operand_aliasing={{0}: (7, {}), {1}: (8, {})} | custom-call | flops 540672 | bytes 6488064 | tf_op jit(solution)/shard_map/apply/pallas_call | solution.py:202
  (36 shorter events, 0.5 us)
Async XLA Ops:
  3.5 26.1 %collective-permute-start.9 = (f32[3,336,256]{2,1,0:T(8,128)S(1)}, f32[3,336,256]{2,1,0:T(8,128)S(1)}, u32[]{:S(2)}, u32[]{:S(2)}) collective-permute-start(f32[3,336,256]{2,1,0:T(8,128)S(1)} %get-tuple-element.34), channel_id=1, source_target_pairs={{0,64},{16,80},{32,96},{48,112},{64,0},{80,16},{96,32},{112,48},{1... | collective-permute-start | bytes 3096584 | tf_op jit(solution)/shard_map/ppermute | solution.py:26
  6.8 24.3 %collective-permute-start.5 = (f32[3,336,256]{2,1,0:T(8,128)S(1)}, f32[3,336,256]{2,1,0:T(8,128)S(1)}, u32[]{:S(2)}, u32[]{:S(2)}) collective-permute-start(f32[3,336,256]{2,1,0:T(8,128)S(1)} %get-tuple-element.31), channel_id=1, source_target_pairs={{0,48},{16,32},{32,16},{48,0},{64,112},{80,96},{96,80},{112,64},{1... | collective-permute-start | bytes 3096584 | tf_op jit(solution)/shard_map/ppermute | solution.py:26
  7.3 27.1 %collective-permute-start.1 = (f32[3,352,256]{2,1,0:T(8,128)S(1)}, f32[3,352,256]{2,1,0:T(8,128)S(1)}, u32[]{:S(2)}, u32[]{:S(2)}) collective-permute-start(f32[3,352,256]{2,1,0:T(8,128)S(1)} %get-tuple-element.28), channel_id=1, source_target_pairs={{0,16},{16,0},{32,48},{48,32},{64,80},{80,64},{96,112},{112,96},{1... | collective-permute-start | bytes 3244040 | tf_op jit(solution)/shard_map/ppermute | solution.py:26
  29.7 17.4 %collective-permute-start.10 = (f32[2,336,256]{2,1,0:T(8,128)S(1)}, f32[2,336,256]{2,1,0:T(8,128)S(1)}, u32[]{:S(2)}, u32[]{:S(2)}) collective-permute-start(f32[2,336,256]{2,1,0:T(8,128)S(1)} %slice_add_fusion.1), channel_id=1, source_target_pairs={{0,16},{16,0},{32,48},{48,32},{64,80},{80,64},{96,112},{112,96},{1... | collective-permute-start | bytes 2064392 | tf_op jit(solution)/shard_map/ppermute | solution.py:26
  31.1 20.0 %collective-permute-start.6 = (f32[2,336,256]{2,1,0:T(8,128)S(1)}, f32[2,336,256]{2,1,0:T(8,128)S(1)}, u32[]{:S(2)}, u32[]{:S(2)}) collective-permute-start(f32[2,336,256]{2,1,0:T(8,128)S(1)} %slice_add_fusion.2), channel_id=1, source_target_pairs={{0,64},{16,80},{32,96},{48,112},{64,0},{80,16},{96,32},{112,48},{1... | collective-permute-start | bytes 2064392 | tf_op jit(solution)/shard_map/ppermute | solution.py:26
  34.5 19.2 %collective-permute-start.2 = (f32[2,352,256]{2,1,0:T(8,128)S(1)}, f32[2,352,256]{2,1,0:T(8,128)S(1)}, u32[]{:S(2)}, u32[]{:S(2)}) collective-permute-start(f32[2,352,256]{2,1,0:T(8,128)S(1)} %slice_add_fusion), channel_id=1, source_target_pairs={{0,48},{16,32},{32,16},{48,0},{64,112},{80,96},{96,80},{112,64},{1... | collective-permute-start | bytes 2162696 | tf_op jit(solution)/shard_map/ppermute | solution.py:26
  35.8 30.1 %collective-permute-start.4 = (f32[336,256]{1,0:T(8,128)S(1)}, f32[336,256]{1,0:T(8,128)S(1)}, u32[]{:S(2)}, u32[]{:S(2)}) collective-permute-start(f32[336,256]{1,0:T(8,128)S(1)} %bitcast.67), channel_id=1, source_target_pairs={{0,48},{16,32},{32,16},{48,0},{64,112},{80,96},{96,80},{112,64},{1... | collective-permute-start | bytes 1032200 | tf_op jit(solution)/shard_map/ppermute | solution.py:26
  36.6 19.5 %collective-permute-start.8 = (f32[336,256]{1,0:T(8,128)S(1)}, f32[336,256]{1,0:T(8,128)S(1)}, u32[]{:S(2)}, u32[]{:S(2)}) collective-permute-start(f32[336,256]{1,0:T(8,128)S(1)} %bitcast.68), channel_id=1, source_target_pairs={{0,64},{16,80},{32,96},{48,112},{64,0},{80,16},{96,32},{112,48},{1... | collective-permute-start | bytes 1032200 | tf_op jit(solution)/shard_map/ppermute | solution.py:26
  47.1 18.9 %collective-permute-start = (f32[352,256]{1,0:T(8,128)S(1)}, f32[352,256]{1,0:T(8,128)S(1)}, u32[]{:S(2)}, u32[]{:S(2)}) collective-permute-start(f32[352,256]{1,0:T(8,128)S(1)} %bitcast.66), channel_id=1, source_target_pairs={{0,16},{16,0},{32,48},{48,32},{64,80},{80,64},{96,112},{112,96},{1... | collective-permute-start | bytes 1081352 | tf_op jit(solution)/shard_map/ppermute | solution.py:26
  51.1 14.7 %collective-permute-start.11 = (f32[336,256]{1,0:T(8,128)S(1)}, f32[336,256]{1,0:T(8,128)S(1)}, u32[]{:S(2)}, u32[]{:S(2)}) collective-permute-start(f32[336,256]{1,0:T(8,128)S(1)} %fusion.3), channel_id=1, source_target_pairs={{0,48},{16,32},{32,16},{48,0},{64,112},{80,96},{96,80},{112,64},{1... | collective-permute-start | bytes 1032200 | tf_op jit(solution)/shard_map/ppermute | solution.py:26
  53.6 12.2 %collective-permute-start.7 = (f32[336,256]{1,0:T(8,128)S(1)}, f32[336,256]{1,0:T(8,128)S(1)}, u32[]{:S(2)}, u32[]{:S(2)}) collective-permute-start(f32[336,256]{1,0:T(8,128)S(1)} %fusion.6), channel_id=1, source_target_pairs={{0,16},{16,0},{32,48},{48,32},{64,80},{80,64},{96,112},{112,96},{1... | collective-permute-start | bytes 1032200 | tf_op jit(solution)/shard_map/ppermute | solution.py:26
  56.1 9.9 %collective-permute-start.3 = (f32[352,256]{1,0:T(8,128)S(1)}, f32[352,256]{1,0:T(8,128)S(1)}, u32[]{:S(2)}, u32[]{:S(2)}) collective-permute-start(f32[352,256]{1,0:T(8,128)S(1)} %fusion), channel_id=1, source_target_pairs={{0,64},{16,80},{32,96},{48,112},{64,0},{80,16},{96,32},{112,48},{1... | collective-permute-start | bytes 1081352 | tf_op jit(solution)/shard_map/ppermute | solution.py:26
  65.8 8.0 %copy-start = (f32[2,512,256]{2,1,0:T(8,128)S(1)}, f32[2,512,256]{2,1,0:T(8,128)}, u32[]{:S(2)}) copy-start(f32[2,512,256]{2,1,0:T(8,128)} %param.5) | copy-start | bytes 3145732
  66.1 5.2 %collective-permute-start.13 = (f32[8,128]{1,0:T(8,128)S(1)}, f32[8,128]{1,0:T(8,128)S(1)}, u32[]{:S(2)}, u32[]{:S(2)}) collective-permute-start(f32[8,128]{1,0:T(8,128)S(1)} %broadcast_in_dim.4), channel_id=1, source_target_pairs={{0,64},{1,65},{2,66},{3,67},{4,68},{5,69},{6,70},{7,71},{8,72},{9,... | collective-permute-start | bytes 12296 | tf_op jit(solution)/shard_map/ppermute | solution.py:31
  69.0 4.8 %collective-permute-start.14 = (f32[8,128]{1,0:T(8,128)S(1)}, f32[8,128]{1,0:T(8,128)S(1)}, u32[]{:S(2)}, u32[]{:S(2)}) collective-permute-start(f32[8,128]{1,0:T(8,128)S(1)} %broadcast_in_dim.4), channel_id=1, source_target_pairs={{0,72},{1,73},{2,74},{3,75},{4,76},{5,77},{6,78},{7,79},{8,64},{9,... | collective-permute-start | bytes 12296 | tf_op jit(solution)/shard_map/ppermute | solution.py:31
  70.1 3.7 %collective-permute-start.12 = (f32[8,128]{1,0:T(8,128)S(1)}, f32[8,128]{1,0:T(8,128)S(1)}, u32[]{:S(2)}, u32[]{:S(2)}) collective-permute-start(f32[8,128]{1,0:T(8,128)S(1)} %broadcast_in_dim.4), channel_id=1, source_target_pairs={{0,8},{1,9},{2,10},{3,11},{4,12},{5,13},{6,14},{7,15},{8,0},{9,1},... | collective-permute-start | bytes 12296 | tf_op jit(solution)/shard_map/ppermute | solution.py:31
  73.9 24.8 %collective-permute-start.21 = (f32[1024,256]{1,0:T(8,128)S(1)}, f32[1024,256]{1,0:T(8,128)S(1)}, u32[]{:S(2)}, u32[]{:S(2)}) collective-permute-start(f32[1024,256]{1,0:T(8,128)S(1)} %bitcast.77), channel_id=1, source_target_pairs={{0,16},{16,32},{32,48},{48,64},{64,80},{80,96},{96,112},{112,0},{1... | collective-permute-start | bytes 3145736 | tf_op jit(solution)/shard_map/ppermute | solution.py:255
  75.3 3.6 %collective-permute-start.15 = (f32[8,128]{1,0:T(8,128)S(1)}, f32[8,128]{1,0:T(8,128)S(1)}, u32[]{:S(2)}, u32[]{:S(2)}) collective-permute-start(f32[8,128]{1,0:T(8,128)S(1)} %add_add_fusion), channel_id=1, source_target_pairs={{0,2},{1,3},{2,0},{3,1},{4,6},{5,7},{6,4},{7,5},{8,10},{9,11},{10,... | collective-permute-start | bytes 12296 | tf_op jit(solution)/shard_map/ppermute | solution.py:26
  78.9 5.6 %collective-permute-start.16 = (f32[8,128]{1,0:T(8,128)S(1)}, f32[8,128]{1,0:T(8,128)S(1)}, u32[]{:S(2)}, u32[]{:S(2)}) collective-permute-start(f32[8,128]{1,0:T(8,128)S(1)} %add.154), channel_id=1, source_target_pairs={{0,6},{1,7},{2,4},{3,5},{4,2},{5,3},{6,0},{7,1},{8,14},{9,15},{10,... | collective-permute-start | bytes 12296 | tf_op jit(solution)/shard_map/ppermute | solution.py:26
  84.5 1.2 collective-permute-start.17
  85.7 3.6 %collective-permute-start.18 = (f32[8,128]{1,0:T(8,128)S(1)}, f32[8,128]{1,0:T(8,128)S(1)}, u32[]{:S(2)}, u32[]{:S(2)}) collective-permute-start(f32[8,128]{1,0:T(8,128)S(1)} %add.156), channel_id=1, source_target_pairs={{0,48},{16,0},{32,16},{48,32},{64,112},{80,64},{96,80},{112,96},{1... | collective-permute-start | bytes 12296 | tf_op jit(solution)/shard_map/ppermute | solution.py:260
  89.3 4.4 %collective-permute-start.19 = (f32[8,128]{1,0:T(8,128)S(1)}, f32[8,128]{1,0:T(8,128)S(1)}, u32[]{:S(2)}, u32[]{:S(2)}) collective-permute-start(f32[8,128]{1,0:T(8,128)S(1)} %collective-permute-done.18), channel_id=1, source_target_pairs={{0,48},{16,0},{32,16},{48,32},{64,112},{80,64},{96,80},{112,96},{1... | collective-permute-start | bytes 12296 | tf_op jit(solution)/shard_map/ppermute | solution.py:260
  93.7 4.8 %collective-permute-start.20 = (f32[8,128]{1,0:T(8,128)S(1)}, f32[8,128]{1,0:T(8,128)S(1)}, u32[]{:S(2)}, u32[]{:S(2)}) collective-permute-start(f32[8,128]{1,0:T(8,128)S(1)} %collective-permute-done.19), channel_id=1, source_target_pairs={{0,48},{16,0},{32,16},{48,32},{64,112},{80,64},{96,80},{112,96},{1... | collective-permute-start | bytes 12296 | tf_op jit(solution)/shard_map/ppermute | solution.py:260
  98.9 8.5 %collective-permute-start.23 = (f32[336,256]{1,0:T(8,128)S(1)}, f32[336,256]{1,0:T(8,128)S(1)}, u32[]{:S(2)}, u32[]{:S(2)}) collective-permute-start(f32[336,256]{1,0:T(8,128)S(1)} %get-tuple-element.58.refs_2_), channel_id=1, source_target_pairs={{0,16},{16,0},{32,48},{48,32},{64,80},{80,64},{96,112},{112,96},{1... | collective-permute-start | bytes 1032200 | tf_op jit(solution)/shard_map/ppermute | solution.py:26
  102.3 12.8 %collective-permute-start.22 = (f32[352,256]{1,0:T(8,128)S(1)}, f32[352,256]{1,0:T(8,128)S(1)}, u32[]{:S(2)}, u32[]{:S(2)}) collective-permute-start(f32[352,256]{1,0:T(8,128)S(1)} %get-tuple-element.56.refs_1_), channel_id=1, source_target_pairs={{0,64},{16,80},{32,96},{48,112},{64,0},{80,16},{96,32},{112,48},{1... | collective-permute-start | bytes 1081352 | tf_op jit(solution)/shard_map/ppermute | solution.py:26
  104.9 10.4 %collective-permute-start.24 = (f32[336,256]{1,0:T(8,128)S(1)}, f32[336,256]{1,0:T(8,128)S(1)}, u32[]{:S(2)}, u32[]{:S(2)}) collective-permute-start(f32[336,256]{1,0:T(8,128)S(1)} %get-tuple-element.61.refs_3_), channel_id=1, source_target_pairs={{0,48},{16,32},{32,16},{48,0},{64,112},{80,96},{96,80},{112,64},{1... | collective-permute-start | bytes 1032200 | tf_op jit(solution)/shard_map/ppermute | solution.py:26
  107.5 18.6 %collective-permute-start.25 = (f32[2,336,256]{2,1,0:T(8,128)S(1)}, f32[2,336,256]{2,1,0:T(8,128)S(1)}, u32[]{:S(2)}, u32[]{:S(2)}) collective-permute-start(f32[2,336,256]{2,1,0:T(8,128)S(1)} %pad_maximum_fusion.2), channel_id=1, source_target_pairs={{0,64},{16,80},{32,96},{48,112},{64,0},{80,16},{96,32},{112,48},{1... | collective-permute-start | bytes 2064392 | tf_op jit(solution)/shard_map/ppermute | solution.py:26
  115.1 19.2 %collective-permute-start.26 = (f32[2,352,256]{2,1,0:T(8,128)S(1)}, f32[2,352,256]{2,1,0:T(8,128)S(1)}, u32[]{:S(2)}, u32[]{:S(2)}) collective-permute-start(f32[2,352,256]{2,1,0:T(8,128)S(1)} %pad_maximum_fusion.1), channel_id=1, source_target_pairs={{0,48},{16,32},{32,16},{48,0},{64,112},{80,96},{96,80},{112,64},{1... | collective-permute-start | bytes 2162696 | tf_op jit(solution)/shard_map/ppermute | solution.py:26
  115.3 20.9 %collective-permute-start.29 = (f32[2,336,256]{2,1,0:T(8,128)S(1)}, f32[2,336,256]{2,1,0:T(8,128)S(1)}, u32[]{:S(2)}, u32[]{:S(2)}) collective-permute-start(f32[2,336,256]{2,1,0:T(8,128)S(1)} %pad_maximum_fusion.3), channel_id=1, source_target_pairs={{0,16},{16,0},{32,48},{48,32},{64,80},{80,64},{96,112},{112,96},{1... | collective-permute-start | bytes 2064392 | tf_op jit(solution)/shard_map/ppermute | solution.py:26
  115.5 30.8 %collective-permute-start.31 = (f32[2,336,256]{2,1,0:T(8,128)S(1)}, f32[2,336,256]{2,1,0:T(8,128)S(1)}, u32[]{:S(2)}, u32[]{:S(2)}) collective-permute-start(f32[2,336,256]{2,1,0:T(8,128)S(1)} %pad_maximum_fusion.2), channel_id=1, source_target_pairs={{0,48},{16,32},{32,16},{48,0},{64,112},{80,96},{96,80},{112,64},{1... | collective-permute-start | bytes 2064392 | tf_op jit(solution)/shard_map/ppermute | solution.py:26
  117.5 30.6 %collective-permute-start.32 = (f32[2,352,256]{2,1,0:T(8,128)S(1)}, f32[2,352,256]{2,1,0:T(8,128)S(1)}, u32[]{:S(2)}, u32[]{:S(2)}) collective-permute-start(f32[2,352,256]{2,1,0:T(8,128)S(1)} %pad_maximum_fusion.1), channel_id=1, source_target_pairs={{0,16},{16,0},{32,48},{48,32},{64,80},{80,64},{96,112},{112,96},{1... | collective-permute-start | bytes 2162696 | tf_op jit(solution)/shard_map/ppermute | solution.py:26
  134.3 23.0 %collective-permute-start.27 = (f32[2,352,256]{2,1,0:T(8,128)S(1)}, f32[2,352,256]{2,1,0:T(8,128)S(1)}, u32[]{:S(2)}, u32[]{:S(2)}) collective-permute-start(f32[2,352,256]{2,1,0:T(8,128)S(1)} %collective-permute-done.26.refs_7_), channel_id=1, source_target_pairs={{0,16},{16,0},{32,48},{48,32},{64,80},{80,64},{96,112},{112,96},{1... | collective-permute-start | bytes 2162696 | tf_op jit(solution)/shard_map/ppermute | solution.py:26
  134.3 15.6 %collective-permute-start.33 = (f32[2,336,256]{2,1,0:T(8,128)S(1)}, f32[2,336,256]{2,1,0:T(8,128)S(1)}, u32[]{:S(2)}, u32[]{:S(2)}) collective-permute-start(f32[2,336,256]{2,1,0:T(8,128)S(1)} %pad_maximum_fusion.3), channel_id=1, source_target_pairs={{0,64},{16,80},{32,96},{48,112},{64,0},{80,16},{96,32},{112,48},{1... | collective-permute-start | bytes 2064392 | tf_op jit(solution)/shard_map/ppermute | solution.py:26
  136.2 21.1 %collective-permute-start.30 = (f32[2,336,256]{2,1,0:T(8,128)S(1)}, f32[2,336,256]{2,1,0:T(8,128)S(1)}, u32[]{:S(2)}, u32[]{:S(2)}) collective-permute-start(f32[2,336,256]{2,1,0:T(8,128)S(1)} %collective-permute-done.29.refs_9_), channel_id=1, source_target_pairs={{0,64},{16,80},{32,96},{48,112},{64,0},{80,16},{96,32},{112,48},{1... | collective-permute-start | bytes 2064392 | tf_op jit(solution)/shard_map/ppermute | solution.py:26
  146.3 11.0 %collective-permute-start.28 = (f32[2,336,256]{2,1,0:T(8,128)S(1)}, f32[2,336,256]{2,1,0:T(8,128)S(1)}, u32[]{:S(2)}, u32[]{:S(2)}) collective-permute-start(f32[2,336,256]{2,1,0:T(8,128)S(1)} %collective-permute-done.25.refs_8_), channel_id=1, source_target_pairs={{0,48},{16,32},{32,16},{48,0},{64,112},{80,96},{96,80},{112,64},{1... | collective-permute-start | bytes 2064392 | tf_op jit(solution)/shard_map/ppermute | solution.py:26
